TPU v7x, 768 devices: a whole 4x8x12 slice. The times are simulated.
768 devices in a mesh: row: 48 (over z, x_lo, core), col: 16 (over x_hi, y).
Axes of the slice: x: 4 (x_hi: 2, x_lo: 2; x = x_hi * 2 + x_lo), y: 8, z: 12, core: 2. Of those that a mesh axis runs over, the one named last changes fastest.
Arguments:
- master_weight: float32 [12288, 12288], P('col', 'row'), may hold values from -3 to 3
- gradient: bfloat16 [12288, 12288], P('col', 'row'), may hold values from -6 to 6
- first_moment: float32 [768, 12288], P('row', 'col'), may hold values from -4 to 4
- second_moment: float32 [768, 12288], P('row', 'col'), may hold values from 0.05 to 2
- left_basis: float32 [12288, 768], P('col'), may hold values from -0.0546875 to 0.0546875
- right_basis: float32 [12288, 12288], P('row', 'col'), may hold values from -0.0546875 to 0.0546875
Outputs:
- new_weight: bfloat16 [12288, 12288], P('col', 'row')
- direction: float32 [12288, 12288], P('col', 'row')
- new_first: float32 [768, 12288], P('row', 'col')
- new_second: float32 [768, 12288], P('row', 'col')
All inputs are finite; a program needn't handle non-finite values.
Results may differ from a plain program's by a relative error of at most 0.001.
Values sent between devices are 32-bit elements; how exact they have to be, the bound alone decides.
No kernel may reach another device: no remote copies, remote signals or barrier semaphores. Data moves between devices by JAX's collectives and lax.ppermute only.
A program may use at most 32 MiB of HBM per device.

v0:
```python
import jax
import jax.numpy as jnp
from jax import lax
from jax.sharding import PartitionSpec as P

STEP = 10


def make_rotate(chosen, right_basis):
    return jnp.dot(chosen, right_basis, precision=lax.Precision.HIGHEST)


def shards(master_weight, gradient, first_moment, second_moment, left_basis, right_basis):
    highest = lax.Precision.HIGHEST
    tile_rows = gradient.shape[0]
    own_rows = first_moment.shape[0]
    groups = lax.axis_size("row")
    partial_left = lax.dot_general(
        left_basis, gradient.astype(jnp.float32), (((0,), (0,)), ((), ())), precision=highest
    )
    left_rotated = lax.psum(partial_left, "col")
    count_pieces = 1
    piece_rows = own_rows // count_pieces
    grouped = left_rotated.reshape(groups, own_rows, left_rotated.shape[1])
    basis_grouped = left_basis.reshape(tile_rows, groups, own_rows)
    correction = 1.0 - 0.95**STEP
    chosen = grouped.reshape(groups * piece_rows, left_rotated.shape[1])
    rotated = lax.psum_scatter(
        make_rotate(chosen, right_basis), "row", scatter_dimension=0, tiled=True
    )
    first_piece = 0.95 * first_moment + 0.05 * rotated
    second_piece = 0.95 * second_moment + 0.05 * rotated * rotated
    normed = first_piece / correction / (jnp.sqrt(second_piece / correction) + 1e-08)
    gathered = lax.all_gather(normed, "row", axis=0, tiled=True)
    back_part = lax.dot_general(gathered, right_basis, (((1,), (1,)), ((), ())), precision=highest)
    back_whole = lax.psum(back_part, "col")
    basis_cols = basis_grouped.reshape(tile_rows, groups * piece_rows)
    direction = jnp.dot(basis_cols, back_whole, precision=highest)
    new_weight = (master_weight - 0.003 * (direction + 0.1 * master_weight)).astype(jnp.bfloat16)
    return (new_weight, direction, first_piece, second_piece)


def solution(mesh):
    in_specs = (
        P("col", "row"),
        P("col", "row"),
        P("row", "col"),
        P("row", "col"),
        P("col", None),
        P("row", "col"),
    )
    out_specs = (P("col", "row"), P("col", "row"), P("row", "col"), P("row", "col"))
    return jax.shard_map(shards, mesh=mesh, in_specs=in_specs, out_specs=out_specs, check_vma=False)
```

profile of v0, /device:TPU:64, one launch (start us, length us, event | category | flops | bytes accessed | tf_op | source)
XLA Modules:
  0.0 650.4 jit_solution(13363115641218779363)
XLA Ops:
  7.2 0.0 copy-start
  7.2 0.0 all-reduce.3.cloned.1.call-start
  7.2 1.6 copy-done
  8.8 3.9 fusion.2
  12.7 0.0 all-reduce.3.cloned.1.call-update
  12.8 0.0 copy-start.2
  12.8 0.0 copy-start.3
  12.8 0.0 reduce-scatter.2.cloned.1.call-start
  12.8 174.3 %all-reduce.3.cloned.1.call-done = f32[768,256]{1,0:T(8,128)} async-done(((f32[768,256]{1,0:T(8,128)}), f32[768,256]{1,0:T(8,128)}) %all-reduce.3.cloned.1.call-update) | async-done | bytes 786448 | tf_op jit(solution)/shard_map/psum | solution.py:21
  187.2 4.6 fusion.3
  191.8 0.0 reduce-scatter.2.cloned.1.call-update
  191.8 0.0 all-gather.2.cloned.1.call-start
  191.8 168.7 %reduce-scatter.2.cloned.1.call-done = f32[16,768]{1,0:T(8,128)} async-done(((f32[768,768]{1,0:T(8,128)}), f32[16,768]{1,0:T(8,128)}) %reduce-scatter.2.cloned.1.call-update) | async-done | bytes 49168 | tf_op jit(solution)/shard_map/reduce_scatter | solution.py:28
  360.5 1.5 add_divide_fusion
  362.0 0.0 all-gather.2.cloned.1.call-update
  362.0 0.0 all-reduce.5.cloned.1.call-start
  362.1 101.7 %all-gather.2.cloned.1.call-done = f32[768,768]{1,0:T(8,128)} async-done(((f32[16,768]{1,0:T(8,128)}), f32[768,768]{1,0:T(8,128)}) %all-gather.2.cloned.1.call-update) | async-done | bytes 2359312 | tf_op jit(solution)/shard_map/all_gather | solution.py:34
  463.8 4.6 fusion.4
  468.3 0.0 all-reduce.5.cloned.1.call-update
  468.4 1.4 copy.11
  469.8 165.0 %all-reduce.5.cloned.1.call-done = f32[768,256]{1,0:T(8,128)} async-done(((f32[768,256]{1,0:T(8,128)}), f32[768,256]{1,0:T(8,128)}) %all-reduce.5.cloned.1.call-update) | async-done | bytes 786448 | tf_op jit(solution)/shard_map/psum | solution.py:36
  634.7 5.9 subtract_convert_fusion
  640.7 2.3 copy.13
  642.9 0.9 copy.12
  (4 shorter events, 0.0 us)
Async XLA Ops:
  7.2 1.7 copy-start
  7.2 180.0 %copy-start.1 = (f32[256,768]{1,0:T(8,128)S(1)}, f32[256,768]{1,0:T(8,128)}, u32[]{:S(2)}) copy-start(f32[256,768]{1,0:T(8,128)} %param.11) | copy-start | bytes 2359300
  7.2 180.0 %all-reduce.3.cloned.1.call-start = ((), (), s32[]{:S(2)}) async-start(), calls=%async_computation.1 | async-start | bytes 1572864 | tf_op jit(solution)/shard_map/psum | solution.py:21
  12.8 347.8 %copy-start.2 = (f32[16,768]{1,0:T(8,128)S(1)}, f32[16,768]{1,0:T(8,128)}, u32[]{:S(2)}) copy-start(f32[16,768]{1,0:T(8,128)} %param.8) | copy-start | bytes 147460
  12.8 347.8 %copy-start.3 = (f32[16,768]{1,0:T(8,128)S(1)}, f32[16,768]{1,0:T(8,128)}, u32[]{:S(2)}) copy-start(f32[16,768]{1,0:T(8,128)} %param.9) | copy-start | bytes 147460
  12.8 347.7 %reduce-scatter.2.cloned.1.call-start = ((), (), s32[]{:S(2)}) async-start(), calls=%async_computation.2 | async-start | bytes 2408448 | tf_op jit(solution)/shard_map/reduce_scatter | solution.py:28
  191.8 272.0 %all-gather.2.cloned.1.call-start = ((), (), s32[]{:S(2)}) async-start(), calls=%async_computation.3 | async-start | bytes 2408448 | tf_op jit(solution)/shard_map/all_gather | solution.py:34
  362.0 272.7 %all-reduce.5.cloned.1.call-start = ((), (), s32[]{:S(2)}) async-start(), calls=%async_computation.4 | async-start | bytes 1572864 | tf_op jit(solution)/shard_map/psum | solution.py:36
Sparse Core Ops, SparseCore 0:
  12.9 174.2 all-reduce.2
  191.9 168.5 reduce-scatter.1
  363.6 100.1 all-gather.1
  468.5 166.2 all-reduce.4
where the time goes:
time: 651 us; the launch traced here: 650 us
  waiting for transfers between devices  610 us (94%)
  matrix products  19 us (3%)
  between operations  13.8 us (2%)
    psum x1, waiting for transfers between devices, shards(): left_rotated = lax.psum(partial_left, 'col')  174 us
    reduce_scatter x1, waiting for transfers between devices, shards(): lax.psum_scatter(make_rotate(chosen, right_basis), 'row', scatter_dimensi...  169 us
    psum x1, waiting for transfers between devices, shards(): back_whole = lax.psum(back_part, 'col')  165 us
    all_gather x1, waiting for transfers between devices, shards(): gathered = lax.all_gather(normed, 'row', axis=0, tiled=True)  102 us
  transfers between devices with their start and end apart: 4, of which 4 were waited for; matrix products, arithmetic and copies ran while one was open for 0% of the time, Pallas kernels for 0%

commit v1 on v0

v1 whole, which is shorter than its diff:
```python
import jax
import jax.numpy as jnp
from jax import lax
from jax.sharding import Mesh, PartitionSpec as P

STEP = 10
ROW = ("z", "xl", "core")
COL = ("xh", "y")
HIGH = lax.Precision.HIGH


def swap(x, axis):
    return lax.ppermute(x, axis, [(0, 1), (1, 0)])


def sum_over_col(part):
    count = lax.axis_size("y")
    pieces = part.reshape(count, part.shape[0] // count, part.shape[1])
    mine = jnp.sum(lax.all_to_all(pieces, "y", 0, 0, tiled=True), axis=0)
    mine = mine + swap(mine, "xh")
    return lax.all_gather(mine, "y", axis=0, tiled=True)


def shards(master_weight, gradient, first_moment, second_moment, left_basis, right_basis):
    own, cols = first_moment.shape
    depth = lax.axis_size("z")
    keys = gradient.shape[1]
    core = lax.axis_index("core")
    correction = 1.0 - 0.95**STEP

    partial_left = lax.dot_general(
        left_basis, gradient.astype(jnp.float32), (((0,), (0,)), ((), ())), precision=HIGH
    )
    left_rotated = sum_over_col(partial_left)

    grouped = left_rotated.reshape(depth, 2, 2, own, keys)

    def half(which):
        picked = lax.dynamic_index_in_dim(grouped, which, 2, keepdims=False)
        picked = jnp.transpose(picked, (1, 0, 2, 3)).reshape(2 * depth * own, keys)
        return jnp.dot(picked, right_basis, precision=HIGH)

    theirs = swap(half(1 - core), "core")
    summed = half(core) + theirs
    pair = lax.all_to_all(summed.reshape(2, depth * own, cols), "xl", 0, 0, tiled=True)
    summed = (pair[0] + pair[1]).reshape(depth, own, cols)
    rotated = jnp.sum(lax.all_to_all(summed, "z", 0, 0, tiled=True), axis=0)

    new_first = 0.95 * first_moment + 0.05 * rotated
    new_second = 0.95 * second_moment + 0.05 * rotated * rotated
    normed = new_first / correction / (jnp.sqrt(new_second / correction) + 1e-08)

    column = lax.all_gather(normed, "z", axis=0, tiled=True)
    both = lax.all_to_all(jnp.stack([column, column]), "xl", 0, 0, tiled=True)
    mine = both.reshape(2 * depth * own, cols)
    other = swap(mine, "core")
    contract = (((1,), (1,)), ((), ()))
    back_part = jnp.concatenate(
        [
            lax.dot_general(mine, right_basis, contract, precision=HIGH),
            lax.dot_general(other, right_basis, contract, precision=HIGH),
        ]
    )
    back = sum_over_col(back_part).reshape(2, 2, depth, own, keys)
    back = jnp.where(core == 0, back, back[::-1])
    back = jnp.transpose(back, (2, 1, 0, 3, 4)).reshape(back_part.shape)
    direction = jnp.dot(left_basis, back, precision=HIGH)
    new_weight = (master_weight - 0.003 * (direction + 0.1 * master_weight)).astype(jnp.bfloat16)
    return (new_weight, direction, new_first, new_second)


def solution(mesh):
    fine = Mesh(mesh.devices.reshape(12, 2, 2, 2, 8), ROW + COL)
    in_specs = (P(COL, ROW), P(COL, ROW), P(ROW, COL), P(ROW, COL), P(COL, None), P(ROW, COL))
    out_specs = (P(COL, ROW), P(COL, ROW), P(ROW, COL), P(ROW, COL))
    return jax.shard_map(shards, mesh=fine, in_specs=in_specs, out_specs=out_specs, check_vma=False)
```

time: 651 us -> 248 us (0.38)
  the two profiles are of different devices: /device:TPU:64 before, /device:TPU:4 now
where the time goes in v1:
time: 248 us; the launch traced here: 247 us
  blocking collectives  205 us (83%)
  waiting for transfers between devices  14.7 us (6%)
  starting transfers between devices  8.59 us (3%)
  matrix products  8.16 us (3%)
  local copies, waits for them, and re-layouts  7.48 us (3%)
    all_to_all x2, blocking collectives, sum_over_col(): mine = jnp.sum(lax.all_to_all(pieces, 'y', 0, 0, tiled=True), axis=0)  56.1 us
    all_gather x2, blocking collectives, sum_over_col(): return lax.all_gather(mine, 'y', axis=0, tiled=True)  52.3 us
    all_to_all x1, blocking collectives, shards(): rotated = jnp.sum(lax.all_to_all(summed, 'z', 0, 0, tiled=True), axis=0)  41.5 us
    all_gather x1, blocking collectives, shards(): column = lax.all_gather(normed, 'z', axis=0, tiled=True)  24.4 us
    all_to_all x1, blocking collectives, shards(): lax.all_to_all(summed.reshape(2, depth * own, cols), 'xl', 0, 0, tiled=True)  18 us
    ppermute x4, waiting for transfers between devices, swap(): return lax.ppermute(x, axis, [(0, 1), (1, 0)])  14.7 us
    all_to_all x1, blocking collectives, shards(): both = lax.all_to_all(jnp.stack([column, column]), 'xl', 0, 0, tiled=True)  12.6 us
    ppermute x4, starting transfers between devices, swap(): return lax.ppermute(x, axis, [(0, 1), (1, 0)])  8.59 us
  transfers between devices with their start and end apart: 4, of which 4 were waited for; matrix products, arithmetic and copies ran while one was open for 1% of the time, Pallas kernels for 0%

profile of v1, /device:TPU:4, one launch (start us, length us, event | category | flops | bytes accessed | tf_op | source)
XLA Modules:
  0.0 247.0 jit_solution(12796066965822716018)
XLA Ops:
  0.6 1.7 copy-done
  2.3 2.4 fusion.3
  4.7 30.0 %all_to_all.25 = f32[8,96,256]{2,1,0:T(8,128)S(1)} all-to-all(f32[8,96,256]{2,1,0:T(8,128)S(1)} %bitcast.39), channel_id=1, replica_groups=mesh['z'=12,'xl'=2,'core'=2,'xh'=2,'y'=8] {'y'}, dimensions={0} | all-to-all | bytes 1572864 | tf_op jit(solution)/shard_map/all_to_all | solution.py:19
  34.8 2.4 collective-permute-start
  37.2 5.6 %collective-permute-done = f32[96,256]{1,0:T(8,128)S(1)} collective-permute-done((f32[96,256]{1,0:T(8,128)S(1)}, f32[96,256]{1,0:T(8,128)S(1)}, u32[]{:S(2)}, u32[]{:S(2)}) %collective-permute-start) | collective-permute-done | bytes 98336 | tf_op jit(solution)/shard_map/ppermute | solution.py:13
  42.8 26.4 %all_gather.9 = f32[768,256]{1,0:T(8,128)S(1)} all-gather(f32[96,256]{1,0:T(8,128)S(1)} %add.39), channel_id=1, replica_groups=mesh['z'=12,'xl'=2,'core'=2,'xh'=2,'y'=8] {'y'}, dimensions={0}, use_global_device_ids=true | all-gather | bytes 884736 | tf_op jit(solution)/shard_map/all_gather | solution.py:21
  69.3 1.0 copy-done.1
  71.0 1.9 collective-permute-start.1
  73.0 2.8 %collective-permute-done.1 = f32[384,768]{1,0:T(8,128)S(1)} collective-permute-done((f32[384,768]{1,0:T(8,128)S(1)}, f32[384,768]{1,0:T(8,128)S(1)}, u32[]{:S(2)}, u32[]{:S(2)}) %collective-permute-start.1) | collective-permute-done | bytes 1179680 | tf_op jit(solution)/shard_map/ppermute | solution.py:13
  76.4 18.0 %all_to_all.26 = f32[2,192,768]{2,1,0:T(8,128)S(1)} all-to-all(f32[2,192,768]{2,1,0:T(8,128)S(1)} %bitcast.35), channel_id=1, replica_groups=mesh['z'=12,'xl'=2,'core'=2,'xh'=2,'y'=8] {'xl'}, dimensions={0} | all-to-all | bytes 2359296 | tf_op jit(solution)/shard_map/all_to_all | solution.py:45
  94.5 41.5 %all_to_all.27 = f32[12,16,768]{2,1,0:T(8,128)} all-to-all(f32[12,16,768]{2,1,0:T(8,128)S(1)} %bitcast.43), channel_id=1, replica_groups=mesh['z'=12,'xl'=2,'core'=2,'xh'=2,'y'=8] {'z'}, dimensions={0} | all-to-all | bytes 1179648 | tf_op jit(solution)/shard_map/all_to_all | solution.py:47
  136.0 1.1 reduce_sum.28
  137.8 24.4 %all_gather.10 = f32[192,768]{1,0:T(8,128)S(1)} all-gather(f32[16,768]{1,0:T(8,128)S(1)} %get-tuple-element.20), channel_id=1, replica_groups=mesh['z'=12,'xl'=2,'core'=2,'xh'=2,'y'=8] {'z'}, dimensions={0}, use_global_device_ids=true | all-gather | bytes 638976 | tf_op jit(solution)/shard_map/all_gather | solution.py:53
  162.3 12.6 %all_to_all.28 = f32[2,192,768]{2,1,0:T(8,128)S(1)} all-to-all(f32[2,192,768]{2,1,0:T(8,128)S(1)} %pad_maximum_fusion), channel_id=1, replica_groups=mesh['z'=12,'xl'=2,'core'=2,'xh'=2,'y'=8] {'xl'}, dimensions={0} | all-to-all | bytes 2359296 | tf_op jit(solution)/shard_map/all_to_all | solution.py:54
  174.9 1.9 collective-permute-start.2
  177.5 2.1 collective-permute-done.2
  180.4 26.1 %all_to_all.29 = f32[8,96,256]{2,1,0:T(8,128)S(1)} all-to-all(f32[8,96,256]{2,1,0:T(8,128)S(1)} %bitcast.40), channel_id=1, replica_groups=mesh['z'=12,'xl'=2,'core'=2,'xh'=2,'y'=8] {'y'}, dimensions={0} | all-to-all | bytes 1572864 | tf_op jit(solution)/shard_map/all_to_all | solution.py:19
  206.6 2.4 collective-permute-start.3
  208.9 1.4 copy.27
  210.3 4.3 %collective-permute-done.3 = f32[96,256]{1,0:T(8,128)S(1)} collective-permute-done((f32[96,256]{1,0:T(8,128)S(1)}, f32[96,256]{1,0:T(8,128)S(1)}, u32[]{:S(2)}, u32[]{:S(2)}) %collective-permute-start.3) | collective-permute-done | bytes 98336 | tf_op jit(solution)/shard_map/ppermute | solution.py:13
  214.6 25.9 %all_gather.11 = f32[768,256]{1,0:T(8,128)S(1)} all-gather(f32[96,256]{1,0:T(8,128)S(1)} %add.49), channel_id=1, replica_groups=mesh['z'=12,'xl'=2,'core'=2,'xh'=2,'y'=8] {'y'}, dimensions={0}, use_global_device_ids=true | all-gather | bytes 884736 | tf_op jit(solution)/shard_map/all_gather | solution.py:21
  240.7 3.1 %subtract_convert_fusion = (bf16[768,256]{0,1:T(8,128)(2,1)S(1)}, f32[768,256]{0,1:T(8,128)}) fusion(f32[768,256]{0,1:T(8,128)S(1)} %copy.27, f32[768,256]{1,0:T(8,128)S(1)} %bitcast.38, f32[768,768]{1,0:T(8,128)S(1)} %copy-done), kind=kOutput, calls=%fused_computation.6 | convolution fusion | flops 906952704 | bytes 5111808 | tf_op jit(solution)/shard_map/dot_general | solution.py:67
  243.8 2.3 copy.29
  246.0 0.9 copy.28
  (23 shorter events, 3.9 us)
Async XLA Ops:
  0.6 1.7 copy-start
  34.8 8.0 %collective-permute-start = (f32[96,256]{1,0:T(8,128)S(1)}, f32[96,256]{1,0:T(8,128)S(1)}, u32[]{:S(2)}, u32[]{:S(2)}) collective-permute-start(f32[96,256]{1,0:T(8,128)S(1)} %reduce_sum.27), channel_id=1, source_target_pairs={{0,8},{8,0},{1,9},{9,1},{2,10},{10,2},{3,11},{11,3},{4,12},{12,4},... | collective-permute-start | bytes 294920 | tf_op jit(solution)/shard_map/ppermute | solution.py:13
  69.2 1.1 copy-start.1
  71.0 4.7 %collective-permute-start.1 = (f32[384,768]{1,0:T(8,128)S(1)}, f32[384,768]{1,0:T(8,128)S(1)}, u32[]{:S(2)}, u32[]{:S(2)}) collective-permute-start(f32[384,768]{1,0:T(8,128)S(1)} %fusion.4), channel_id=1, source_target_pairs={{0,16},{16,0},{1,17},{17,1},{2,18},{18,2},{3,19},{19,3},{4,20},{20... | collective-permute-start | bytes 3538952 | tf_op jit(solution)/shard_map/ppermute | solution.py:13
  94.5 42.6 %copy-start.2 = (f32[16,768]{1,0:T(8,128)S(1)}, f32[16,768]{1,0:T(8,128)}, u32[]{:S(2)}) copy-start(f32[16,768]{1,0:T(8,128)} %param.8) | copy-start | bytes 147460
  94.5 42.6 %copy-start.3 = (f32[16,768]{1,0:T(8,128)S(1)}, f32[16,768]{1,0:T(8,128)}, u32[]{:S(2)}) copy-start(f32[16,768]{1,0:T(8,128)} %param.9) | copy-start | bytes 147460
  174.9 4.7 %collective-permute-start.2 = (f32[384,768]{1,0:T(8,128)S(1)}, f32[384,768]{1,0:T(8,128)S(1)}, u32[]{:S(2)}, u32[]{:S(2)}) collective-permute-start(f32[384,768]{1,0:T(8,128)S(1)} %bitcast.36), channel_id=1, source_target_pairs={{0,16},{16,0},{1,17},{17,1},{2,18},{18,2},{3,19},{19,3},{4,20},{20... | collective-permute-start | bytes 3538952 | tf_op jit(solution)/shard_map/ppermute | solution.py:13
  206.6 8.0 %collective-permute-start.3 = (f32[96,256]{1,0:T(8,128)S(1)}, f32[96,256]{1,0:T(8,128)S(1)}, u32[]{:S(2)}, u32[]{:S(2)}) collective-permute-start(f32[96,256]{1,0:T(8,128)S(1)} %reduce_sum.29), channel_id=1, source_target_pairs={{0,8},{8,0},{1,9},{9,1},{2,10},{10,2},{3,11},{11,3},{4,12},{12,4},... | collective-permute-start | bytes 294920 | tf_op jit(solution)/shard_map/ppermute | solution.py:13

commit v2 on v1

v2 whole, which is shorter than its diff:
```python
import jax
import jax.numpy as jnp
from jax import lax
from jax.sharding import Mesh, PartitionSpec as P

STEP = 10
ROW = ("z", "xl", "core")
COL = ("xh", "y")
HIGH = lax.Precision.HIGH


def swap(x, axis):
    return lax.ppermute(x, axis, [(0, 1), (1, 0)])


def scatter_sum(x, axes):
    return jnp.sum(lax.all_to_all(x, axes, 0, 0, tiled=True), axis=0)


def gather(x, axes):
    copies = jnp.broadcast_to(x[None], (lax.axis_size(axes),) + x.shape)
    return lax.all_to_all(copies, axes, 0, 0, tiled=True)


def shards(master_weight, gradient, first_moment, second_moment, left_basis, right_basis):
    own, cols = first_moment.shape
    window = left_basis.shape[1]
    depth = lax.axis_size("z")
    peers = lax.axis_size(COL)
    piece = window // 2 // peers
    keys = gradient.shape[1]
    core = lax.axis_index("core")
    xl = lax.axis_index("xl")
    correction = 1.0 - 0.95**STEP

    basis = jnp.concatenate([right_basis, swap(right_basis, "xl")], axis=0)

    partial_left = lax.dot_general(
        left_basis, gradient.astype(jnp.float32), (((0,), (0,)), ((), ())), precision=HIGH
    )
    parts = partial_left.reshape(depth, 2, 2 * own, keys).transpose(1, 0, 2, 3)
    parts = parts.reshape(2, peers, piece, keys).transpose(1, 0, 2, 3)
    mine, basis = lax.optimization_barrier((scatter_sum(parts, COL), basis))
    keep = lax.dynamic_index_in_dim(mine, xl, 0, keepdims=False)
    got = swap(lax.dynamic_index_in_dim(mine, 1 - xl, 0, keepdims=False), "xl")
    left_rotated = gather(jnp.concatenate([keep, got], axis=1), COL)
    grouped = left_rotated.reshape(depth, 2, own, 2 * keys)

    def half(which):
        picked = lax.dynamic_index_in_dim(grouped, which, 1, keepdims=False)
        return jnp.dot(picked.reshape(depth * own, 2 * keys), basis, precision=HIGH)

    theirs = swap(half(1 - core), "core")
    summed = half(core) + theirs
    rotated = scatter_sum(summed.reshape(depth, own, cols), "z")

    new_first = 0.95 * first_moment + 0.05 * rotated
    new_second = 0.95 * second_moment + 0.05 * rotated * rotated
    normed = new_first / correction / (jnp.sqrt(new_second / correction) + 1e-08)

    column = lax.all_gather(normed, "z", axis=0, tiled=True)
    other = swap(column, "core")
    contract = (((1,), (1,)), ((), ()))
    back_part = jnp.concatenate(
        [
            lax.dot_general(column, basis, contract, precision=HIGH),
            lax.dot_general(other, basis, contract, precision=HIGH),
        ]
    )
    mine = scatter_sum(back_part.reshape(peers, piece, 2 * keys), COL)
    keep, got = mine[:, :keys], swap(mine[:, keys:], "xl")
    pair = jnp.where(xl == 0, jnp.stack([keep, got]), jnp.stack([got, keep]))
    back = gather(pair, COL).transpose(1, 0, 2, 3).reshape(2, 2, depth, own, keys)
    back = jnp.where(core == 0, back, back[:, ::-1])
    back = back.transpose(2, 0, 1, 3, 4).reshape(window, keys)
    direction = jnp.dot(left_basis, back, precision=HIGH)
    new_weight = (master_weight - 0.003 * (direction + 0.1 * master_weight)).astype(jnp.bfloat16)
    return (new_weight, direction, new_first, new_second)


def solution(mesh):
    fine = Mesh(mesh.devices.reshape(12, 2, 2, 2, 8), ROW + COL)
    in_specs = (P(COL, ROW), P(COL, ROW), P(ROW, COL), P(ROW, COL), P(COL, None), P(ROW, COL))
    out_specs = (P(COL, ROW), P(COL, ROW), P(ROW, COL), P(ROW, COL))
    return jax.shard_map(shards, mesh=fine, in_specs=in_specs, out_specs=out_specs, check_vma=False)
```

time: 248 us -> 232 us (0.935)
  the two profiles are of different devices: /device:TPU:4 before, /device:TPU:8 now
where the time goes in v2:
time: 232 us; the launch traced here: 231 us
  blocking collectives  96.4 us (42%)
  waiting for transfers between devices  69.8 us (30%)
  starting transfers between devices  38.4 us (17%)
  local copies, waits for them, and re-layouts  11.9 us (5%)
  matrix products  10.2 us (4%)
  other arithmetic  3.59 us (2%)
    all_to_all x2, blocking collectives, scatter_sum(): return jnp.sum(lax.all_to_all(x, axes, 0, 0, tiled=True), axis=0)  71.9 us
    all_to_all x2, waiting for transfers between devices, gather(): return lax.all_to_all(copies, axes, 0, 0, tiled=True)  39.9 us
    ppermute x5, waiting for transfers between devices, swap(): return lax.ppermute(x, axis, [(0, 1), (1, 0)])  30 us
    all_gather x1, blocking collectives, shards(): column = lax.all_gather(normed, 'z', axis=0, tiled=True)  24.5 us
    all_to_all x2, starting transfers between devices, gather(): return lax.all_to_all(copies, axes, 0, 0, tiled=True)  13.4 us
    all_to_all x1, starting transfers between devices, scatter_sum(): return jnp.sum(lax.all_to_all(x, axes, 0, 0, tiled=True), axis=0)  12.9 us
    ppermute x5, starting transfers between devices, swap(): return lax.ppermute(x, axis, [(0, 1), (1, 0)])  12.2 us
    unnamed x13, local copies, waits for them, and re-layouts  7.61 us
  transfers between devices with their start and end apart: 8, of which 6 were waited for; matrix products, arithmetic and copies ran while one was open for 3% of the time, Pallas kernels for 0%

profile of v2, /device:TPU:8, one launch (start us, length us, event | category | flops | bytes accessed | tf_op | source)
XLA Modules:
  0.0 231.2 jit_solution(16885115248556182311)
XLA Ops:
  0.6 1.7 copy-done
  2.3 2.4 %fusion.3 = f32[768,256]{1,0:T(8,128)S(1)} fusion(f32[768,768]{1,0:T(8,128)S(1)} %copy-done, bf16[768,256]{1,0:T(8,128)(2,1)} %param.7), kind=kOutput, calls=%fused_computation.18 | convolution fusion | flops 905969664 | bytes 3538944 | tf_op jit(solution)/shard_map/dot_general | solution.py:38
  5.7 12.9 %all-to-all-start = ((f32[16,2,24,256]{3,2,1,0:T(8,128)}), f32[16,2,24,256]{3,2,1,0:T(8,128)S(1)}, u32[]{:S(2)}, u32[]{:S(2)}) async-start(f32[16,2,24,256]{3,2,1,0:T(8,128)} %copy.26), calls=%async_computation | async-start | bytes 1572864 | tf_op jit(solution)/shard_map/all_to_all | solution.py:17
  18.6 1.9 collective-permute-start
  20.5 23.0 %collective-permute-done = f32[256,768]{1,0:T(8,128)} collective-permute-done((f32[256,768]{1,0:T(8,128)}, f32[256,768]{1,0:T(8,128)}, u32[]{:S(2)}, u32[]{:S(2)}) %collective-permute-start) | collective-permute-done | bytes 786464 | tf_op jit(solution)/shard_map/ppermute | solution.py:13
  43.5 2.6 %pad_maximum_fusion = f32[512,768]{1,0:T(8,128)} fusion(f32[256,768]{1,0:T(8,128)} %collective-permute-done, f32[256,768]{1,0:T(8,128)} %param.11), kind=kLoop, calls=%fused_computation | loop fusion | flops 393216 | bytes 3145728 | tf_op jit(solution)/shard_map/concatenate | solution.py:36
  46.2 3.6 %collective-permute-start.1 = (f32[24,256]{1,0:T(8,128)S(1)}, f32[24,256]{1,0:T(8,128)S(1)}, u32[]{:S(2)}, u32[]{:S(2)}) collective-permute-start(f32[24,256]{1,0:T(8,128)S(1)} %get-tuple-element.32), channel_id=1, source_target_pairs={{0,32},{32,0},{1,33},{33,1},{2,34},{34,2},{3,35},{35,3},{4,36},{36... | collective-permute-start | bytes 73736 | tf_op jit(solution)/shard_map/ppermute | solution.py:13
  49.8 2.2 collective-permute-done.1
  52.9 9.2 %all-to-all-start.1 = ((f32[16,24,512]{2,1,0:T(8,128)}), f32[16,24,512]{2,1,0:T(8,128)S(1)}, u32[]{:S(2)}, u32[]{:S(2)}) async-start(f32[16,24,512]{2,1,0:T(8,128)} %broadcast_in_dim.4), calls=%async_computation.1 | async-start | bytes 1572864 | tf_op jit(solution)/shard_map/all_to_all | solution.py:22
  62.1 19.9 %all-to-all-done.1 = f32[16,24,512]{2,1,0:T(8,128)S(1)} async-done(((f32[16,24,512]{2,1,0:T(8,128)}), f32[16,24,512]{2,1,0:T(8,128)S(1)}, u32[]{:S(2)}, u32[]{:S(2)}) %all-to-all-start.1) | async-done | bytes 786464 | tf_op jit(solution)/shard_map/all_to_all | solution.py:22
  84.1 1.9 collective-permute-start.2
  86.1 2.0 collective-permute-done.2
  88.8 43.1 %all_to_all.25 = f32[12,16,768]{2,1,0:T(8,128)S(1)} all-to-all(f32[12,16,768]{2,1,0:T(8,128)S(1)} %bitcast.44), channel_id=1, replica_groups=mesh['z'=12,'xl'=2,'core'=2,'xh'=2,'y'=8] {'z'}, dimensions={0} | all-to-all | bytes 1179648 | tf_op jit(solution)/shard_map/all_to_all | solution.py:17
  132.6 24.5 %all_gather.3 = f32[192,768]{1,0:T(8,128)S(1)} all-gather(f32[16,768]{1,0:T(8,128)S(1)} %get-tuple-element.24), channel_id=1, replica_groups=mesh['z'=12,'xl'=2,'core'=2,'xh'=2,'y'=8] {'z'}, dimensions={0}, use_global_device_ids=true | all-gather | bytes 638976 | tf_op jit(solution)/shard_map/all_gather | solution.py:61
  157.2 1.9 collective-permute-start.3
  159.1 2.3 %fusion.5 = f32[192,512]{1,0:T(8,128)S(1)} fusion(f32[192,768]{1,0:T(8,128)S(1)} %all_gather.3, f32[512,768]{1,0:T(8,128)} %pad_maximum_fusion), kind=kOutput, calls=%fused_computation.20 | convolution fusion | flops 452984832 | bytes 2555904 | tf_op jit(solution)/shard_map/dot_general | solution.py:66
  162.5 28.7 %all_to_all.26 = f32[16,24,512]{2,1,0:T(8,128)S(1)} all-to-all(f32[16,24,512]{2,1,0:T(8,128)S(1)} %bitcast.40), channel_id=1, replica_groups=mesh['z'=12,'xl'=2,'core'=2,'xh'=2,'y'=8] {'xh','y'}, dimensions={0} | all-to-all | bytes 1572864 | tf_op jit(solution)/shard_map/all_to_all | solution.py:17
  191.3 2.9 %collective-permute-start.4 = (f32[24,256]{1,0:T(8,128)S(1)}, f32[24,256]{1,0:T(8,128)S(1)}, u32[]{:S(2)}, u32[]{:S(2)}) collective-permute-start(f32[24,256]{1,0:T(8,128)S(1)} %get-tuple-element.30), channel_id=1, source_target_pairs={{0,32},{32,0},{1,33},{33,1},{2,34},{34,2},{3,35},{35,3},{4,36},{36... | collective-permute-start | bytes 73736 | tf_op jit(solution)/shard_map/ppermute | solution.py:13
  194.2 2.8 %collective-permute-done.4 = f32[24,256]{1,0:T(8,128)S(1)} collective-permute-done((f32[24,256]{1,0:T(8,128)S(1)}, f32[24,256]{1,0:T(8,128)S(1)}, u32[]{:S(2)}, u32[]{:S(2)}) %collective-permute-start.4) | collective-permute-done | bytes 24608 | tf_op jit(solution)/shard_map/ppermute | solution.py:13
  197.9 4.2 %all-to-all-start.4 = ((f32[16,2,24,256]{3,2,1,0:T(8,128)}), f32[16,2,24,256]{3,2,1,0:T(8,128)}, u32[]{:S(2)}, u32[]{:S(2)}) async-start(f32[16,2,24,256]{3,2,1,0:T(8,128)} %broadcast_in_dim.5), calls=%async_computation.4 | async-start | bytes 1572864 | tf_op jit(solution)/shard_map/all_to_all | solution.py:22
  202.2 1.4 copy.30
  203.6 20.0 %all-to-all-done.4 = f32[16,2,24,256]{3,2,1,0:T(8,128)} async-done(((f32[16,2,24,256]{3,2,1,0:T(8,128)}), f32[16,2,24,256]{3,2,1,0:T(8,128)}, u32[]{:S(2)}, u32[]{:S(2)}) %all-to-all-start.4) | async-done | bytes 786464 | tf_op jit(solution)/shard_map/all_to_all | solution.py:22
  224.9 3.1 %subtract_convert_fusion = (bf16[768,256]{0,1:T(8,128)(2,1)S(1)}, f32[768,256]{0,1:T(8,128)}) fusion(f32[768,256]{0,1:T(8,128)S(1)} %copy.30, f32[768,256]{1,0:T(8,128)S(1)} %bitcast.38, f32[768,768]{1,0:T(8,128)S(1)} %copy-done), kind=kOutput, calls=%fused_computation.6 | convolution fusion | flops 906952704 | bytes 5111808 | tf_op jit(solution)/shard_map/dot_general | solution.py:76
  228.0 2.3 copy.32
  (32 shorter events, 9.9 us)
Async XLA Ops:
  0.6 1.7 copy-start
  5.7 40.4 %all-to-all-start = ((f32[16,2,24,256]{3,2,1,0:T(8,128)}), f32[16,2,24,256]{3,2,1,0:T(8,128)S(1)}, u32[]{:S(2)}, u32[]{:S(2)}) async-start(f32[16,2,24,256]{3,2,1,0:T(8,128)} %copy.26), calls=%async_computation | async-start | bytes 1572864 | tf_op jit(solution)/shard_map/all_to_all | solution.py:17
  18.6 24.9 %collective-permute-start = (f32[256,768]{1,0:T(8,128)}, f32[256,768]{1,0:T(8,128)}, u32[]{:S(2)}, u32[]{:S(2)}) collective-permute-start(f32[256,768]{1,0:T(8,128)} %param.11), channel_id=1, source_target_pairs={{0,32},{32,0},{1,33},{33,1},{2,34},{34,2},{3,35},{35,3},{4,36},{36... | collective-permute-start | bytes 2359304 | tf_op jit(solution)/shard_map/ppermute | solution.py:13
  46.2 5.7 %collective-permute-start.1 = (f32[24,256]{1,0:T(8,128)S(1)}, f32[24,256]{1,0:T(8,128)S(1)}, u32[]{:S(2)}, u32[]{:S(2)}) collective-permute-start(f32[24,256]{1,0:T(8,128)S(1)} %get-tuple-element.32), channel_id=1, source_target_pairs={{0,32},{32,0},{1,33},{33,1},{2,34},{34,2},{3,35},{35,3},{4,36},{36... | collective-permute-start | bytes 73736 | tf_op jit(solution)/shard_map/ppermute | solution.py:13
  52.9 29.1 %all-to-all-start.1 = ((f32[16,24,512]{2,1,0:T(8,128)}), f32[16,24,512]{2,1,0:T(8,128)S(1)}, u32[]{:S(2)}, u32[]{:S(2)}) async-start(f32[16,24,512]{2,1,0:T(8,128)} %broadcast_in_dim.4), calls=%async_computation.1 | async-start | bytes 1572864 | tf_op jit(solution)/shard_map/all_to_all | solution.py:22
  82.0 1.4 copy-start.1
  84.1 3.9 %collective-permute-start.2 = (f32[192,768]{1,0:T(8,128)S(1)}, f32[192,768]{1,0:T(8,128)S(1)}, u32[]{:S(2)}, u32[]{:S(2)}) collective-permute-start(f32[192,768]{1,0:T(8,128)S(1)} %fusion.4), channel_id=1, source_target_pairs={{0,16},{16,0},{1,17},{17,1},{2,18},{18,2},{3,19},{19,3},{4,20},{20... | collective-permute-start | bytes 1769480 | tf_op jit(solution)/shard_map/ppermute | solution.py:13
  88.7 43.2 %copy-start.3 = (f32[16,768]{1,0:T(8,128)S(1)}, f32[16,768]{1,0:T(8,128)}, u32[]{:S(2)}) copy-start(f32[16,768]{1,0:T(8,128)} %param.8) | copy-start | bytes 147460
  88.8 43.2 %copy-start.4 = (f32[16,768]{1,0:T(8,128)S(1)}, f32[16,768]{1,0:T(8,128)}, u32[]{:S(2)}) copy-start(f32[16,768]{1,0:T(8,128)} %param.9) | copy-start | bytes 147460
  132.6 28.8 %copy-start.2 = (f32[512,768]{1,0:T(8,128)S(1)}, f32[512,768]{1,0:T(8,128)}, u32[]{:S(2)}) copy-start(f32[512,768]{1,0:T(8,128)} %pad_maximum_fusion) | copy-start | bytes 4718596
  157.2 4.3 %collective-permute-start.3 = (f32[192,768]{1,0:T(8,128)S(1)}, f32[192,768]{1,0:T(8,128)S(1)}, u32[]{:S(2)}, u32[]{:S(2)}) collective-permute-start(f32[192,768]{1,0:T(8,128)S(1)} %all_gather.3), channel_id=1, source_target_pairs={{0,16},{16,0},{1,17},{17,1},{2,18},{18,2},{3,19},{19,3},{4,20},{20... | collective-permute-start | bytes 1769480 | tf_op jit(solution)/shard_map/ppermute | solution.py:13
  191.3 5.7 %collective-permute-start.4 = (f32[24,256]{1,0:T(8,128)S(1)}, f32[24,256]{1,0:T(8,128)S(1)}, u32[]{:S(2)}, u32[]{:S(2)}) collective-permute-start(f32[24,256]{1,0:T(8,128)S(1)} %get-tuple-element.30), channel_id=1, source_target_pairs={{0,32},{32,0},{1,33},{33,1},{2,34},{34,2},{3,35},{35,3},{4,36},{36... | collective-permute-start | bytes 73736 | tf_op jit(solution)/shard_map/ppermute | solution.py:13
  197.9 25.6 %all-to-all-start.4 = ((f32[16,2,24,256]{3,2,1,0:T(8,128)}), f32[16,2,24,256]{3,2,1,0:T(8,128)}, u32[]{:S(2)}, u32[]{:S(2)}) async-start(f32[16,2,24,256]{3,2,1,0:T(8,128)} %broadcast_in_dim.5), calls=%async_computation.4 | async-start | bytes 1572864 | tf_op jit(solution)/shard_map/all_to_all | solution.py:22

commit v3 on v1

v3 whole, which is shorter than its diff:
```python
import jax
import jax.numpy as jnp
from jax import lax
from jax.sharding import Mesh, PartitionSpec as P

STEP = 10
ROW = ("z", "xl", "core")
COL = ("xh", "y")
HIGH = lax.Precision.HIGH


def swap(x, axis):
    return lax.ppermute(x, axis, [(0, 1), (1, 0)])


def cross(x):
    return lax.ppermute(x, ("xl", "xh"), [(0, 3), (3, 0), (1, 2), (2, 1)])


def exchange(x, axes):
    return lax.all_to_all(x, axes, 0, 0, tiled=True)


def mine_first(x, index):
    return jnp.where(index == 0, x, x[::-1])


def shards(master_weight, gradient, first_moment, second_moment, left_basis, right_basis):
    own, cols = first_moment.shape
    window = left_basis.shape[1]
    depth = lax.axis_size("z")
    peers = lax.axis_size("y")
    few = own // 2
    piece = window // 4 // peers
    keys = gradient.shape[1]
    core, xl, xh = lax.axis_index("core"), lax.axis_index("xl"), lax.axis_index("xh")
    correction = 1.0 - 0.95**STEP

    by_xl, by_both = swap(right_basis, "xl"), cross(right_basis)

    partial_left = lax.dot_general(
        left_basis, gradient.astype(jnp.float32), (((0,), (0,)), ((), ())), precision=HIGH
    )
    parts = partial_left.reshape(depth, 2, 2, 2, few, keys).transpose(1, 3, 0, 2, 4, 5)
    parts = exchange(parts.reshape(4 * peers, piece, keys), ("xl", "xh", "y"))
    parts, by_xl, by_both = lax.optimization_barrier((parts, by_xl, by_both))
    left_chunk = jnp.sum(parts.reshape(2, 2 * peers, piece, keys), axis=1)
    left_chunk = mine_first(left_chunk, xl).transpose(1, 0, 2).reshape(piece, 2 * keys)
    left_rotated = exchange(jnp.broadcast_to(left_chunk[None], (peers, piece, 2 * keys)), "y")

    middle = right_basis.shape[0] // 2
    by_xh = jnp.concatenate([swap(by_both[:middle], "xl"), cross(by_xl[middle:])])
    basis_own = jnp.concatenate([right_basis, by_xl])
    basis_other = jnp.concatenate([by_xh, by_both])

    grouped = left_rotated.reshape(depth, 2, few, 2 * keys)

    def half(which):
        picked = lax.dynamic_index_in_dim(grouped, which, 1, keepdims=False)
        picked = picked.reshape(depth * few, 2 * keys)
        return jnp.stack(
            [jnp.dot(picked, basis_own, precision=HIGH), jnp.dot(picked, basis_other, precision=HIGH)]
        )

    theirs = swap(half(1 - core), "core")
    summed = mine_first(half(core) + theirs, xh).reshape(2, depth, few, cols)
    summed = summed.transpose(1, 0, 2, 3).reshape(2 * depth, few, cols)
    rotated = jnp.sum(exchange(summed, ("z", "xh")).reshape(depth, own, cols), axis=0)

    new_first = 0.95 * first_moment + 0.05 * rotated
    new_second = 0.95 * second_moment + 0.05 * rotated * rotated
    normed = new_first / correction / (jnp.sqrt(new_second / correction) + 1e-08)

    copies = jnp.broadcast_to(normed.reshape(1, 2, few, cols), (depth, 2, few, cols))
    column = exchange(copies.reshape(2 * depth, few, cols), ("z", "xh"))
    other = swap(column, "core")
    contract = (((1,), (1,)), ((), ()))

    def rotate_back(x):
        x = x.reshape(depth, 2, few, cols).transpose(1, 0, 2, 3).reshape(2, depth * few, cols)
        x = mine_first(x, xh)
        return lax.dot_general(x[0], basis_own, contract, precision=HIGH) + lax.dot_general(
            x[1], basis_other, contract, precision=HIGH
        )

    back_part = jnp.concatenate([rotate_back(column), rotate_back(other)])
    back_part = back_part.reshape(peers, piece, 2, keys).transpose(2, 0, 1, 3)
    back_part = mine_first(back_part, xl).reshape(2 * peers, piece, keys)
    back_chunk = exchange(back_part, ("xl", "y")).reshape(2, peers, piece, keys)
    back_chunk = jnp.sum(back_chunk, axis=1)
    copies = jnp.broadcast_to(back_chunk[None], (2 * peers, 2, piece, keys))
    back = exchange(copies, COL).reshape(2, peers, 2, piece, keys).transpose(0, 2, 1, 3, 4)
    back = back.reshape(2, 2, 2, depth, few, keys)
    back = jnp.where(core == 0, back, back[:, :, ::-1])
    back = back.transpose(3, 1, 2, 0, 4, 5).reshape(window, keys)
    direction = jnp.dot(left_basis, back, precision=HIGH)
    new_weight = (master_weight - 0.003 * (direction + 0.1 * master_weight)).astype(jnp.bfloat16)
    return (new_weight, direction, new_first, new_second)


def solution(mesh):
    fine = Mesh(mesh.devices.reshape(12, 2, 2, 2, 8), ROW + COL)
    in_specs = (P(COL, ROW), P(COL, ROW), P(ROW, COL), P(ROW, COL), P(COL, None), P(ROW, COL))
    out_specs = (P(COL, ROW), P(COL, ROW), P(ROW, COL), P(ROW, COL))
    return jax.shard_map(shards, mesh=fine, in_specs=in_specs, out_specs=out_specs, check_vma=False)
```

time: 248 us -> 236 us (0.952)
  the two profiles are of different devices: /device:TPU:4 before, /device:TPU:8 now
where the time goes in v3:
time: 236 us; the launch traced here: 234 us
  blocking collectives  97.9 us (41%)
  waiting for transfers between devices  45.5 us (19%)
  starting transfers between devices  43.4 us (18%)
  matrix products  22.5 us (10%)
  local copies, waits for them, and re-layouts  22.1 us (9%)
    all_to_all x3, blocking collectives, exchange(): return lax.all_to_all(x, axes, 0, 0, tiled=True)  97.9 us
    all_to_all x3, starting transfers between devices, exchange(): return lax.all_to_all(x, axes, 0, 0, tiled=True)  26.9 us
    all_to_all x3, waiting for transfers between devices, exchange(): return lax.all_to_all(x, axes, 0, 0, tiled=True)  20 us
    ppermute x4, waiting for transfers between devices, swap(): return lax.ppermute(x, axis, [(0, 1), (1, 0)])  19.9 us
    unnamed x12, local copies, waits for them, and re-layouts  9.89 us
    ppermute x4, starting transfers between devices, swap(): return lax.ppermute(x, axis, [(0, 1), (1, 0)])  9.29 us
    ppermute x2, starting transfers between devices, cross(): return lax.ppermute(x, ('xl', 'xh'), [(0, 3), (3, 0), (1, 2), (2, 1)])  7.25 us
    ppermute x2, waiting for transfers between devices, cross(): return lax.ppermute(x, ('xl', 'xh'), [(0, 3), (3, 0), (1, 2), (2, 1)])  5.58 us
  transfers between devices with their start and end apart: 9, of which 5 were waited for; matrix products, arithmetic and copies ran while one was open for 7% of the time, Pallas kernels for 0%

profile of v3, /device:TPU:8, one launch (start us, length us, event | category | flops | bytes accessed | tf_op | source)
XLA Modules:
  0.0 234.2 jit_solution(6976680494616237572)
XLA Ops:
  2.3 2.4 %fusion.19 = f32[768,256]{1,0:T(8,128)S(1)} fusion(f32[768,768]{1,0:T(8,128)S(1)} %copy-done, bf16[768,256]{1,0:T(8,128)(2,1)} %param.7), kind=kOutput, calls=%fused_computation.53 | convolution fusion | flops 905969664 | bytes 3538944 | tf_op jit(solution)/shard_map/dot_general | solution.py:41
  5.7 13.0 %all-to-all-start = ((f32[32,24,256]{2,1,0:T(8,128)}), f32[32,24,256]{2,1,0:T(8,128)S(1)}, u32[]{:S(2)}, u32[]{:S(2)}) async-start(f32[32,24,256]{2,1,0:T(8,128)} %bitcast.97), calls=%async_computation | async-start | bytes 1572864 | tf_op jit(solution)/shard_map/all_to_all | solution.py:21
  18.7 3.5 %collective-permute-start = (f32[256,768]{1,0:T(8,128)}, f32[256,768]{1,0:T(8,128)}, u32[]{:S(2)}, u32[]{:S(2)}) collective-permute-start(f32[256,768]{1,0:T(8,128)} %param.11), channel_id=1, source_target_pairs={{0,32},{32,0},{1,33},{33,1},{2,34},{34,2},{3,35},{35,3},{4,36},{36... | collective-permute-start | bytes 2359304 | tf_op jit(solution)/shard_map/ppermute | solution.py:13
  22.2 3.9 %collective-permute-start.1 = (f32[256,768]{1,0:T(8,128)}, f32[256,768]{1,0:T(8,128)}, u32[]{:S(2)}, u32[]{:S(2)}) collective-permute-start(f32[256,768]{1,0:T(8,128)} %param.11), channel_id=1, source_target_pairs={{0,40},{40,0},{8,32},{32,8},{1,41},{41,1},{9,33},{33,9},{2,42},{42... | collective-permute-start | bytes 2359304 | tf_op jit(solution)/shard_map/ppermute | solution.py:17
  26.2 18.0 %collective-permute-done = f32[256,768]{1,0:T(8,128)} collective-permute-done((f32[256,768]{1,0:T(8,128)}, f32[256,768]{1,0:T(8,128)}, u32[]{:S(2)}, u32[]{:S(2)}) %collective-permute-start) | collective-permute-done | bytes 786464 | tf_op jit(solution)/shard_map/ppermute | solution.py:13
  44.1 2.8 %collective-permute-done.1 = f32[256,768]{1,0:T(8,128)} collective-permute-done((f32[256,768]{1,0:T(8,128)}, f32[256,768]{1,0:T(8,128)}, u32[]{:S(2)}, u32[]{:S(2)}) %collective-permute-start.1) | collective-permute-done | bytes 786464 | tf_op jit(solution)/shard_map/ppermute | solution.py:17
  48.7 2.0 collective-permute-start.2
  51.6 6.9 %all-to-all-start.1 = ((f32[8,24,512]{2,1,0:T(8,128)}), f32[8,24,512]{2,1,0:T(8,128)S(1)}, u32[]{:S(2)}, u32[]{:S(2)}) async-start(f32[8,24,512]{2,1,0:T(8,128)} %broadcast_in_dim.21), calls=%async_computation.1 | async-start | bytes 786432 | tf_op jit(solution)/shard_map/all_to_all | solution.py:21
  60.2 3.3 %collective-permute-start.3 = (f32[128,768]{1,0:T(8,128)}, f32[128,768]{1,0:T(8,128)S(1)}, u32[]{:S(2)}, u32[]{:S(2)}) collective-permute-start(f32[128,768]{1,0:T(8,128)} %slice.19), channel_id=1, source_target_pairs={{0,40},{40,0},{8,32},{32,8},{1,41},{41,1},{9,33},{33,9},{2,42},{42... | collective-permute-start | bytes 1179656 | tf_op jit(solution)/shard_map/ppermute | solution.py:17
  63.5 2.1 constant_dynamic-update-slice_fusion.1
  65.6 2.1 constant_dynamic-update-slice_fusion
  68.5 2.8 %collective-permute-done.3 = f32[128,768]{1,0:T(8,128)S(1)} collective-permute-done((f32[128,768]{1,0:T(8,128)}, f32[128,768]{1,0:T(8,128)S(1)}, u32[]{:S(2)}, u32[]{:S(2)}) %collective-permute-start.3) | collective-permute-done | bytes 393248 | tf_op jit(solution)/shard_map/ppermute | solution.py:17
  72.0 2.1 constant_dynamic-update-slice_fusion.2
  85.0 44.5 %all_to_all.30 = f32[24,8,768]{2,1,0:T(8,128)S(1)} all-to-all(f32[24,8,768]{2,1,0:T(8,128)S(1)} %bitcast.102), channel_id=1, replica_groups=mesh['z'=12,'xl'=2,'core'=2,'xh'=2,'y'=8] {'z','xh'}, dimensions={0} | all-to-all | bytes 1179648 | tf_op jit(solution)/shard_map/all_to_all | solution.py:21
  130.4 32.9 %all_to_all.31 = f32[24,8,768]{2,1,0:T(8,128)S(1)} all-to-all(f32[24,8,768]{2,1,0:T(8,128)S(1)} %bitcast.104), channel_id=1, replica_groups=mesh['z'=12,'xl'=2,'core'=2,'xh'=2,'y'=8] {'z','xh'}, dimensions={0} | all-to-all | bytes 1179648 | tf_op jit(solution)/shard_map/all_to_all | solution.py:21
  167.3 2.3 fusion.3
  169.6 2.3 convolution_add_fusion.1
  171.9 2.3 fusion.2
  174.1 2.3 convolution_add_fusion
  176.8 20.4 %all_to_all.32 = f32[16,24,256]{2,1,0:T(8,128)S(1)} all-to-all(f32[16,24,256]{2,1,0:T(8,128)S(1)} %bitcast.106), channel_id=1, replica_groups=mesh['z'=12,'xl'=2,'core'=2,'xh'=2,'y'=8] {'xl','y'}, dimensions={0} | all-to-all | bytes 786432 | tf_op jit(solution)/shard_map/all_to_all | solution.py:21
  198.2 7.0 %all-to-all-start.5 = ((f32[16,2,24,256]{3,2,1,0:T(8,128)}), f32[16,2,24,256]{3,2,1,0:T(8,128)}, u32[]{:S(2)}, u32[]{:S(2)}) async-start(f32[16,2,24,256]{3,2,1,0:T(8,128)} %broadcast_in_dim.24), calls=%async_computation.5 | async-start | bytes 1572864 | tf_op jit(solution)/shard_map/all_to_all | solution.py:21
  206.6 20.0 %all-to-all-done.5 = f32[16,2,24,256]{3,2,1,0:T(8,128)} async-done(((f32[16,2,24,256]{3,2,1,0:T(8,128)}), f32[16,2,24,256]{3,2,1,0:T(8,128)}, u32[]{:S(2)}, u32[]{:S(2)}) %all-to-all-start.5) | async-done | bytes 786464 | tf_op jit(solution)/shard_map/all_to_all | solution.py:21
  227.9 3.1 %subtract_convert_fusion = (bf16[768,256]{0,1:T(8,128)(2,1)S(1)}, f32[768,256]{0,1:T(8,128)}) fusion(f32[768,256]{0,1:T(8,128)S(1)} %copy.43, f32[768,256]{1,0:T(8,128)S(1)} %bitcast.95, f32[768,768]{1,0:T(8,128)S(1)} %copy-done), kind=kOutput, calls=%fused_computation.13 | convolution fusion | flops 906952704 | bytes 5111808 | tf_op jit(solution)/shard_map/dot_general | solution.py:96
  231.0 2.3 copy.45
  (47 shorter events, 29.2 us)
Async XLA Ops:
  0.6 1.7 copy-start
  5.7 41.2 %all-to-all-start = ((f32[32,24,256]{2,1,0:T(8,128)}), f32[32,24,256]{2,1,0:T(8,128)S(1)}, u32[]{:S(2)}, u32[]{:S(2)}) async-start(f32[32,24,256]{2,1,0:T(8,128)} %bitcast.97), calls=%async_computation | async-start | bytes 1572864 | tf_op jit(solution)/shard_map/all_to_all | solution.py:21
  18.7 25.4 %collective-permute-start = (f32[256,768]{1,0:T(8,128)}, f32[256,768]{1,0:T(8,128)}, u32[]{:S(2)}, u32[]{:S(2)}) collective-permute-start(f32[256,768]{1,0:T(8,128)} %param.11), channel_id=1, source_target_pairs={{0,32},{32,0},{1,33},{33,1},{2,34},{34,2},{3,35},{35,3},{4,36},{36... | collective-permute-start | bytes 2359304 | tf_op jit(solution)/shard_map/ppermute | solution.py:13
  22.2 24.7 %collective-permute-start.1 = (f32[256,768]{1,0:T(8,128)}, f32[256,768]{1,0:T(8,128)}, u32[]{:S(2)}, u32[]{:S(2)}) collective-permute-start(f32[256,768]{1,0:T(8,128)} %param.11), channel_id=1, source_target_pairs={{0,40},{40,0},{8,32},{32,8},{1,41},{41,1},{9,33},{33,9},{2,42},{42... | collective-permute-start | bytes 2359304 | tf_op jit(solution)/shard_map/ppermute | solution.py:17
  48.7 19.0 %collective-permute-start.2 = (f32[128,768]{1,0:T(8,128)}, f32[128,768]{1,0:T(8,128)S(1)}, u32[]{:S(2)}, u32[]{:S(2)}) collective-permute-start(f32[128,768]{1,0:T(8,128)} %slice.18), channel_id=1, source_target_pairs={{0,32},{32,0},{1,33},{33,1},{2,34},{34,2},{3,35},{35,3},{4,36},{36... | collective-permute-start | bytes 1179656 | tf_op jit(solution)/shard_map/ppermute | solution.py:13
  51.6 22.6 %all-to-all-start.1 = ((f32[8,24,512]{2,1,0:T(8,128)}), f32[8,24,512]{2,1,0:T(8,128)S(1)}, u32[]{:S(2)}, u32[]{:S(2)}) async-start(f32[8,24,512]{2,1,0:T(8,128)} %broadcast_in_dim.21), calls=%async_computation.1 | async-start | bytes 786432 | tf_op jit(solution)/shard_map/all_to_all | solution.py:21
  60.2 11.1 %collective-permute-start.3 = (f32[128,768]{1,0:T(8,128)}, f32[128,768]{1,0:T(8,128)S(1)}, u32[]{:S(2)}, u32[]{:S(2)}) collective-permute-start(f32[128,768]{1,0:T(8,128)} %slice.19), channel_id=1, source_target_pairs={{0,40},{40,0},{8,32},{32,8},{1,41},{41,1},{9,33},{33,9},{2,42},{42... | collective-permute-start | bytes 1179656 | tf_op jit(solution)/shard_map/ppermute | solution.py:17
  78.9 5.9 %collective-permute-start.4 = (f32[2,96,768]{2,1,0:T(8,128)}, f32[2,96,768]{2,1,0:T(8,128)S(1)}, u32[]{:S(2)}, u32[]{:S(2)}) collective-permute-start(f32[2,96,768]{2,1,0:T(8,128)} %pad_maximum_fusion), channel_id=1, source_target_pairs={{0,16},{16,0},{1,17},{17,1},{2,18},{18,2},{3,19},{19,3},{4,20},{20... | collective-permute-start | bytes 1769480 | tf_op jit(solution)/shard_map/ppermute | solution.py:13
  85.0 44.7 %copy-start.1 = (f32[16,768]{1,0:T(8,128)S(1)}, f32[16,768]{1,0:T(8,128)}, u32[]{:S(2)}) copy-start(f32[16,768]{1,0:T(8,128)} %param.8) | copy-start | bytes 147460
  85.0 44.7 %copy-start.2 = (f32[16,768]{1,0:T(8,128)S(1)}, f32[16,768]{1,0:T(8,128)}, u32[]{:S(2)}) copy-start(f32[16,768]{1,0:T(8,128)} %param.9) | copy-start | bytes 147460
  163.3 3.9 %collective-permute-start.5 = (f32[24,8,768]{2,1,0:T(8,128)S(1)}, f32[24,8,768]{2,1,0:T(8,128)S(1)}, u32[]{:S(2)}, u32[]{:S(2)}) collective-permute-start(f32[24,8,768]{2,1,0:T(8,128)S(1)} %all_to_all.31), channel_id=1, source_target_pairs={{0,16},{16,0},{1,17},{17,1},{2,18},{18,2},{3,19},{19,3},{4,20},{20... | collective-permute-start | bytes 1769480 | tf_op jit(solution)/shard_map/ppermute | solution.py:13
  198.2 28.4 %all-to-all-start.5 = ((f32[16,2,24,256]{3,2,1,0:T(8,128)}), f32[16,2,24,256]{3,2,1,0:T(8,128)}, u32[]{:S(2)}, u32[]{:S(2)}) async-start(f32[16,2,24,256]{3,2,1,0:T(8,128)} %broadcast_in_dim.24), calls=%async_computation.5 | async-start | bytes 1572864 | tf_op jit(solution)/shard_map/all_to_all | solution.py:21

commit v4 on v3

v4 whole, which is shorter than its diff:
```python
import jax
import jax.numpy as jnp
from jax import lax
from jax.sharding import Mesh, PartitionSpec as P

STEP = 10
ROW = ("z", "xl", "core")
COL = ("xh", "y")
HIGH = lax.Precision.HIGH


def swap(x, axis):
    return lax.ppermute(x, axis, [(0, 1), (1, 0)])


def exchange(x, axes):
    return lax.all_to_all(x, axes, 0, 0, tiled=True)


def shards(master_weight, gradient, first_moment, second_moment, left_basis, right_basis):
    own, cols = first_moment.shape
    window = left_basis.shape[1]
    depth = lax.axis_size("z")
    peers = lax.axis_size("y")
    few = own // 2
    piece = window // 4 // peers
    keys = gradient.shape[1]
    core = lax.axis_index("core")
    correction = 1.0 - 0.95**STEP

    basis = lax.all_gather(right_basis, ("xh", "xl"), axis=0, tiled=True)
    basis = basis.reshape(2, 2, keys, cols).swapaxes(0, 1)

    partial_left = lax.dot_general(
        left_basis, gradient.astype(jnp.float32), (((0,), (0,)), ((), ())), precision=HIGH
    )
    parts = partial_left.reshape(depth, 2, 2, 2, few, keys).transpose(1, 3, 0, 2, 4, 5)
    parts = exchange(parts.reshape(4 * peers, piece, keys), ("xl", "xh", "y"))
    left_chunk = jnp.sum(parts.reshape(2, 2 * peers, piece, keys), axis=1)
    left_chunk = left_chunk.transpose(1, 0, 2).reshape(piece, 2 * keys)
    left_rotated = exchange(jnp.broadcast_to(left_chunk[None], (peers, piece, 2 * keys)), "y")
    grouped = left_rotated.reshape(depth, 2, few, 2, keys)

    def half(which):
        picked = lax.dynamic_index_in_dim(grouped, which, 1, keepdims=False)
        picked = picked.reshape(depth * few, 2, keys)

        def block(xh):
            return jnp.dot(picked[:, 0], basis[0, xh], precision=HIGH) + jnp.dot(
                picked[:, 1], basis[1, xh], precision=HIGH
            )

        return jnp.stack([block(0), block(1)])

    theirs = swap(half(1 - core), "core")
    summed = (half(core) + theirs).reshape(2, depth, few, cols)
    summed = summed.transpose(1, 0, 2, 3).reshape(2 * depth, few, cols)
    rotated = jnp.sum(exchange(summed, ("z", "xh")).reshape(depth, own, cols), axis=0)

    new_first = 0.95 * first_moment + 0.05 * rotated
    new_second = 0.95 * second_moment + 0.05 * rotated * rotated
    normed = new_first / correction / (jnp.sqrt(new_second / correction) + 1e-08)

    copies = jnp.broadcast_to(normed.reshape(1, 2, few, cols), (depth, 2, few, cols))
    column = exchange(copies.reshape(2 * depth, few, cols), ("z", "xh"))
    other = swap(column, "core")
    contract = (((1,), (1,)), ((), ()))

    def rotate_back(x):
        x = x.reshape(depth, 2, few, cols).transpose(1, 0, 2, 3).reshape(2, depth * few, cols)

        def block(xl):
            return lax.dot_general(x[0], basis[xl, 0], contract, precision=HIGH) + lax.dot_general(
                x[1], basis[xl, 1], contract, precision=HIGH
            )

        return jnp.stack([block(0), block(1)])

    back_part = jnp.concatenate([rotate_back(column), rotate_back(other)], axis=1)
    back_part = back_part.reshape(2 * peers, piece, keys)
    back_chunk = exchange(back_part, ("xl", "y")).reshape(2, peers, piece, keys)
    back_chunk = jnp.sum(back_chunk, axis=1)
    copies = jnp.broadcast_to(back_chunk[None], (2 * peers, 2, piece, keys))
    back = exchange(copies, COL).reshape(2, peers, 2, piece, keys).transpose(0, 2, 1, 3, 4)
    back = back.reshape(2, 2, 2, depth, few, keys)
    back = jnp.where(core == 0, back, back[:, :, ::-1])
    back = back.transpose(3, 1, 2, 0, 4, 5).reshape(window, keys)
    direction = jnp.dot(left_basis, back, precision=HIGH)
    new_weight = (master_weight - 0.003 * (direction + 0.1 * master_weight)).astype(jnp.bfloat16)
    return (new_weight, direction, new_first, new_second)


def solution(mesh):
    fine = Mesh(mesh.devices.reshape(12, 2, 2, 2, 8), ROW + COL)
    in_specs = (P(COL, ROW), P(COL, ROW), P(ROW, COL), P(ROW, COL), P(COL, None), P(ROW, COL))
    out_specs = (P(COL, ROW), P(COL, ROW), P(ROW, COL), P(ROW, COL))
    return jax.shard_map(shards, mesh=fine, in_specs=in_specs, out_specs=out_specs, check_vma=False)
```

time: 236 us -> 220 us (0.932)
  starting transfers between devices: 43.4 us -> 13.7 us
  blocking collectives: 97.9 us -> 126 us
  between operations: 0.96 us -> 14.4 us
  local copies, waits for them, and re-layouts: 22.1 us -> 9.19 us
  waiting for transfers between devices: 45.5 us -> 38.2 us
  matrix products: 22.5 us -> 16 us
    all_to_all x3 -> x4, blocking collectives: 97.9 us -> 126 us  [exchange(): return lax.all_to_all(x, axes, 0, 0, tiled=True)]
    ppermute x4 -> x2, waiting for transfers between devices: 19.9 us -> 0.52 us  [swap(): return lax.ppermute(x, axis, [(0, 1), (1, 0)])]
    all_to_all x3 -> x2, starting transfers between devices: 26.9 us -> 9.88 us  [exchange(): return lax.all_to_all(x, axes, 0, 0, tiled=True)]
    all_to_all x3 -> x2, waiting for transfers between devices: 20 us -> 30.6 us  [exchange(): return lax.all_to_all(x, axes, 0, 0, tiled=True)]
    ppermute x2 -> x0, starting transfers between devices: 7.25 us -> none  [cross(): return lax.ppermute(x, ('xl', 'xh'), [(0, 3), (3, 0), (1, 2), (2, 1)])]
    dot_general x8 -> x16, matrix products: 17 us -> 10.6 us  [the longest x4 3.79 us: block(): jnp.dot(picked[:, 0], basis[0, xh], precision=HIGH)]
    all_gather x0 -> x1, waiting for transfers between devices: none -> 6.35 us  [shards(): basis = lax.all_gather(right_basis, ('xh', 'xl'), axis=0, tiled=True)]
    ppermute x2 -> x0, waiting for transfers between devices: 5.58 us -> none  [cross(): return lax.ppermute(x, ('xl', 'xh'), [(0, 3), (3, 0), (1, 2), (2, 1)])]
  transfers between devices with their start and end apart: 9 -> 5, of which waited for: 5 -> 4; matrix products, arithmetic and copies ran while one was open for 7% -> 4% of each run, Pallas kernels for 0% -> 0%
where the time goes in v4:
time: 220 us; the launch traced here: 219 us
  blocking collectives  126 us (57%)
  waiting for transfers between devices  38.2 us (17%)
  matrix products  16 us (7%)
  between operations  14.4 us (7%)
  starting transfers between devices  13.7 us (6%)
  local copies, waits for them, and re-layouts  9.19 us (4%)
    all_to_all x4, blocking collectives, exchange(): return lax.all_to_all(x, axes, 0, 0, tiled=True)  126 us
    all_to_all x2, waiting for transfers between devices, exchange(): return lax.all_to_all(x, axes, 0, 0, tiled=True)  30.6 us
    all_to_all x2, starting transfers between devices, exchange(): return lax.all_to_all(x, axes, 0, 0, tiled=True)  9.88 us
    all_gather x1, waiting for transfers between devices, shards(): basis = lax.all_gather(right_basis, ('xh', 'xl'), axis=0, tiled=True)  6.35 us
    unnamed x11, local copies, waits for them, and re-layouts  5.54 us
  transfers between devices with their start and end apart: 5, of which 4 were waited for; matrix products, arithmetic and copies ran while one was open for 4% of the time, Pallas kernels for 0%

profile of v4, /device:TPU:8, one launch (start us, length us, event | category | flops | bytes accessed | tf_op | source)
XLA Modules:
  0.0 219.0 jit_solution(1409068215178470013)
XLA Ops:
  7.2 0.7 all-gather.2.cloned.1.call-update
  7.9 0.9 copy-done
  8.8 2.4 %fusion.20 = f32[768,256]{1,0:T(8,128)S(1)} fusion(f32[768,768]{1,0:T(8,128)S(1)} %copy-done, bf16[768,256]{1,0:T(8,128)(2,1)} %param.7), kind=kOutput, calls=%fused_computation.55 | convolution fusion | flops 905969664 | bytes 3538944 | tf_op jit(solution)/shard_map/dot_general | solution.py:34
  11.3 33.5 %all_to_all.30 = f32[32,24,256]{2,1,0:T(8,128)S(1)} all-to-all(f32[32,24,256]{2,1,0:T(8,128)S(1)} %bitcast.146), channel_id=1, replica_groups=mesh['z'=12,'xl'=2,'core'=2,'xh'=2,'y'=8] {'xl','xh','y'}, dimensions={0} | all-to-all | bytes 1572864 | tf_op jit(solution)/shard_map/all_to_all | solution.py:17
  44.9 0.8 broadcast_in_dim.21
  45.7 3.9 %all-to-all-start.1 = ((f32[8,24,512]{2,1,0:T(8,128)}), f32[8,24,512]{2,1,0:T(8,128)S(1)}, u32[]{:S(2)}, u32[]{:S(2)}) async-start(f32[8,24,512]{2,1,0:T(8,128)} %broadcast_in_dim.21), calls=%async_computation.1 | async-start | bytes 786432 | tf_op jit(solution)/shard_map/all_to_all | solution.py:17
  49.6 9.9 %all-to-all-done.1 = f32[8,24,512]{2,1,0:T(8,128)S(1)} async-done(((f32[8,24,512]{2,1,0:T(8,128)}), f32[8,24,512]{2,1,0:T(8,128)S(1)}, u32[]{:S(2)}, u32[]{:S(2)}) %all-to-all-start.1) | async-done | bytes 393248 | tf_op jit(solution)/shard_map/all_to_all | solution.py:17
  60.0 6.3 %all-gather.2.cloned.1.call-done = f32[1024,768]{1,0:T(8,128)} async-done(((f32[256,768]{1,0:T(8,128)}), f32[1024,768]{1,0:T(8,128)}) %all-gather.2.cloned.1.call-update) | async-done | bytes 3145744 | tf_op jit(solution)/shard_map/all_gather | solution.py:31
  66.3 1.6 fusion.10
  67.9 1.5 fusion.14
  69.4 1.5 fusion.1
  71.3 1.9 collective-permute-start
  75.3 39.8 %all_to_all.31 = f32[24,8,768]{2,1,0:T(8,128)S(1)} all-to-all(f32[24,8,768]{2,1,0:T(8,128)S(1)} %bitcast.151), channel_id=1, replica_groups=mesh['z'=12,'xl'=2,'core'=2,'xh'=2,'y'=8] {'z','xh'}, dimensions={0} | all-to-all | bytes 1179648 | tf_op jit(solution)/shard_map/all_to_all | solution.py:17
  115.9 32.6 %all_to_all.32 = f32[24,8,768]{2,1,0:T(8,128)S(1)} all-to-all(f32[24,8,768]{2,1,0:T(8,128)S(1)} %bitcast.153), channel_id=1, replica_groups=mesh['z'=12,'xl'=2,'core'=2,'xh'=2,'y'=8] {'z','xh'}, dimensions={0} | all-to-all | bytes 1179648 | tf_op jit(solution)/shard_map/all_to_all | solution.py:17
  148.5 1.9 collective-permute-start.1
  154.7 20.7 %all_to_all.33 = f32[16,24,256]{2,1,0:T(8,128)S(1)} all-to-all(f32[16,24,256]{2,1,0:T(8,128)S(1)} %bitcast.162), channel_id=1, replica_groups=mesh['z'=12,'xl'=2,'core'=2,'xh'=2,'y'=8] {'xl','y'}, dimensions={0} | all-to-all | bytes 786432 | tf_op jit(solution)/shard_map/all_to_all | solution.py:17
  175.4 1.0 broadcast_in_dim.24
  176.4 5.9 %all-to-all-start.5 = ((f32[16,2,24,256]{3,2,1,0:T(8,128)}), f32[16,2,24,256]{3,2,1,0:T(8,128)}, u32[]{:S(2)}, u32[]{:S(2)}) async-start(f32[16,2,24,256]{3,2,1,0:T(8,128)} %broadcast_in_dim.24), calls=%async_computation.5 | async-start | bytes 1572864 | tf_op jit(solution)/shard_map/all_to_all | solution.py:17
  182.3 1.4 copy.38
  183.7 20.7 %all-to-all-done.5 = f32[16,2,24,256]{3,2,1,0:T(8,128)} async-done(((f32[16,2,24,256]{3,2,1,0:T(8,128)}), f32[16,2,24,256]{3,2,1,0:T(8,128)}, u32[]{:S(2)}, u32[]{:S(2)}) %all-to-all-start.5) | async-done | bytes 786464 | tf_op jit(solution)/shard_map/all_to_all | solution.py:17
  204.4 1.2 copy.35
  205.8 3.1 %subtract_convert_fusion = (bf16[768,256]{0,1:T(8,128)(2,1)S(1)}, f32[768,256]{0,1:T(8,128)}) fusion(f32[768,256]{0,1:T(8,128)S(1)} %copy.38, f32[768,256]{1,0:T(8,128)S(1)} %bitcast.143, f32[768,768]{1,0:T(8,128)S(1)} %copy-done), kind=kOutput, calls=%fused_computation.24 | convolution fusion | flops 906952704 | bytes 5111808 | tf_op jit(solution)/shard_map/dot_general | solution.py:88
  208.9 2.3 %copy.40 = f32[768,256]{1,0:T(8,128)} copy(f32[768,256]{0,1:T(8,128)} %get-tuple-element.26) | data formatting | bytes 1572864
  211.2 0.9 copy.39
  (40 shorter events, 8.3 us)
Async XLA Ops:
  7.2 1.7 copy-start
  7.2 59.1 %all-gather.2.cloned.1.call-start = ((), (), s32[]{:S(2)}) async-start(), calls=%async_computation.6 | async-start | bytes 3932160 | tf_op jit(solution)/shard_map/all_gather | solution.py:31
  45.7 13.9 %all-to-all-start.1 = ((f32[8,24,512]{2,1,0:T(8,128)}), f32[8,24,512]{2,1,0:T(8,128)S(1)}, u32[]{:S(2)}, u32[]{:S(2)}) async-start(f32[8,24,512]{2,1,0:T(8,128)} %broadcast_in_dim.21), calls=%async_computation.1 | async-start | bytes 786432 | tf_op jit(solution)/shard_map/all_to_all | solution.py:17
  66.3 4.6 %copy-start.1 = (f32[1024,768]{1,0:T(8,128)S(1)}, f32[1024,768]{1,0:T(8,128)}, u32[]{:S(2)}) copy-start(f32[1024,768]{1,0:T(8,128)} %all-gather.2.cloned.1.call-done) | copy-start | bytes 9437188
  71.3 3.9 %collective-permute-start = (f32[2,96,768]{2,1,0:T(8,128)S(1)}, f32[2,96,768]{2,1,0:T(8,128)S(1)}, u32[]{:S(2)}, u32[]{:S(2)}) collective-permute-start(f32[2,96,768]{2,1,0:T(8,128)S(1)} %pad_maximum_fusion), channel_id=1, source_target_pairs={{0,16},{16,0},{1,17},{17,1},{2,18},{18,2},{3,19},{19,3},{4,20},{20... | collective-permute-start | bytes 1769480 | tf_op jit(solution)/shard_map/ppermute | solution.py:13
  74.3 40.8 %copy-start.2 = (f32[16,768]{1,0:T(8,128)S(1)}, f32[16,768]{1,0:T(8,128)}, u32[]{:S(2)}) copy-start(f32[16,768]{1,0:T(8,128)} %param.8) | copy-start | bytes 147460
  74.3 40.8 %copy-start.3 = (f32[16,768]{1,0:T(8,128)S(1)}, f32[16,768]{1,0:T(8,128)}, u32[]{:S(2)}) copy-start(f32[16,768]{1,0:T(8,128)} %param.9) | copy-start | bytes 147460
  148.5 4.1 %collective-permute-start.1 = (f32[24,8,768]{2,1,0:T(8,128)S(1)}, f32[24,8,768]{2,1,0:T(8,128)S(1)}, u32[]{:S(2)}, u32[]{:S(2)}) collective-permute-start(f32[24,8,768]{2,1,0:T(8,128)S(1)} %all_to_all.32), channel_id=1, source_target_pairs={{0,16},{16,0},{1,17},{17,1},{2,18},{18,2},{3,19},{19,3},{4,20},{20... | collective-permute-start | bytes 1769480 | tf_op jit(solution)/shard_map/ppermute | solution.py:13
  176.4 28.0 %all-to-all-start.5 = ((f32[16,2,24,256]{3,2,1,0:T(8,128)}), f32[16,2,24,256]{3,2,1,0:T(8,128)}, u32[]{:S(2)}, u32[]{:S(2)}) async-start(f32[16,2,24,256]{3,2,1,0:T(8,128)} %broadcast_in_dim.24), calls=%async_computation.5 | async-start | bytes 1572864 | tf_op jit(solution)/shard_map/all_to_all | solution.py:17
Sparse Core Ops, SparseCore 0:
  10.4 55.8 all-gather.1

commit v5 on v1

v5 whole, which is shorter than its diff:
```python
import jax
import jax.numpy as jnp
from jax import lax
from jax.experimental import pallas as pl
from jax.experimental.pallas import tpu as pltpu
from jax.sharding import Mesh, PartitionSpec as P

STEP = 10
LANES = 128
ROW = ("z", "xl", "core")
COL = ("xh", "y")


def exchange(x, axes):
    return lax.all_to_all(x, axes, 0, 0, tiled=True)


def copies_to(x, axes):
    return exchange(jnp.broadcast_to(x[None], (lax.axis_size(axes),) + x.shape), axes)


def split(x):
    high = x.astype(jnp.bfloat16)
    return high, (x - high.astype(jnp.float32)).astype(jnp.bfloat16)


def three_passes(a, b, contract):
    a_high, a_low = a
    b_high, b_low = b

    def one(x, y):
        return lax.dot_general(x, y, (contract, ((), ())), preferred_element_type=jnp.float32)

    return one(a_high, b_high) + (one(a_high, b_low) + one(a_low, b_high))


def start_kernel(left_ref, gradient_ref, out_ref, total, rows):
    step = pl.program_id(0)
    high, low = split(left_ref[...])

    def one(x):
        return lax.dot_general(
            x, gradient_ref[...], (((0,), (0,)), ((), ())), preferred_element_type=jnp.float32
        )

    part = one(high) + one(low)

    @pl.when(step == 0)
    def _():
        total[...] = part

    @pl.when(step > 0)
    def _():
        total[...] += part

    @pl.when(step == pl.num_programs(0) - 1)
    def _():
        peers, piece, few = out_ref.shape[2], out_ref.shape[3] // 2, 8
        for ring in range(4):
            for xh in range(2):
                for z in range(total.shape[0] // 64):
                    at = 64 * z + 16 * ring + few * xh
                    rows[few * z : few * (z + 1), :] = total[at : at + few, :]
                for y in range(peers):
                    for part_of in range(2):
                        out_ref[ring, xh, y, piece * part_of : piece * (part_of + 1), :] = rows[
                            piece * y : piece * (y + 1), LANES * part_of : LANES * (part_of + 1)
                        ]


def start(left_basis, gradient, peers):
    height, window = left_basis.shape
    keys = gradient.shape[1]
    block = height // 3
    shape = (4, 2, peers, window // 8 // peers * (keys // LANES), LANES)
    return pl.pallas_call(
        start_kernel,
        grid=(3,),
        in_specs=[
            pl.BlockSpec((block, window), lambda i: (i, 0)),
            pl.BlockSpec((block, keys), lambda i: (i, 0)),
        ],
        out_specs=pl.BlockSpec(shape, lambda i: (0,) * 5),
        out_shape=jax.ShapeDtypeStruct(shape, jnp.float32),
        scratch_shapes=[
            pltpu.VMEM((window, keys), jnp.float32),
            pltpu.VMEM((window // 8, keys), jnp.float32),
        ],
        compiler_params=pltpu.CompilerParams(vmem_limit_bytes=60 * 2**20),
        cost_estimate=pl.CostEstimate(
            flops=4 * height * window * keys, bytes_accessed=4_000_000, transcendentals=0
        ),
    )(left_basis, gradient)


def forth_kernel(left_ref, basis_ref, out_ref, rows, high, low):
    @pl.when((pl.program_id(0) == 0) & (pl.program_id(1) == 0))
    def _():
        peers, tiles = left_ref.shape[0], rows.shape[1] // LANES
        piece = left_ref.shape[1] // tiles
        for y in range(peers):
            for tile in range(tiles):
                rows[piece * y : piece * (y + 1), LANES * tile : LANES * (tile + 1)] = left_ref[
                    y, piece * tile : piece * (tile + 1), :
                ]
        high[...], low[...] = split(rows[...])

    out_ref[...] = three_passes((high[...], low[...]), split(basis_ref[0]), ((1,), (0,)))


def forth(left, basis):
    halves, keys, cols = basis.shape
    count = left.shape[0] * left.shape[1] * LANES // keys
    block = cols // 3
    return pl.pallas_call(
        forth_kernel,
        grid=(halves, 3),
        in_specs=[
            pl.BlockSpec(left.shape, lambda i, j: (0, 0, 0)),
            pl.BlockSpec((1, keys, block), lambda i, j: (i, 0, j)),
        ],
        out_specs=pl.BlockSpec((count, block), lambda i, j: (0, 3 * i + j)),
        out_shape=jax.ShapeDtypeStruct((count, halves * cols), jnp.float32),
        scratch_shapes=[
            pltpu.VMEM((count, keys), jnp.float32),
            pltpu.VMEM((count, keys), jnp.bfloat16),
            pltpu.VMEM((count, keys), jnp.bfloat16),
        ],
        compiler_params=pltpu.CompilerParams(vmem_limit_bytes=57 * 2**20),
        cost_estimate=pl.CostEstimate(
            flops=6 * count * keys * halves * cols, bytes_accessed=8_000_000, transcendentals=0
        ),
    )(left, basis)


def back_kernel(column_ref, basis_ref, out_ref, rows, high, low):
    @pl.when(pl.program_id(0) == 0)
    def _():
        high[...], low[...] = split(column_ref[...])

    cols = basis_ref.shape[2]
    contract = ((1,), (1,))
    first, second = (
        three_passes(
            (high[:, cols * i : cols * (i + 1)], low[:, cols * i : cols * (i + 1)]),
            split(basis_ref[i]),
            contract,
        )
        for i in range(2)
    )
    rows[...] = first + second
    peers, piece = out_ref.shape[1], out_ref.shape[2] // 2
    for y in range(peers):
        for part in range(2):
            out_ref[0, y, piece * part : piece * (part + 1), :] = rows[
                piece * y : piece * (y + 1), LANES * part : LANES * (part + 1)
            ]


def rotate_back(column, basis, peers):
    halves, keys, cols = basis.shape
    count = column.shape[0]
    block = keys // 4
    shape = (4, peers, count // peers * (block // LANES), LANES)
    return pl.pallas_call(
        back_kernel,
        grid=(4,),
        in_specs=[
            pl.BlockSpec(column.shape, lambda i: (0, 0)),
            pl.BlockSpec((halves, block, cols), lambda i: (0, i, 0)),
        ],
        out_specs=pl.BlockSpec((1,) + shape[1:], lambda i: (i, 0, 0, 0)),
        out_shape=jax.ShapeDtypeStruct(shape, jnp.float32),
        scratch_shapes=[
            pltpu.VMEM((count, block), jnp.float32),
            pltpu.VMEM(column.shape, jnp.bfloat16),
            pltpu.VMEM(column.shape, jnp.bfloat16),
        ],
        compiler_params=pltpu.CompilerParams(vmem_limit_bytes=57 * 2**20),
        cost_estimate=pl.CostEstimate(
            flops=6 * count * keys * halves * cols, bytes_accessed=8_000_000, transcendentals=0
        ),
    )(column, basis)


def finish_kernel(got_ref, left_ref, master_ref, weight_ref, direction_ref, rows, back, high, low):
    peers, few = got_ref.shape[1], 8
    piece = got_ref.shape[3] // 2
    depth = back.shape[0] // 64

    @pl.when(pl.program_id(0) == 0)
    def _():
        for xh in range(2):
            for ring in range(4):
                for y in range(peers):
                    for part in range(2):
                        rows[piece * y : piece * (y + 1), LANES * part : LANES * (part + 1)] = got_ref[
                            xh, y, ring, piece * part : piece * (part + 1), :
                        ]
                for z in range(depth):
                    at = 64 * z + 16 * ring + few * xh
                    back[at : at + few, :] = rows[few * z : few * (z + 1), :]
        high[...], low[...] = split(back[...])

    step = three_passes(split(left_ref[...]), (high[...], low[...]), ((1,), (0,)))
    master = master_ref[...]
    direction_ref[...] = step
    weight_ref[...] = (master - 0.003 * (step + 0.1 * master)).astype(jnp.bfloat16)


def finish(got, left_basis, master_weight):
    height, keys = master_weight.shape
    window = left_basis.shape[1]
    block = height // 4
    by_rows = pl.BlockSpec((block, keys), lambda i: (i, 0))
    return pl.pallas_call(
        finish_kernel,
        grid=(4,),
        in_specs=[
            pl.BlockSpec(got.shape, lambda i: (0,) * got.ndim),
            pl.BlockSpec((block, window), lambda i: (i, 0)),
            by_rows,
        ],
        out_specs=[by_rows, by_rows],
        out_shape=[
            jax.ShapeDtypeStruct((height, keys), jnp.bfloat16),
            jax.ShapeDtypeStruct((height, keys), jnp.float32),
        ],
        scratch_shapes=[
            pltpu.VMEM((window // 8, keys), jnp.float32),
            pltpu.VMEM((window, keys), jnp.float32),
            pltpu.VMEM((window, keys), jnp.bfloat16),
            pltpu.VMEM((window, keys), jnp.bfloat16),
        ],
        compiler_params=pltpu.CompilerParams(vmem_limit_bytes=24 * 2**20),
        cost_estimate=pl.CostEstimate(
            flops=6 * height * window * keys, bytes_accessed=6_000_000, transcendentals=0
        ),
    )(got, left_basis, master_weight)


def shards(master_weight, gradient, first_moment, second_moment, left_basis, right_basis):
    own, cols = first_moment.shape
    depth = lax.axis_size("z")
    peers = lax.axis_size("y")
    few = own // 2
    keys = gradient.shape[1]
    xh = lax.axis_index("xh")
    correction = 1.0 - 0.95**STEP

    def in_order(mine, other, axis):
        pair = jnp.stack([mine, other], axis=axis)
        return jnp.where(xh == 0, pair, jnp.stack([other, mine], axis=axis))

    def trade(x, axis):
        mine = lax.dynamic_index_in_dim(x, xh, axis, keepdims=False)
        other = lax.dynamic_index_in_dim(x, 1 - xh, axis, keepdims=False)
        return mine, lax.ppermute(other, "xh", [(0, 1), (1, 0)])

    basis = lax.all_gather(right_basis, ("xh", "xl", "core"), axis=0, tiled=True)
    basis = basis.reshape(2, 4 * keys, cols)
    moments = jnp.stack([first_moment, second_moment]).reshape(2, 2, few, cols)
    moments = in_order(*trade(moments, 1), axis=2).reshape(2, few, 2 * cols)

    parts = start(left_basis, gradient, peers)
    parts = exchange(parts.reshape((-1,) + parts.shape[3:]), ("xl", "core", "xh", "y"))
    left_chunk = jnp.sum(parts.reshape(4, 2 * peers, -1, LANES), axis=1).reshape(-1, LANES)
    left_rotated = copies_to(left_chunk, "y")

    summed = forth(left_rotated, basis).reshape(depth, few, 2 * cols)
    rotated = jnp.sum(exchange(summed, "z"), axis=0)

    new_first = 0.95 * moments[0] + 0.05 * rotated
    new_second = 0.95 * moments[1] + 0.05 * rotated * rotated
    normed = new_first / correction / (jnp.sqrt(new_second / correction) + 1e-08)

    column = copies_to(normed, "z").reshape(depth * few, 2 * cols)
    moments = jnp.stack([new_first, new_second]).reshape(2, few, 2, cols)
    moments = in_order(*trade(moments, 2), axis=1).reshape(2, own, cols)

    back_part = rotate_back(column, basis, peers)
    back_part = exchange(back_part.reshape((-1,) + back_part.shape[2:]), ("xl", "core", "y"))
    back_chunk = jnp.sum(back_part.reshape((4, peers) + back_part.shape[1:]), axis=1)
    got = copies_to(back_chunk, COL).reshape((2, peers) + back_chunk.shape)
    new_weight, direction = finish(got, left_basis, master_weight)
    return (new_weight, direction, moments[0], moments[1])


def solution(mesh):
    fine = Mesh(mesh.devices.reshape(12, 2, 2, 2, 8), ROW + COL)
    in_specs = (P(COL, ROW), P(COL, ROW), P(ROW, COL), P(ROW, COL), P(COL, None), P(ROW, COL))
    out_specs = (P(COL, ROW), P(COL, ROW), P(ROW, COL), P(ROW, COL))
    return jax.shard_map(shards, mesh=fine, in_specs=in_specs, out_specs=out_specs, check_vma=False)
```

time: 248 us -> 212 us (0.85)
  the two profiles are of different devices: /device:TPU:4 before, /device:TPU:8 now
where the time goes in v5:
time: 212 us; the launch traced here: 211 us
  blocking collectives  107 us (50%)
  waiting for transfers between devices  41.6 us (20%)
  starting transfers between devices  25 us (12%)
  Pallas kernels  20.2 us (10%)
  between operations  14.2 us (7%)
  local copies, waits for them, and re-layouts  2.82 us (1%)
    all_to_all x4, blocking collectives, exchange(): return lax.all_to_all(x, axes, 0, 0, tiled=True)  107 us
    all_to_all x2, waiting for transfers between devices, exchange(): return lax.all_to_all(x, axes, 0, 0, tiled=True)  31.9 us
    all_to_all x2, starting transfers between devices, exchange(): return lax.all_to_all(x, axes, 0, 0, tiled=True)  15.7 us
    ppermute x2, starting transfers between devices, trade(): return (mine, lax.ppermute(other, 'xh', [(0, 1), (1, 0)]))  9.27 us
    pallas_call x1, Pallas kernels, forth(): pl.pallas_call(forth_kernel, grid=(halves, 3), in_specs=[pl.BlockSpec(lef...  6.53 us
    pallas_call x1, Pallas kernels, rotate_back(): pl.pallas_call(back_kernel, grid=(4,), in_specs=[pl.BlockSpec(column.shap...  6.46 us
    ppermute x2, waiting for transfers between devices, trade(): return (mine, lax.ppermute(other, 'xh', [(0, 1), (1, 0)]))  5.69 us
  transfers between devices with their start and end apart: 5, of which 5 were waited for; matrix products, arithmetic and copies ran while one was open for 0% of the time, Pallas kernels for 2%

profile of v5, /device:TPU:8, one launch (start us, length us, event | category | flops | bytes accessed | tf_op | source)
XLA Modules:
  0.0 210.7 jit_solution(3823617278446789217)
XLA Ops:
  7.2 0.0 all-gather.2.cloned.1.call-start
  7.2 0.7 all-gather.2.cloned.1.call-update
  7.9 4.2 %shard_map.93 = f32[4,2,8,24,128]{4,3,2,1,0:T(8,128)} custom-call(f32[768,768]{1,0:T(8,128)} %left_ref.3, bf16[768,256]{1,0:T(8,128)(2,1)} %gradient_ref.1), custom_call_target="tpu_custom_call" | custom-call | flops 603979776 | bytes 4000000 | tf_op jit(solution)/shard_map/pallas_call | solution.py:76
  12.1 36.7 %all_to_all.30 = f32[64,24,128]{2,1,0:T(8,128)S(1)} all-to-all(f32[64,24,128]{2,1,0:T(8,128)} %bitcast.35), channel_id=1, replica_groups=mesh['z'=12,'xl'=2,'core'=2,'xh'=2,'y'=8] {'xl','core','xh','y'}, dimensions={0} | all-to-all | bytes 1572864 | tf_op jit(solution)/shard_map/all_to_all | solution.py:15
  48.9 18.1 %all_to_all.31.left_ref = f32[8,96,128]{2,1,0:T(8,128)} all-to-all(f32[8,96,128]{2,1,0:T(8,128)S(1)} %broadcast_in_dim.9), channel_id=1, replica_groups=mesh['z'=12,'xl'=2,'core'=2,'xh'=2,'y'=8] {'y'}, dimensions={0} | all-to-all | bytes 786432 | tf_op jit(solution)/shard_map/all_to_all | solution.py:15
  67.0 3.3 %all-gather.2.cloned.1.call-done = f32[2048,768]{1,0:T(8,128)} async-done(((f32[256,768]{1,0:T(8,128)}), f32[2048,768]{1,0:T(8,128)}) %all-gather.2.cloned.1.call-update) | async-done | bytes 6291472 | tf_op jit(solution)/shard_map/all_gather | solution.py:260
  70.3 6.5 %shard_map.94 = f32[96,1536]{1,0:T(8,128)} custom-call(f32[8,96,128]{2,1,0:T(8,128)} %all_to_all.31.left_ref, f32[2,1024,768]{2,1,0:T(8,128)} %bitcast.33), custom_call_target="tpu_custom_call" | custom-call | flops 905969664 | bytes 8000000 | tf_op jit(solution)/shard_map/pallas_call | solution.py:115
  76.8 10.7 %all-to-all-start.2 = ((f32[12,8,1536]{2,1,0:T(8,128)}), f32[12,8,1536]{2,1,0:T(8,128)S(1)}, u32[]{:S(2)}, u32[]{:S(2)}) async-start(f32[12,8,1536]{2,1,0:T(8,128)} %bitcast.36), calls=%async_computation.2 | async-start | bytes 1179648 | tf_op jit(solution)/shard_map/all_to_all | solution.py:15
  87.6 4.4 %collective-permute-start = (f32[2,8,768]{2,1,0:T(8,128)S(1)}, f32[2,8,768]{2,1,0:T(8,128)S(1)}, u32[]{:S(2)}, u32[]{:S(2)}) collective-permute-start(f32[2,8,768]{2,1,0:T(8,128)S(1)} %get-tuple-element.17), channel_id=1, source_target_pairs={{0,8},{8,0},{1,9},{9,1},{2,10},{10,2},{3,11},{11,3},{4,12},{12,4},... | collective-permute-start | bytes 147464 | tf_op jit(solution)/shard_map/ppermute | solution.py:258
  92.0 3.1 %collective-permute-done = f32[2,8,768]{2,1,0:T(8,128)S(1)} collective-permute-done((f32[2,8,768]{2,1,0:T(8,128)S(1)}, f32[2,8,768]{2,1,0:T(8,128)S(1)}, u32[]{:S(2)}, u32[]{:S(2)}) %collective-permute-start) | collective-permute-done | bytes 49184 | tf_op jit(solution)/shard_map/ppermute | solution.py:258
  95.1 18.0 %all-to-all-done.2 = f32[12,8,1536]{2,1,0:T(8,128)S(1)} async-done(((f32[12,8,1536]{2,1,0:T(8,128)}), f32[12,8,1536]{2,1,0:T(8,128)S(1)}, u32[]{:S(2)}, u32[]{:S(2)}) %all-to-all-start.2) | async-done | bytes 589856 | tf_op jit(solution)/shard_map/all_to_all | solution.py:15
  113.2 0.0 copy-start
  113.2 31.2 %all_to_all.32 = f32[12,8,1536]{2,1,0:T(8,128)} all-to-all(f32[12,8,1536]{2,1,0:T(8,128)S(1)} %broadcast_in_dim.10), channel_id=1, replica_groups=mesh['z'=12,'xl'=2,'core'=2,'xh'=2,'y'=8] {'z'}, dimensions={0} | all-to-all | bytes 1179648 | tf_op jit(solution)/shard_map/all_to_all | solution.py:15
  144.4 6.5 %shard_map.95 = f32[4,8,24,128]{3,2,1,0:T(8,128)} custom-call(f32[96,1536]{1,0:T(8,128)} %bitcast.37, f32[2,1024,768]{2,1,0:T(8,128)} %bitcast.34), custom_call_target="tpu_custom_call" | custom-call | flops 905969664 | bytes 8000000 | tf_op jit(solution)/shard_map/pallas_call | solution.py:165
  150.8 20.9 %all_to_all.33 = f32[32,24,128]{2,1,0:T(8,128)S(1)} all-to-all(f32[32,24,128]{2,1,0:T(8,128)} %bitcast.38), channel_id=1, replica_groups=mesh['z'=12,'xl'=2,'core'=2,'xh'=2,'y'=8] {'xl','core','y'}, dimensions={0} | all-to-all | bytes 786432 | tf_op jit(solution)/shard_map/all_to_all | solution.py:15
  171.7 1.0 broadcast_in_dim.22
  172.7 5.0 %all-to-all-start.5 = ((f32[16,4,24,128]{3,2,1,0:T(8,128)}), f32[16,4,24,128]{3,2,1,0:T(8,128)S(1)}, u32[]{:S(2)}, u32[]{:S(2)}) async-start(f32[16,4,24,128]{3,2,1,0:T(8,128)} %broadcast_in_dim.22), calls=%async_computation.5 | async-start | bytes 1572864 | tf_op jit(solution)/shard_map/all_to_all | solution.py:15
  177.7 4.9 %collective-permute-start.1 = (f32[2,8,768]{2,1,0:T(8,128)S(1)}, f32[2,8,768]{2,1,0:T(8,128)S(1)}, u32[]{:S(2)}, u32[]{:S(2)}) collective-permute-start(f32[2,8,768]{2,1,0:T(8,128)S(1)} %get-tuple-element.13), channel_id=1, source_target_pairs={{0,8},{8,0},{1,9},{9,1},{2,10},{10,2},{3,11},{11,3},{4,12},{12,4},... | collective-permute-start | bytes 147464 | tf_op jit(solution)/shard_map/ppermute | solution.py:258
  182.6 2.6 %collective-permute-done.1 = f32[2,8,768]{2,1,0:T(8,128)S(1)} collective-permute-done((f32[2,8,768]{2,1,0:T(8,128)S(1)}, f32[2,8,768]{2,1,0:T(8,128)S(1)}, u32[]{:S(2)}, u32[]{:S(2)}) %collective-permute-start.1) | collective-permute-done | bytes 49184 | tf_op jit(solution)/shard_map/ppermute | solution.py:258
  185.2 0.6 slice_bitcast_fusion
  185.9 13.9 %all-to-all-done.5 = f32[16,4,24,128]{3,2,1,0:T(8,128)S(1)} async-done(((f32[16,4,24,128]{3,2,1,0:T(8,128)}), f32[16,4,24,128]{3,2,1,0:T(8,128)S(1)}, u32[]{:S(2)}, u32[]{:S(2)}) %all-to-all-start.5) | async-done | bytes 786464 | tf_op jit(solution)/shard_map/all_to_all | solution.py:15
  199.8 0.0 copy-done
  199.8 1.1 copy-done.1
  200.9 2.9 %shard_map.96 = (bf16[768,256]{1,0:T(8,128)(2,1)}, f32[768,256]{1,0:T(8,128)}) custom-call(f32[2,8,4,24,128]{4,3,2,1,0:T(8,128)S(1)} %bitcast.32, f32[768,768]{1,0:T(8,128)S(1)} %copy-done, f32[768,256]{1,0:T(8,128)S(1)} %copy-done.1), custom_call_target="tpu_custom_call" | custom-call | flops 905969664 | bytes 6000000 | tf_op jit(solution)/shard_map/pallas_call | solution.py:216
  (16 shorter events, 0.3 us)
Async XLA Ops:
  7.2 63.1 %all-gather.2.cloned.1.call-start = ((), (), s32[]{:S(2)}) async-start(), calls=%async_computation.6 | async-start | bytes 7077888 | tf_op jit(solution)/shard_map/all_gather | solution.py:260
  12.1 75.4 %copy-start.2 = (f32[16,768]{1,0:T(8,128)S(1)}, f32[16,768]{1,0:T(8,128)}, u32[]{:S(2)}) copy-start(f32[16,768]{1,0:T(8,128)} %param.8) | copy-start | bytes 147460
  12.1 75.4 %copy-start.3 = (f32[16,768]{1,0:T(8,128)S(1)}, f32[16,768]{1,0:T(8,128)}, u32[]{:S(2)}) copy-start(f32[16,768]{1,0:T(8,128)} %param.9) | copy-start | bytes 147460
  76.8 36.2 %all-to-all-start.2 = ((f32[12,8,1536]{2,1,0:T(8,128)}), f32[12,8,1536]{2,1,0:T(8,128)S(1)}, u32[]{:S(2)}, u32[]{:S(2)}) async-start(f32[12,8,1536]{2,1,0:T(8,128)} %bitcast.36), calls=%async_computation.2 | async-start | bytes 1179648 | tf_op jit(solution)/shard_map/all_to_all | solution.py:15
  87.6 7.5 %collective-permute-start = (f32[2,8,768]{2,1,0:T(8,128)S(1)}, f32[2,8,768]{2,1,0:T(8,128)S(1)}, u32[]{:S(2)}, u32[]{:S(2)}) collective-permute-start(f32[2,8,768]{2,1,0:T(8,128)S(1)} %get-tuple-element.17), channel_id=1, source_target_pairs={{0,8},{8,0},{1,9},{9,1},{2,10},{10,2},{3,11},{11,3},{4,12},{12,4},... | collective-permute-start | bytes 147464 | tf_op jit(solution)/shard_map/ppermute | solution.py:258
  113.2 86.6 %copy-start = (f32[768,768]{1,0:T(8,128)S(1)}, f32[768,768]{1,0:T(8,128)}, u32[]{:S(2)}) copy-start(f32[768,768]{1,0:T(8,128)} %left_ref.3) | copy-start | bytes 7077892
  172.7 27.1 %all-to-all-start.5 = ((f32[16,4,24,128]{3,2,1,0:T(8,128)}), f32[16,4,24,128]{3,2,1,0:T(8,128)S(1)}, u32[]{:S(2)}, u32[]{:S(2)}) async-start(f32[16,4,24,128]{3,2,1,0:T(8,128)} %broadcast_in_dim.22), calls=%async_computation.5 | async-start | bytes 1572864 | tf_op jit(solution)/shard_map/all_to_all | solution.py:15
  177.7 7.5 %collective-permute-start.1 = (f32[2,8,768]{2,1,0:T(8,128)S(1)}, f32[2,8,768]{2,1,0:T(8,128)S(1)}, u32[]{:S(2)}, u32[]{:S(2)}) collective-permute-start(f32[2,8,768]{2,1,0:T(8,128)S(1)} %get-tuple-element.13), channel_id=1, source_target_pairs={{0,8},{8,0},{1,9},{9,1},{2,10},{10,2},{3,11},{11,3},{4,12},{12,4},... | collective-permute-start | bytes 147464 | tf_op jit(solution)/shard_map/ppermute | solution.py:258
  199.8 1.1 copy-start.1
Sparse Core Ops, SparseCore 0:
  10.4 59.8 all-gather.1

commit v6 on v5

v6 whole, which is shorter than its diff:
```python
import jax
import jax.numpy as jnp
from jax import lax
from jax.experimental import pallas as pl
from jax.experimental.pallas import tpu as pltpu
from jax.sharding import Mesh, PartitionSpec as P

STEP = 10
LANES = 128
ROW = ("z", "xl", "core")
COL = ("xh", "y")


def swap(x, axis):
    return lax.ppermute(x, axis, [(0, 1), (1, 0)])


def cross(x):
    return lax.ppermute(x, ("xl", "xh"), [(0, 3), (3, 0), (1, 2), (2, 1)])


def relay(x):
    flip = (4, 7)
    pairs = [(i, i ^ flip[(i >> 1) & 1] ^ (2 * ((i >> 1) & 1))) for i in range(8)]
    return lax.ppermute(x, ("xl", "core", "xh"), pairs)


def exchange(x, axes):
    return lax.all_to_all(x, axes, 0, 0, tiled=True)


def copies_to(x, axes):
    return exchange(jnp.broadcast_to(x[None], (lax.axis_size(axes),) + x.shape), axes)


def split(x):
    high = x.astype(jnp.bfloat16)
    return high, (x - high.astype(jnp.float32)).astype(jnp.bfloat16)


def three_passes(a, b, contract):
    a_high, a_low = a
    b_high, b_low = b

    def one(x, y):
        return lax.dot_general(x, y, (contract, ((), ())), preferred_element_type=jnp.float32)

    return one(a_high, b_high) + (one(a_high, b_low) + one(a_low, b_high))


def start_kernel(left_ref, gradient_ref, out_ref, total, rows):
    step = pl.program_id(0)
    high, low = split(left_ref[...])
    turned = gradient_ref[...].astype(jnp.float32).T.astype(jnp.bfloat16)

    def one(x):
        return jnp.dot(turned, x, preferred_element_type=jnp.float32)

    part = one(high) + one(low)

    @pl.when(step == 0)
    def _():
        total[...] = part

    @pl.when(step > 0)
    def _():
        total[...] += part

    @pl.when(step == pl.num_programs(0) - 1)
    def _():
        whole = total[...].T
        peers, piece, few = out_ref.shape[2], out_ref.shape[3] // 2, 8
        for ring in range(4):
            for xh in range(2):
                for z in range(total.shape[1] // 64):
                    at = 64 * z + 16 * ring + few * xh
                    rows[few * z : few * (z + 1), :] = whole[at : at + few, :]
                for y in range(peers):
                    for part_of in range(2):
                        out_ref[ring, xh, y, piece * part_of : piece * (part_of + 1), :] = rows[
                            piece * y : piece * (y + 1), LANES * part_of : LANES * (part_of + 1)
                        ]


def start(left_basis, gradient, peers):
    height, window = left_basis.shape
    keys = gradient.shape[1]
    block = height // 3
    shape = (4, 2, peers, window // 8 // peers * (keys // LANES), LANES)
    return pl.pallas_call(
        start_kernel,
        grid=(3,),
        in_specs=[
            pl.BlockSpec((block, window), lambda i: (i, 0)),
            pl.BlockSpec((block, keys), lambda i: (i, 0)),
        ],
        out_specs=pl.BlockSpec(shape, lambda i: (0,) * 5),
        out_shape=jax.ShapeDtypeStruct(shape, jnp.float32),
        scratch_shapes=[
            pltpu.VMEM((keys, window), jnp.float32),
            pltpu.VMEM((window // 8, keys), jnp.float32),
        ],
        compiler_params=pltpu.CompilerParams(vmem_limit_bytes=24 * 2**20),
        cost_estimate=pl.CostEstimate(
            flops=4 * height * window * keys, bytes_accessed=4_000_000, transcendentals=0
        ),
    )(left_basis, gradient)


def forth_kernel(left_ref, *refs):
    basis, (out_ref, rows, high, low) = refs[:8], refs[8:]
    keys = basis[0].shape[0]

    @pl.when(pl.program_id(0) == 0)
    def _():
        peers, tiles = left_ref.shape[0], rows.shape[1] // LANES
        piece = left_ref.shape[1] // tiles
        for y in range(peers):
            for tile in range(tiles):
                rows[piece * y : piece * (y + 1), LANES * tile : LANES * (tile + 1)] = left_ref[
                    y, piece * tile : piece * (tile + 1), :
                ]
        high[...], low[...] = split(rows[...])

    few = out_ref.shape[1] // 2
    for half in range(2):
        total = None
        for i in range(4):
            at = slice(keys * i, keys * (i + 1))
            term = three_passes(
                (high[:, at], low[:, at]), split(basis[4 * half + i][...]), ((1,), (0,))
            )
            total = term if total is None else total + term
        out_ref[:, few * half : few * (half + 1), :] = total.reshape(-1, few, total.shape[1])


def forth(left, basis, few):
    keys, cols = basis[0].shape
    count = left.shape[0] * left.shape[1] * LANES // (4 * keys)
    block = cols // 3
    depth = count // few
    return pl.pallas_call(
        forth_kernel,
        grid=(3,),
        in_specs=[pl.BlockSpec(left.shape, lambda j: (0, 0, 0))]
        + [pl.BlockSpec((keys, block), lambda j: (0, j))] * 8,
        out_specs=pl.BlockSpec((depth, 2 * few, block), lambda j: (0, 0, j)),
        out_shape=jax.ShapeDtypeStruct((depth, 2 * few, cols), jnp.float32),
        scratch_shapes=[
            pltpu.VMEM((count, 4 * keys), jnp.float32),
            pltpu.VMEM((count, 4 * keys), jnp.bfloat16),
            pltpu.VMEM((count, 4 * keys), jnp.bfloat16),
        ],
        compiler_params=pltpu.CompilerParams(vmem_limit_bytes=24 * 2**20),
        cost_estimate=pl.CostEstimate(
            flops=48 * count * keys * cols, bytes_accessed=8_000_000, transcendentals=0
        ),
    )(left, *basis)


def back_kernel(me_ref, column_ref, *refs):
    basis, (out_ref, rows, whole, high, low) = refs[:8], refs[8:]
    few = column_ref.shape[1] // 2
    step = pl.program_id(0)

    @pl.when(step == 0)
    def _():
        for half in range(2):
            for z in range(column_ref.shape[0]):
                whole[half, few * z : few * (z + 1), :] = column_ref[
                    z, few * half : few * (half + 1), :
                ]
        high[...], low[...] = split(whole[...])

    peers, piece = out_ref.shape[1], out_ref.shape[2] // 2
    for i in range(4):
        first, second = (
            three_passes((high[half], low[half]), split(basis[4 * half + i][...]), ((1,), (1,)))
            for half in range(2)
        )
        rows[i] = first + second
    for part in range(2):

        @pl.when(step == part)
        def _():
            for i in range(4):
                ring = jnp.bitwise_xor(me_ref[0], i)
                for y in range(peers):
                    out_ref[ring, y, piece * part : piece * (part + 1), :] = rows[
                        i, piece * y : piece * (y + 1), :
                    ]


def rotate_back(me, column, basis, peers):
    keys, cols = basis[0].shape
    depth, both, _ = column.shape
    count = depth * both // 2
    shape = (4, peers, 2 * count // peers, LANES)
    return pl.pallas_call(
        back_kernel,
        grid=(2,),
        in_specs=[
            pl.BlockSpec(memory_space=pltpu.SMEM),
            pl.BlockSpec(column.shape, lambda i: (0, 0, 0)),
        ]
        + [pl.BlockSpec((LANES, cols), lambda i: (i, 0))] * 8,
        out_specs=pl.BlockSpec(shape, lambda i: (0, 0, 0, 0)),
        out_shape=jax.ShapeDtypeStruct(shape, jnp.float32),
        scratch_shapes=[
            pltpu.VMEM((4, count, LANES), jnp.float32),
            pltpu.VMEM((2, count, cols), jnp.float32),
            pltpu.VMEM((2, count, cols), jnp.bfloat16),
            pltpu.VMEM((2, count, cols), jnp.bfloat16),
        ],
        compiler_params=pltpu.CompilerParams(vmem_limit_bytes=24 * 2**20),
        cost_estimate=pl.CostEstimate(
            flops=48 * count * keys * cols, bytes_accessed=8_000_000, transcendentals=0
        ),
    )(me, column, *basis)


def finish_kernel(got_ref, left_ref, master_ref, weight_ref, direction_ref, rows, back, high, low):
    peers, few = got_ref.shape[1], 8
    piece = got_ref.shape[3] // 2
    depth = back.shape[0] // 64

    @pl.when(pl.program_id(0) == 0)
    def _():
        for xh in range(2):
            for ring in range(4):
                for y in range(peers):
                    for part in range(2):
                        rows[piece * y : piece * (y + 1), LANES * part : LANES * (part + 1)] = got_ref[
                            xh, y, ring, piece * part : piece * (part + 1), :
                        ]
                for z in range(depth):
                    at = 64 * z + 16 * ring + few * xh
                    back[at : at + few, :] = rows[few * z : few * (z + 1), :]
        high[...], low[...] = split(back[...])

    step = three_passes(split(left_ref[...]), (high[...], low[...]), ((1,), (0,)))
    master = master_ref[...]
    direction_ref[...] = step
    weight_ref[...] = (master - 0.003 * (step + 0.1 * master)).astype(jnp.bfloat16)


def finish(got, left_basis, master_weight):
    height, keys = master_weight.shape
    window = left_basis.shape[1]
    block = height // 4
    by_rows = pl.BlockSpec((block, keys), lambda i: (i, 0))
    return pl.pallas_call(
        finish_kernel,
        grid=(4,),
        in_specs=[
            pl.BlockSpec(got.shape, lambda i: (0,) * got.ndim),
            pl.BlockSpec((block, window), lambda i: (i, 0)),
            by_rows,
        ],
        out_specs=[by_rows, by_rows],
        out_shape=[
            jax.ShapeDtypeStruct((height, keys), jnp.bfloat16),
            jax.ShapeDtypeStruct((height, keys), jnp.float32),
        ],
        scratch_shapes=[
            pltpu.VMEM((window // 8, keys), jnp.float32),
            pltpu.VMEM((window, keys), jnp.float32),
            pltpu.VMEM((window, keys), jnp.bfloat16),
            pltpu.VMEM((window, keys), jnp.bfloat16),
        ],
        compiler_params=pltpu.CompilerParams(vmem_limit_bytes=24 * 2**20),
        cost_estimate=pl.CostEstimate(
            flops=6 * height * window * keys, bytes_accessed=6_000_000, transcendentals=0
        ),
    )(got, left_basis, master_weight)


def shards(master_weight, gradient, first_moment, second_moment, left_basis, right_basis):
    own, cols = first_moment.shape
    depth = lax.axis_size("z")
    peers = lax.axis_size("y")
    few = own // 2
    keys = gradient.shape[1]
    xl, core, xh = lax.axis_index("xl"), lax.axis_index("core"), lax.axis_index("xh")
    correction = 1.0 - 0.95**STEP

    def trade(x, axis):
        mine = lax.dynamic_index_in_dim(x, xh, axis, keepdims=False)
        other = lax.dynamic_index_in_dim(x, 1 - xh, axis, keepdims=False)
        return mine, swap(other, "xh")

    by_xl = swap(right_basis, "xl")
    by_both = cross(right_basis)
    by_xh = relay(jnp.where(core == 0, by_both, by_xl))
    early = [x for ring in (right_basis, by_xl, by_both) for x in (ring, swap(ring, "core"))]

    parts = start(left_basis, gradient, peers)
    parts = exchange(parts.reshape((-1,) + parts.shape[3:]), ("xl", "core", "xh", "y"))
    parts, by_xh, early = lax.optimization_barrier((parts, by_xh, early))
    left_chunk = jnp.sum(parts.reshape(2, 2, 2 * peers, -1, LANES), axis=2)
    left_chunk = jnp.where(xl == 0, left_chunk, left_chunk[::-1])
    left_chunk = jnp.where(core == 0, left_chunk, left_chunk[:, ::-1])
    left_rotated = copies_to(left_chunk.reshape(-1, LANES), "y")
    basis = early[:4] + [by_xh, swap(by_xh, "core")] + early[4:]

    rotated = jnp.sum(exchange(forth(left_rotated, basis, few), "z"), axis=0)

    moments = jnp.stack([first_moment, second_moment]).reshape(2, 2, few, cols)
    moments = jnp.concatenate(trade(moments, 1), axis=1)
    new_first = 0.95 * moments[0] + 0.05 * rotated
    new_second = 0.95 * moments[1] + 0.05 * rotated * rotated
    normed = new_first / correction / (jnp.sqrt(new_second / correction) + 1e-08)

    column = lax.all_gather(normed, "z", axis=0, tiled=False)
    moments = jnp.stack([new_first, new_second]).reshape(2, 2, few, cols)
    mine, other = moments[:, 0], swap(moments[:, 1], "xh")
    moments = jnp.where(
        xh == 0, jnp.concatenate([mine, other], axis=1), jnp.concatenate([other, mine], axis=1)
    )

    me = (2 * xl + core).astype(jnp.int32).reshape(1)
    back_part = rotate_back(me, column, basis, peers)
    back_part = exchange(back_part.reshape((-1,) + back_part.shape[2:]), ("xl", "core", "y"))
    back_chunk = jnp.sum(back_part.reshape((4, peers) + back_part.shape[1:]), axis=1)
    got = copies_to(back_chunk, COL).reshape((2, peers) + back_chunk.shape)
    new_weight, direction = finish(got, left_basis, master_weight)
    return (new_weight, direction, moments[0], moments[1])


def solution(mesh):
    fine = Mesh(mesh.devices.reshape(12, 2, 2, 2, 8), ROW + COL)
    in_specs = (P(COL, ROW), P(COL, ROW), P(ROW, COL), P(ROW, COL), P(COL, None), P(ROW, COL))
    out_specs = (P(COL, ROW), P(COL, ROW), P(ROW, COL), P(ROW, COL))
    return jax.shard_map(shards, mesh=fine, in_specs=in_specs, out_specs=out_specs, check_vma=False)
```

time: 212 us -> 202 us (0.953)
  blocking collectives: 107 us -> 64.9 us
  starting transfers between devices: 25 us -> 59 us
  between operations: 14.2 us -> 0.92 us
  waiting for transfers between devices: 41.6 us -> 50.4 us
  Pallas kernels: 20.2 us -> 14.1 us
  local copies, waits for them, and re-layouts: 2.82 us -> 8.27 us
  other arithmetic: 0.2 us -> 3.37 us
    all_to_all x4 -> x2, blocking collectives: 107 us -> 39.2 us  [exchange(): return lax.all_to_all(x, axes, 0, 0, tiled=True)]
    all_gather x0 -> x1, blocking collectives: none -> 25.7 us  [shards(): column = lax.all_gather(normed, 'z', axis=0, tiled=False)]
    ppermute x2 -> x9, starting transfers between devices: 9.27 us -> 26.7 us  [the longest x7 18.5 us: swap(): return lax.ppermute(x, axis, [(0, 1), (1, 0)])]
    all_to_all x2 -> x3, starting transfers between devices: 15.7 us -> 32.3 us  [exchange(): return lax.all_to_all(x, axes, 0, 0, tiled=True)]
    all_to_all x2 -> x3, waiting for transfers between devices: 31.9 us -> 47.8 us  [exchange(): return lax.all_to_all(x, axes, 0, 0, tiled=True)]
    unnamed x8 -> x20, local copies, waits for them, and re-layouts: 1.15 us -> 6.64 us
    pallas_call x2, Pallas kernels: 13 us -> 8.54 us  [the longest x1 4.66 us: rotate_back(): pl.pallas_call(back_kernel, grid=(2,), in_specs=[pl.BlockSpec(memory_spac...]
    all_gather x1 -> x0, waiting for transfers between devices: 3.3 us -> none  [shards(): lax.all_gather(right_basis, ('xh', 'xl', 'core'), axis=0, tiled=True)]
  transfers between devices with their start and end apart: 5 -> 12, of which waited for: 5 -> 4; matrix products, arithmetic and copies ran while one was open for 0% -> 1% of each run, Pallas kernels for 2% -> 1%
where the time goes in v6:
time: 202 us; the launch traced here: 201 us
  blocking collectives  64.9 us (32%)
  starting transfers between devices  59 us (29%)
  waiting for transfers between devices  50.4 us (25%)
  Pallas kernels  14.1 us (7%)
  local copies, waits for them, and re-layouts  8.27 us (4%)
  other arithmetic  3.37 us (2%)
    all_to_all x3, waiting for transfers between devices, exchange(): return lax.all_to_all(x, axes, 0, 0, tiled=True)  47.8 us
    all_to_all x2, blocking collectives, exchange(): return lax.all_to_all(x, axes, 0, 0, tiled=True)  39.2 us
    all_to_all x3, starting transfers between devices, exchange(): return lax.all_to_all(x, axes, 0, 0, tiled=True)  32.3 us
    all_gather x1, blocking collectives, shards(): column = lax.all_gather(normed, 'z', axis=0, tiled=False)  25.7 us
    ppermute x7, starting transfers between devices, swap(): return lax.ppermute(x, axis, [(0, 1), (1, 0)])  18.5 us
    unnamed x20, local copies, waits for them, and re-layouts  6.64 us
    ppermute x1, starting transfers between devices, cross(): return lax.ppermute(x, ('xl', 'xh'), [(0, 3), (3, 0), (1, 2), (2, 1)])  4.67 us
    pallas_call x1, Pallas kernels, rotate_back(): pl.pallas_call(back_kernel, grid=(2,), in_specs=[pl.BlockSpec(memory_spac...  4.66 us
  transfers between devices with their start and end apart: 12, of which 4 were waited for; matrix products, arithmetic and copies ran while one was open for 1% of the time, Pallas kernels for 1%

profile of v6, /device:TPU:8, one launch (start us, length us, event | category | flops | bytes accessed | tf_op | source)
XLA Modules:
  0.0 201.0 jit_solution(17666909207379097944)
XLA Ops:
  0.6 4.7 %collective-permute-start.1 = (f32[256,768]{1,0:T(8,128)}, f32[256,768]{1,0:T(8,128)S(1)}, u32[]{:S(2)}, u32[]{:S(2)}) collective-permute-start(f32[256,768]{1,0:T(8,128)} %refs_0_.1), channel_id=1, source_target_pairs={{0,40},{40,0},{8,32},{32,8},{1,41},{41,1},{9,33},{33,9},{2,42},{42... | collective-permute-start | bytes 2359304 | tf_op jit(solution)/shard_map/ppermute | solution.py:19
  5.3 2.1 %collective-permute-start.2 = (f32[256,768]{1,0:T(8,128)}, f32[256,768]{1,0:T(8,128)S(1)}, u32[]{:S(2)}, u32[]{:S(2)}) collective-permute-start(f32[256,768]{1,0:T(8,128)} %refs_0_.1), channel_id=1, source_target_pairs={{0,32},{32,0},{1,33},{33,1},{2,34},{34,2},{3,35},{35,3},{4,36},{36... | collective-permute-start | bytes 2359304 | tf_op jit(solution)/shard_map/ppermute | solution.py:15
  7.5 1.7 copy-done
  10.1 2.6 %shard_map.93 = f32[4,2,8,24,128]{4,3,2,1,0:T(8,128)} custom-call(f32[768,768]{1,0:T(8,128)S(1)} %copy-done, bf16[768,256]{1,0:T(8,128)(2,1)S(1)} %copy-done.7), custom_call_target="tpu_custom_call" | custom-call | flops 603979776 | bytes 4000000 | tf_op jit(solution)/shard_map/pallas_call | solution.py:90
  12.8 13.2 %all-to-all-start = ((f32[64,24,128]{2,1,0:T(8,128)}), f32[64,24,128]{2,1,0:T(8,128)}, u32[]{:S(2)}, u32[]{:S(2)}) async-start(f32[64,24,128]{2,1,0:T(8,128)} %bitcast.7), calls=%async_computation | async-start | bytes 1572864 | tf_op jit(solution)/shard_map/all_to_all | solution.py:29
  26.0 2.1 %collective-permute-start.4 = (f32[256,768]{1,0:T(8,128)S(1)}, f32[256,768]{1,0:T(8,128)S(1)}, u32[]{:S(2)}, u32[]{:S(2)}) collective-permute-start(f32[256,768]{1,0:T(8,128)S(1)} %copy-done.2), channel_id=1, source_target_pairs={{0,16},{16,0},{1,17},{17,1},{2,18},{18,2},{3,19},{19,3},{4,20},{20... | collective-permute-start | bytes 2359304 | tf_op jit(solution)/shard_map/ppermute | solution.py:15
  29.0 3.5 %collective-permute-start.3 = (f32[256,768]{1,0:T(8,128)}, f32[256,768]{1,0:T(8,128)}, u32[]{:S(2)}, u32[]{:S(2)}) collective-permute-start(f32[256,768]{1,0:T(8,128)} %broadcast_select_fusion), channel_id=1, source_target_pairs={{0,32},{8,40},{16,56},{24,48},{32,0},{40,8},{48,24},{56,16},{1,33}... | collective-permute-start | bytes 2359304 | tf_op jit(solution)/shard_map/ppermute | solution.py:25
  32.6 3.2 %collective-permute-start.5 = (f32[256,768]{1,0:T(8,128)S(1)}, f32[256,768]{1,0:T(8,128)}, u32[]{:S(2)}, u32[]{:S(2)}) collective-permute-start(f32[256,768]{1,0:T(8,128)S(1)} %collective-permute-done.2.refs_2_), channel_id=1, source_target_pairs={{0,16},{16,0},{1,17},{17,1},{2,18},{18,2},{3,19},{19,3},{4,20},{20... | collective-permute-start | bytes 2359304 | tf_op jit(solution)/shard_map/ppermute | solution.py:15
  35.8 1.9 collective-permute-start.6
  37.7 11.0 %all-to-all-done = f32[64,24,128]{2,1,0:T(8,128)} async-done(((f32[64,24,128]{2,1,0:T(8,128)}), f32[64,24,128]{2,1,0:T(8,128)}, u32[]{:S(2)}, u32[]{:S(2)}) %all-to-all-start) | async-done | bytes 786464 | tf_op jit(solution)/shard_map/all_to_all | solution.py:29
  49.9 2.4 %collective-permute-start.7 = (f32[256,768]{1,0:T(8,128)}, f32[256,768]{1,0:T(8,128)S(1)}, u32[]{:S(2)}, u32[]{:S(2)}) collective-permute-start(f32[256,768]{1,0:T(8,128)} %collective-permute-done.3.refs_4_), channel_id=1, source_target_pairs={{0,16},{16,0},{1,17},{17,1},{2,18},{18,2},{3,19},{19,3},{4,20},{20... | collective-permute-start | bytes 2359304 | tf_op jit(solution)/shard_map/ppermute | solution.py:15
  52.4 19.5 %all_to_all.25.left_ref = f32[8,96,128]{2,1,0:T(8,128)S(1)} all-to-all(f32[8,96,128]{2,1,0:T(8,128)S(1)} %broadcast_in_dim.14), channel_id=1, replica_groups=mesh['z'=12,'xl'=2,'core'=2,'xh'=2,'y'=8] {'y'}, dimensions={0} | all-to-all | bytes 786432 | tf_op jit(solution)/shard_map/all_to_all | solution.py:29
  72.0 3.9 %shard_map.94 = f32[12,16,768]{2,1,0:T(8,128)S(1)} custom-call(f32[8,96,128]{2,1,0:T(8,128)S(1)} %all_to_all.25.left_ref, f32[256,768]{1,0:T(8,128)S(1)} %copy-done.2, f32[256,768]{1,0:T(8,128)S(1)} %collective-permute-done.4.refs_1_, f32[256,768]{1,0:T(8,128)S(1)} %collective-permute-done.2.refs_2_, f32[256,768]{1,0:T(8,128)} %collective-permute-done.5.refs_3_, ...), custom_call_target="tpu_custom_call" | custom-call | flops 905969664 | bytes 8000000 | tf_op jit(solution)/shard_map/pallas_call | solution.py:142
  77.6 15.2 %all-to-all-start.2 = ((f32[12,16,768]{2,1,0:T(8,128)}), f32[12,16,768]{2,1,0:T(8,128)}, u32[]{:S(2)}, u32[]{:S(2)}) async-start(f32[12,16,768]{2,1,0:T(8,128)} %copy-done.5), calls=%async_computation.2 | async-start | bytes 1179648 | tf_op jit(solution)/shard_map/all_to_all | solution.py:29
  92.9 1.9 collective-permute-start
  94.8 22.8 %all-to-all-done.2 = f32[12,16,768]{2,1,0:T(8,128)} async-done(((f32[12,16,768]{2,1,0:T(8,128)}), f32[12,16,768]{2,1,0:T(8,128)}, u32[]{:S(2)}, u32[]{:S(2)}) %all-to-all-start.2) | async-done | bytes 589856 | tf_op jit(solution)/shard_map/all_to_all | solution.py:29
  118.8 25.7 %all_gather.4.column_ref = f32[12,16,768]{2,1,0:T(8,128)S(1)} all-gather(f32[1,16,768]{2,1,0:T(8,128)S(1)} %get-tuple-element.26), channel_id=1, replica_groups=mesh['z'=12,'xl'=2,'core'=2,'xh'=2,'y'=8] {'z'}, dimensions={0}, use_global_device_ids=true | all-gather | bytes 638976 | tf_op jit(solution)/shard_map/all_gather | solution.py:314
  145.6 4.7 %shard_map.95 = f32[4,8,24,128]{3,2,1,0:T(8,128)S(1)} custom-call(s32[1]{0:T(128)} %bitcast.me_ref, f32[12,16,768]{2,1,0:T(8,128)S(1)} %all_gather.4.column_ref, f32[256,768]{1,0:T(8,128)S(1)} %copy-done.2, f32[256,768]{1,0:T(8,128)S(1)} %collective-permute-done.4.refs_1_, f32[256,768]{1,0:T(8,128)S(1)} %collective-permute-done.2.refs_2_, ...), custom_call_target="tpu_custom_call" | custom-call | flops 905969664 | bytes 8000000 | tf_op jit(solution)/shard_map/pallas_call | solution.py:199
  150.3 19.7 %all_to_all.26 = f32[32,24,128]{2,1,0:T(8,128)S(1)} all-to-all(f32[32,24,128]{2,1,0:T(8,128)S(1)} %bitcast.47), channel_id=1, replica_groups=mesh['z'=12,'xl'=2,'core'=2,'xh'=2,'y'=8] {'xl','core','y'}, dimensions={0} | all-to-all | bytes 786432 | tf_op jit(solution)/shard_map/all_to_all | solution.py:29
  171.0 3.9 %all-to-all-start.4 = ((f32[16,4,24,128]{3,2,1,0:T(8,128)}), f32[16,4,24,128]{3,2,1,0:T(8,128)S(1)}, u32[]{:S(2)}, u32[]{:S(2)}) async-start(f32[16,4,24,128]{3,2,1,0:T(8,128)} %broadcast_in_dim.15), calls=%async_computation.4 | async-start | bytes 1572864 | tf_op jit(solution)/shard_map/all_to_all | solution.py:29
  174.9 4.9 %collective-permute-start.8 = (f32[2,8,768]{2,1,0:T(8,128)S(1)}, f32[2,8,768]{2,1,0:T(8,128)S(1)}, u32[]{:S(2)}, u32[]{:S(2)}) collective-permute-start(f32[2,8,768]{2,1,0:T(8,128)S(1)} %get-tuple-element.30), channel_id=1, source_target_pairs={{0,8},{8,0},{1,9},{9,1},{2,10},{10,2},{3,11},{11,3},{4,12},{12,4},... | collective-permute-start | bytes 147464 | tf_op jit(solution)/shard_map/ppermute | solution.py:15
  179.8 2.6 %collective-permute-done.8 = f32[2,8,768]{2,1,0:T(8,128)S(1)} collective-permute-done((f32[2,8,768]{2,1,0:T(8,128)S(1)}, f32[2,8,768]{2,1,0:T(8,128)S(1)}, u32[]{:S(2)}, u32[]{:S(2)}) %collective-permute-start.8) | collective-permute-done | bytes 49184 | tf_op jit(solution)/shard_map/ppermute | solution.py:15
  183.0 13.9 %all-to-all-done.4 = f32[16,4,24,128]{3,2,1,0:T(8,128)S(1)} async-done(((f32[16,4,24,128]{3,2,1,0:T(8,128)}), f32[16,4,24,128]{3,2,1,0:T(8,128)S(1)}, u32[]{:S(2)}, u32[]{:S(2)}) %all-to-all-start.4) | async-done | bytes 786464 | tf_op jit(solution)/shard_map/all_to_all | solution.py:29
  198.1 2.9 %shard_map.96 = (bf16[768,256]{1,0:T(8,128)(2,1)}, f32[768,256]{1,0:T(8,128)}) custom-call(f32[2,8,4,24,128]{4,3,2,1,0:T(8,128)S(1)} %bitcast.46, f32[768,768]{1,0:T(8,128)S(1)} %copy-done.1, f32[768,256]{1,0:T(8,128)S(1)} %copy-done.6), custom_call_target="tpu_custom_call" | custom-call | flops 905969664 | bytes 6000000 | tf_op jit(solution)/shard_map/pallas_call | solution.py:252
  (40 shorter events, 10.0 us)
Async XLA Ops:
  0.6 27.4 %collective-permute-start.1 = (f32[256,768]{1,0:T(8,128)}, f32[256,768]{1,0:T(8,128)S(1)}, u32[]{:S(2)}, u32[]{:S(2)}) collective-permute-start(f32[256,768]{1,0:T(8,128)} %refs_0_.1), channel_id=1, source_target_pairs={{0,40},{40,0},{8,32},{32,8},{1,41},{41,1},{9,33},{33,9},{2,42},{42... | collective-permute-start | bytes 2359304 | tf_op jit(solution)/shard_map/ppermute | solution.py:19
  5.3 22.7 %collective-permute-start.2 = (f32[256,768]{1,0:T(8,128)}, f32[256,768]{1,0:T(8,128)S(1)}, u32[]{:S(2)}, u32[]{:S(2)}) collective-permute-start(f32[256,768]{1,0:T(8,128)} %refs_0_.1), channel_id=1, source_target_pairs={{0,32},{32,0},{1,33},{33,1},{2,34},{34,2},{3,35},{35,3},{4,36},{36... | collective-permute-start | bytes 2359304 | tf_op jit(solution)/shard_map/ppermute | solution.py:15
  7.4 1.7 copy-start
  9.1 1.0 copy-start.7
  10.1 15.8 %copy-start.2 = (f32[256,768]{1,0:T(8,128)S(1)}, f32[256,768]{1,0:T(8,128)}, u32[]{:S(2)}) copy-start(f32[256,768]{1,0:T(8,128)} %refs_0_.1) | copy-start | bytes 2359300
  12.8 36.0 %all-to-all-start = ((f32[64,24,128]{2,1,0:T(8,128)}), f32[64,24,128]{2,1,0:T(8,128)}, u32[]{:S(2)}, u32[]{:S(2)}) async-start(f32[64,24,128]{2,1,0:T(8,128)} %bitcast.7), calls=%async_computation | async-start | bytes 1572864 | tf_op jit(solution)/shard_map/all_to_all | solution.py:29
  26.0 11.8 %collective-permute-start.4 = (f32[256,768]{1,0:T(8,128)S(1)}, f32[256,768]{1,0:T(8,128)S(1)}, u32[]{:S(2)}, u32[]{:S(2)}) collective-permute-start(f32[256,768]{1,0:T(8,128)S(1)} %copy-done.2), channel_id=1, source_target_pairs={{0,16},{16,0},{1,17},{17,1},{2,18},{18,2},{3,19},{19,3},{4,20},{20... | collective-permute-start | bytes 2359304 | tf_op jit(solution)/shard_map/ppermute | solution.py:15
  29.0 19.7 %collective-permute-start.3 = (f32[256,768]{1,0:T(8,128)}, f32[256,768]{1,0:T(8,128)}, u32[]{:S(2)}, u32[]{:S(2)}) collective-permute-start(f32[256,768]{1,0:T(8,128)} %broadcast_select_fusion), channel_id=1, source_target_pairs={{0,32},{8,40},{16,56},{24,48},{32,0},{40,8},{48,24},{56,16},{1,33}... | collective-permute-start | bytes 2359304 | tf_op jit(solution)/shard_map/ppermute | solution.py:25
  32.6 16.2 %collective-permute-start.5 = (f32[256,768]{1,0:T(8,128)S(1)}, f32[256,768]{1,0:T(8,128)}, u32[]{:S(2)}, u32[]{:S(2)}) collective-permute-start(f32[256,768]{1,0:T(8,128)S(1)} %collective-permute-done.2.refs_2_), channel_id=1, source_target_pairs={{0,16},{16,0},{1,17},{17,1},{2,18},{18,2},{3,19},{19,3},{4,20},{20... | collective-permute-start | bytes 2359304 | tf_op jit(solution)/shard_map/ppermute | solution.py:15
  35.8 13.0 %collective-permute-start.6 = (f32[256,768]{1,0:T(8,128)S(1)}, f32[256,768]{1,0:T(8,128)}, u32[]{:S(2)}, u32[]{:S(2)}) collective-permute-start(f32[256,768]{1,0:T(8,128)S(1)} %collective-permute-done.1.refs_6_), channel_id=1, source_target_pairs={{0,16},{16,0},{1,17},{17,1},{2,18},{18,2},{3,19},{19,3},{4,20},{20... | collective-permute-start | bytes 2359304 | tf_op jit(solution)/shard_map/ppermute | solution.py:15
  49.9 22.1 %collective-permute-start.7 = (f32[256,768]{1,0:T(8,128)}, f32[256,768]{1,0:T(8,128)S(1)}, u32[]{:S(2)}, u32[]{:S(2)}) collective-permute-start(f32[256,768]{1,0:T(8,128)} %collective-permute-done.3.refs_4_), channel_id=1, source_target_pairs={{0,16},{16,0},{1,17},{17,1},{2,18},{18,2},{3,19},{19,3},{4,20},{20... | collective-permute-start | bytes 2359304 | tf_op jit(solution)/shard_map/ppermute | solution.py:15
  72.0 20.9 %copy-start.8 = (f32[16,768]{1,0:T(8,128)S(1)}, f32[16,768]{1,0:T(8,128)}, u32[]{:S(2)}) copy-start(f32[16,768]{1,0:T(8,128)} %param.8) | copy-start | bytes 147460
  72.0 20.9 %copy-start.9 = (f32[16,768]{1,0:T(8,128)S(1)}, f32[16,768]{1,0:T(8,128)}, u32[]{:S(2)}) copy-start(f32[16,768]{1,0:T(8,128)} %param.9) | copy-start | bytes 147460
  75.9 0.9 copy-start.3
  76.8 0.8 copy-start.5
  77.6 40.0 %all-to-all-start.2 = ((f32[12,16,768]{2,1,0:T(8,128)}), f32[12,16,768]{2,1,0:T(8,128)}, u32[]{:S(2)}, u32[]{:S(2)}) async-start(f32[12,16,768]{2,1,0:T(8,128)} %copy-done.5), calls=%async_computation.2 | async-start | bytes 1179648 | tf_op jit(solution)/shard_map/all_to_all | solution.py:29
  92.9 25.9 %collective-permute-start = (f32[2,8,768]{2,1,0:T(8,128)S(1)}, f32[2,8,768]{2,1,0:T(8,128)S(1)}, u32[]{:S(2)}, u32[]{:S(2)}) collective-permute-start(f32[2,8,768]{2,1,0:T(8,128)S(1)} %get-tuple-element.32), channel_id=1, source_target_pairs={{0,8},{8,0},{1,9},{9,1},{2,10},{10,2},{3,11},{11,3},{4,12},{12,4},... | collective-permute-start | bytes 147464 | tf_op jit(solution)/shard_map/ppermute | solution.py:15
  144.5 1.1 copy-start.4
  150.3 46.7 %copy-start.1 = (f32[768,768]{1,0:T(8,128)S(1)}, f32[768,768]{1,0:T(8,128)}, u32[]{:S(2)}) copy-start(f32[768,768]{1,0:T(8,128)} %left_ref.3) | copy-start | bytes 7077892
  171.0 26.0 %all-to-all-start.4 = ((f32[16,4,24,128]{3,2,1,0:T(8,128)}), f32[16,4,24,128]{3,2,1,0:T(8,128)S(1)}, u32[]{:S(2)}, u32[]{:S(2)}) async-start(f32[16,4,24,128]{3,2,1,0:T(8,128)} %broadcast_in_dim.15), calls=%async_computation.4 | async-start | bytes 1572864 | tf_op jit(solution)/shard_map/all_to_all | solution.py:29
  174.9 7.5 %collective-permute-start.8 = (f32[2,8,768]{2,1,0:T(8,128)S(1)}, f32[2,8,768]{2,1,0:T(8,128)S(1)}, u32[]{:S(2)}, u32[]{:S(2)}) collective-permute-start(f32[2,8,768]{2,1,0:T(8,128)S(1)} %get-tuple-element.30), channel_id=1, source_target_pairs={{0,8},{8,0},{1,9},{9,1},{2,10},{10,2},{3,11},{11,3},{4,12},{12,4},... | collective-permute-start | bytes 147464 | tf_op jit(solution)/shard_map/ppermute | solution.py:15
  197.0 1.1 copy-start.6

commit v7 on v6

--- a/solution.py
+++ b/solution.py
@@ -15,14 +15,9 @@
     return lax.ppermute(x, axis, [(0, 1), (1, 0)])
 
 
-def cross(x):
-    return lax.ppermute(x, ("xl", "xh"), [(0, 3), (3, 0), (1, 2), (2, 1)])
-
-
-def relay(x):
-    flip = (4, 7)
-    pairs = [(i, i ^ flip[(i >> 1) & 1] ^ (2 * ((i >> 1) & 1))) for i in range(8)]
-    return lax.ppermute(x, ("xl", "core", "xh"), pairs)
+def cross(x, to_core=0):
+    flip = 5 + 2 * to_core
+    return lax.ppermute(x, ("xl", "core", "xh"), [(i, i ^ flip) for i in range(8)])
 
 
 def exchange(x, axes):
@@ -100,7 +95,7 @@
             pltpu.VMEM((keys, window), jnp.float32),
             pltpu.VMEM((window // 8, keys), jnp.float32),
         ],
-        compiler_params=pltpu.CompilerParams(vmem_limit_bytes=24 * 2**20),
+        compiler_params=pltpu.CompilerParams(vmem_limit_bytes=59 * 2**20),
         cost_estimate=pl.CostEstimate(
             flops=4 * height * window * keys, bytes_accessed=4_000_000, transcendentals=0
         ),
@@ -145,7 +140,7 @@
         in_specs=[pl.BlockSpec(left.shape, lambda j: (0, 0, 0))]
         + [pl.BlockSpec((keys, block), lambda j: (0, j))] * 8,
         out_specs=pl.BlockSpec((depth, 2 * few, block), lambda j: (0, 0, j)),
-        out_shape=jax.ShapeDtypeStruct((depth, 2 * few, cols), jnp.float32),
+        out_shape=pltpu.HBM((depth, 2 * few, cols), jnp.float32),
         scratch_shapes=[
             pltpu.VMEM((count, 4 * keys), jnp.float32),
             pltpu.VMEM((count, 4 * keys), jnp.bfloat16),
@@ -289,19 +284,18 @@
         other = lax.dynamic_index_in_dim(x, 1 - xh, axis, keepdims=False)
         return mine, swap(other, "xh")
 
-    by_xl = swap(right_basis, "xl")
-    by_both = cross(right_basis)
-    by_xh = relay(jnp.where(core == 0, by_both, by_xl))
+    by_xl, by_both = swap(right_basis, "xl"), cross(right_basis)
+    by_xh, by_xh_core = swap(by_both, "xl"), cross(by_xl, to_core=1)
     early = [x for ring in (right_basis, by_xl, by_both) for x in (ring, swap(ring, "core"))]
 
     parts = start(left_basis, gradient, peers)
     parts = exchange(parts.reshape((-1,) + parts.shape[3:]), ("xl", "core", "xh", "y"))
-    parts, by_xh, early = lax.optimization_barrier((parts, by_xh, early))
+    parts, early = lax.optimization_barrier((parts, early))
     left_chunk = jnp.sum(parts.reshape(2, 2, 2 * peers, -1, LANES), axis=2)
     left_chunk = jnp.where(xl == 0, left_chunk, left_chunk[::-1])
     left_chunk = jnp.where(core == 0, left_chunk, left_chunk[:, ::-1])
     left_rotated = copies_to(left_chunk.reshape(-1, LANES), "y")
-    basis = early[:4] + [by_xh, swap(by_xh, "core")] + early[4:]
+    basis = early[:4] + [by_xh, by_xh_core] + early[4:]
 
     rotated = jnp.sum(exchange(forth(left_rotated, basis, few), "z"), axis=0)
 

time: 202 us -> 194 us (0.960)
  blocking collectives: 64.9 us -> 46.1 us
  starting transfers between devices: 59 us -> 66.8 us
  waiting for transfers between devices: 50.4 us -> 56 us
  local copies, waits for them, and re-layouts: 8.27 us -> 3.52 us
  Pallas kernels: 14.1 us -> 16.8 us
    all_to_all x2 -> x1, blocking collectives: 39.2 us -> 20.8 us  [exchange(): return lax.all_to_all(x, axes, 0, 0, tiled=True)]
    unnamed x20 -> x6, local copies, waits for them, and re-layouts: 6.64 us -> 1.14 us
    all_to_all x3 -> x4, starting transfers between devices: 32.3 us -> 36.6 us  [exchange(): return lax.all_to_all(x, axes, 0, 0, tiled=True)]
    ppermute x7, starting transfers between devices: 18.5 us -> 22.7 us  [swap(): return lax.ppermute(x, axis, [(0, 1), (1, 0)])]
    ppermute x7, waiting for transfers between devices: 2.61 us -> 5.82 us  [swap(): return lax.ppermute(x, axis, [(0, 1), (1, 0)])]
    ppermute x2, waiting for transfers between devices: 0.01 us -> 2.75 us  [cross(): lax.ppermute(x, ('xl', 'core', 'xh'), [(i, i ^ flip) for i in range(8)])]
    all_to_all x3 -> x4, waiting for transfers between devices: 47.8 us -> 47.5 us  [exchange(): return lax.all_to_all(x, axes, 0, 0, tiled=True)]
  transfers between devices with their start and end apart: 12 -> 13, of which waited for: 4 -> 7; matrix products, arithmetic and copies ran while one was open for 1% -> 2% of each run, Pallas kernels for 1% -> 2%
where the time goes in v7:
time: 194 us; the launch traced here: 193 us
  starting transfers between devices  66.8 us (34%)
  waiting for transfers between devices  56 us (29%)
  blocking collectives  46.1 us (24%)
  Pallas kernels  16.8 us (9%)
  local copies, waits for them, and re-layouts  3.52 us (2%)
  other arithmetic  3.18 us (2%)
    all_to_all x4, waiting for transfers between devices, exchange(): return lax.all_to_all(x, axes, 0, 0, tiled=True)  47.5 us
    all_to_all x4, starting transfers between devices, exchange(): return lax.all_to_all(x, axes, 0, 0, tiled=True)  36.6 us
    all_gather x1, blocking collectives, shards(): column = lax.all_gather(normed, 'z', axis=0, tiled=False)  25.3 us
    ppermute x7, starting transfers between devices, swap(): return lax.ppermute(x, axis, [(0, 1), (1, 0)])  22.7 us
    all_to_all x1, blocking collectives, exchange(): return lax.all_to_all(x, axes, 0, 0, tiled=True)  20.8 us
    ppermute x2, starting transfers between devices, cross(): lax.ppermute(x, ('xl', 'core', 'xh'), [(i, i ^ flip) for i in range(8)])  7.49 us
    ppermute x7, waiting for transfers between devices, swap(): return lax.ppermute(x, axis, [(0, 1), (1, 0)])  5.82 us
    pallas_call x1, Pallas kernels, rotate_back(): pl.pallas_call(back_kernel, grid=(2,), in_specs=[pl.BlockSpec(memory_spac...  4.79 us
  transfers between devices with their start and end apart: 13, of which 7 were waited for; matrix products, arithmetic and copies ran while one was open for 2% of the time, Pallas kernels for 2%

profile of v7, /device:TPU:8, one launch (start us, length us, event | category | flops | bytes accessed | tf_op | source)
XLA Modules:
  0.0 193.4 jit_solution(550164986388549206)
XLA Ops:
  0.6 3.5 %collective-permute-start.2 = (f32[256,768]{1,0:T(8,128)}, f32[256,768]{1,0:T(8,128)S(1)}, u32[]{:S(2)}, u32[]{:S(2)}) collective-permute-start(f32[256,768]{1,0:T(8,128)} %refs_0_.1), channel_id=1, source_target_pairs={{0,32},{32,0},{1,33},{33,1},{2,34},{34,2},{3,35},{35,3},{4,36},{36... | collective-permute-start | bytes 2359304 | tf_op jit(solution)/shard_map/ppermute | solution.py:15
  4.2 4.0 %collective-permute-start.4 = (f32[256,768]{1,0:T(8,128)}, f32[256,768]{1,0:T(8,128)S(1)}, u32[]{:S(2)}, u32[]{:S(2)}) collective-permute-start(f32[256,768]{1,0:T(8,128)} %refs_0_.1), channel_id=1, source_target_pairs={{0,40},{8,32},{16,56},{24,48},{32,8},{40,0},{48,24},{56,16},{1,41}... | collective-permute-start | bytes 2359304 | tf_op jit(solution)/shard_map/ppermute | solution.py:20
  8.2 4.4 %shard_map.93 = f32[4,2,8,24,128]{4,3,2,1,0:T(8,128)} custom-call(f32[768,768]{1,0:T(8,128)} %left_ref.3, bf16[768,256]{1,0:T(8,128)(2,1)} %gradient_ref.1), custom_call_target="tpu_custom_call" | custom-call | flops 603979776 | bytes 4000000 | tf_op jit(solution)/shard_map/pallas_call | solution.py:85
  12.6 12.0 %all-to-all-start = ((f32[64,24,128]{2,1,0:T(8,128)}), f32[64,24,128]{2,1,0:T(8,128)}, u32[]{:S(2)}, u32[]{:S(2)}) async-start(f32[64,24,128]{2,1,0:T(8,128)} %bitcast.48), calls=%async_computation | async-start | bytes 1572864 | tf_op jit(solution)/shard_map/all_to_all | solution.py:24
  26.7 2.3 %collective-permute-start.3 = (f32[256,768]{1,0:T(8,128)S(1)}, f32[256,768]{1,0:T(8,128)}, u32[]{:S(2)}, u32[]{:S(2)}) collective-permute-start(f32[256,768]{1,0:T(8,128)S(1)} %collective-permute-done.2.refs_2_), channel_id=1, source_target_pairs={{0,16},{16,0},{1,17},{17,1},{2,18},{18,2},{3,19},{19,3},{4,20},{20... | collective-permute-start | bytes 2359304 | tf_op jit(solution)/shard_map/ppermute | solution.py:15
  31.1 3.6 %collective-permute-start.6 = (f32[256,768]{1,0:T(8,128)S(1)}, f32[256,768]{1,0:T(8,128)}, u32[]{:S(2)}, u32[]{:S(2)}) collective-permute-start(f32[256,768]{1,0:T(8,128)S(1)} %collective-permute-done.4.refs_6_), channel_id=1, source_target_pairs={{0,32},{32,0},{1,33},{33,1},{2,34},{34,2},{3,35},{35,3},{4,36},{36... | collective-permute-start | bytes 2359304 | tf_op jit(solution)/shard_map/ppermute | solution.py:15
  34.6 3.5 %collective-permute-start.7 = (f32[256,768]{1,0:T(8,128)S(1)}, f32[256,768]{1,0:T(8,128)}, u32[]{:S(2)}, u32[]{:S(2)}) collective-permute-start(f32[256,768]{1,0:T(8,128)S(1)} %collective-permute-done.2.refs_2_), channel_id=1, source_target_pairs={{0,56},{8,48},{16,40},{24,32},{32,24},{40,16},{48,8},{56,0},{1,57}... | collective-permute-start | bytes 2359304 | tf_op jit(solution)/shard_map/ppermute | solution.py:20
  38.1 9.3 %all-to-all-done = f32[64,24,128]{2,1,0:T(8,128)} async-done(((f32[64,24,128]{2,1,0:T(8,128)}), f32[64,24,128]{2,1,0:T(8,128)}, u32[]{:S(2)}, u32[]{:S(2)}) %all-to-all-start) | async-done | bytes 786464 | tf_op jit(solution)/shard_map/all_to_all | solution.py:24
  49.4 5.1 %all-to-all-start.1 = ((f32[8,96,128]{2,1,0:T(8,128)}), f32[8,96,128]{2,1,0:T(8,128)S(1)}, u32[]{:S(2)}, u32[]{:S(2)}) async-start(f32[8,96,128]{2,1,0:T(8,128)} %broadcast_in_dim.14), calls=%async_computation.1 | async-start | bytes 786432 | tf_op jit(solution)/shard_map/all_to_all | solution.py:24
  54.5 3.2 %collective-permute-done.6.refs_4_ = f32[256,768]{1,0:T(8,128)} collective-permute-done((f32[256,768]{1,0:T(8,128)S(1)}, f32[256,768]{1,0:T(8,128)}, u32[]{:S(2)}, u32[]{:S(2)}) %collective-permute-start.6) | collective-permute-done | bytes 786464 | tf_op jit(solution)/shard_map/ppermute | solution.py:15
  57.7 2.7 %collective-permute-done.7.refs_5_ = f32[256,768]{1,0:T(8,128)} collective-permute-done((f32[256,768]{1,0:T(8,128)S(1)}, f32[256,768]{1,0:T(8,128)}, u32[]{:S(2)}, u32[]{:S(2)}) %collective-permute-start.7) | collective-permute-done | bytes 786464 | tf_op jit(solution)/shard_map/ppermute | solution.py:20
  60.4 7.1 %all-to-all-done.1.left_ref = f32[8,96,128]{2,1,0:T(8,128)S(1)} async-done(((f32[8,96,128]{2,1,0:T(8,128)}), f32[8,96,128]{2,1,0:T(8,128)S(1)}, u32[]{:S(2)}, u32[]{:S(2)}) %all-to-all-start.1) | async-done | bytes 393248 | tf_op jit(solution)/shard_map/all_to_all | solution.py:24
  67.5 4.7 %shard_map.94 = f32[12,16,768]{2,1,0:T(8,128)} custom-call(f32[8,96,128]{2,1,0:T(8,128)S(1)} %all-to-all-done.1.left_ref, f32[256,768]{1,0:T(8,128)S(1)} %copy-done.1, f32[256,768]{1,0:T(8,128)S(1)} %collective-permute-done.1.refs_1_, f32[256,768]{1,0:T(8,128)S(1)} %collective-permute-done.2.refs_2_, f32[256,768]{1,0:T(8,128)} %collective-permute-done.3.refs_3_, ...), custom_call_target="tpu_custom_call" | custom-call | flops 905969664 | bytes 8000000 | tf_op jit(solution)/shard_map/pallas_call | solution.py:137
  72.2 12.0 %all-to-all-start.2 = ((f32[12,16,768]{2,1,0:T(8,128)}), f32[12,16,768]{2,1,0:T(8,128)}, u32[]{:S(2)}, u32[]{:S(2)}) async-start(f32[12,16,768]{2,1,0:T(8,128)} %shard_map.94), calls=%async_computation.2 | async-start | bytes 1179648 | tf_op jit(solution)/shard_map/all_to_all | solution.py:24
  85.1 4.3 %collective-permute-start = (f32[2,8,768]{2,1,0:T(8,128)S(1)}, f32[2,8,768]{2,1,0:T(8,128)S(1)}, u32[]{:S(2)}, u32[]{:S(2)}) collective-permute-start(f32[2,8,768]{2,1,0:T(8,128)S(1)} %get-tuple-element.30), channel_id=1, source_target_pairs={{0,8},{8,0},{1,9},{9,1},{2,10},{10,2},{3,11},{11,3},{4,12},{12,4},... | collective-permute-start | bytes 147464 | tf_op jit(solution)/shard_map/ppermute | solution.py:15
  89.4 17.1 %all-to-all-done.2 = f32[12,16,768]{2,1,0:T(8,128)} async-done(((f32[12,16,768]{2,1,0:T(8,128)}), f32[12,16,768]{2,1,0:T(8,128)}, u32[]{:S(2)}, u32[]{:S(2)}) %all-to-all-start.2) | async-done | bytes 589856 | tf_op jit(solution)/shard_map/all_to_all | solution.py:24
  107.7 25.3 %all_gather.4.column_ref = f32[12,16,768]{2,1,0:T(8,128)S(1)} all-gather(f32[1,16,768]{2,1,0:T(8,128)S(1)} %get-tuple-element.24), channel_id=1, replica_groups=mesh['z'=12,'xl'=2,'core'=2,'xh'=2,'y'=8] {'z'}, dimensions={0}, use_global_device_ids=true | all-gather | bytes 638976 | tf_op jit(solution)/shard_map/all_gather | solution.py:308
  133.0 4.8 %shard_map.95 = f32[4,8,24,128]{3,2,1,0:T(8,128)S(1)} custom-call(s32[1]{0:T(128)} %bitcast.me_ref, f32[12,16,768]{2,1,0:T(8,128)S(1)} %all_gather.4.column_ref, f32[256,768]{1,0:T(8,128)S(1)} %copy-done.1, f32[256,768]{1,0:T(8,128)S(1)} %collective-permute-done.1.refs_1_, f32[256,768]{1,0:T(8,128)S(1)} %collective-permute-done.2.refs_2_, ...), custom_call_target="tpu_custom_call" | custom-call | flops 905969664 | bytes 8000000 | tf_op jit(solution)/shard_map/pallas_call | solution.py:194
  137.8 20.8 %all_to_all.25 = f32[32,24,128]{2,1,0:T(8,128)S(1)} all-to-all(f32[32,24,128]{2,1,0:T(8,128)S(1)} %bitcast.47), channel_id=1, replica_groups=mesh['z'=12,'xl'=2,'core'=2,'xh'=2,'y'=8] {'xl','core','y'}, dimensions={0} | all-to-all | bytes 786432 | tf_op jit(solution)/shard_map/all_to_all | solution.py:24
  159.7 7.6 %all-to-all-start.4 = ((f32[16,4,24,128]{3,2,1,0:T(8,128)}), f32[16,4,24,128]{3,2,1,0:T(8,128)S(1)}, u32[]{:S(2)}, u32[]{:S(2)}) async-start(f32[16,4,24,128]{3,2,1,0:T(8,128)} %broadcast_in_dim.15), calls=%async_computation.4 | async-start | bytes 1572864 | tf_op jit(solution)/shard_map/all_to_all | solution.py:24
  167.2 4.9 %collective-permute-start.8 = (f32[2,8,768]{2,1,0:T(8,128)S(1)}, f32[2,8,768]{2,1,0:T(8,128)S(1)}, u32[]{:S(2)}, u32[]{:S(2)}) collective-permute-start(f32[2,8,768]{2,1,0:T(8,128)S(1)} %get-tuple-element.28), channel_id=1, source_target_pairs={{0,8},{8,0},{1,9},{9,1},{2,10},{10,2},{3,11},{11,3},{4,12},{12,4},... | collective-permute-start | bytes 147464 | tf_op jit(solution)/shard_map/ppermute | solution.py:15
  172.1 2.6 %collective-permute-done.8 = f32[2,8,768]{2,1,0:T(8,128)S(1)} collective-permute-done((f32[2,8,768]{2,1,0:T(8,128)S(1)}, f32[2,8,768]{2,1,0:T(8,128)S(1)}, u32[]{:S(2)}, u32[]{:S(2)}) %collective-permute-start.8) | collective-permute-done | bytes 49184 | tf_op jit(solution)/shard_map/ppermute | solution.py:15
  175.4 13.9 %all-to-all-done.4 = f32[16,4,24,128]{3,2,1,0:T(8,128)S(1)} async-done(((f32[16,4,24,128]{3,2,1,0:T(8,128)}), f32[16,4,24,128]{3,2,1,0:T(8,128)S(1)}, u32[]{:S(2)}, u32[]{:S(2)}) %all-to-all-start.4) | async-done | bytes 786464 | tf_op jit(solution)/shard_map/all_to_all | solution.py:24
  190.4 2.9 %shard_map.96 = (bf16[768,256]{1,0:T(8,128)(2,1)}, f32[768,256]{1,0:T(8,128)}) custom-call(f32[2,8,4,24,128]{4,3,2,1,0:T(8,128)S(1)} %bitcast.46, f32[768,768]{1,0:T(8,128)S(1)} %copy-done, f32[768,256]{1,0:T(8,128)S(1)} %copy-done.2), custom_call_target="tpu_custom_call" | custom-call | flops 905969664 | bytes 6000000 | tf_op jit(solution)/shard_map/pallas_call | solution.py:247
  (26 shorter events, 10.8 us)
Async XLA Ops:
  0.6 24.0 %copy-start.1 = (f32[256,768]{1,0:T(8,128)S(1)}, f32[256,768]{1,0:T(8,128)}, u32[]{:S(2)}) copy-start(f32[256,768]{1,0:T(8,128)} %refs_0_.1) | copy-start | bytes 2359300
  0.6 26.0 %collective-permute-start.2 = (f32[256,768]{1,0:T(8,128)}, f32[256,768]{1,0:T(8,128)S(1)}, u32[]{:S(2)}, u32[]{:S(2)}) collective-permute-start(f32[256,768]{1,0:T(8,128)} %refs_0_.1), channel_id=1, source_target_pairs={{0,32},{32,0},{1,33},{33,1},{2,34},{34,2},{3,35},{35,3},{4,36},{36... | collective-permute-start | bytes 2359304 | tf_op jit(solution)/shard_map/ppermute | solution.py:15
  4.2 24.8 %collective-permute-start.4 = (f32[256,768]{1,0:T(8,128)}, f32[256,768]{1,0:T(8,128)S(1)}, u32[]{:S(2)}, u32[]{:S(2)}) collective-permute-start(f32[256,768]{1,0:T(8,128)} %refs_0_.1), channel_id=1, source_target_pairs={{0,40},{8,32},{16,56},{24,48},{32,8},{40,0},{48,24},{56,16},{1,41}... | collective-permute-start | bytes 2359304 | tf_op jit(solution)/shard_map/ppermute | solution.py:20
  12.6 34.8 %all-to-all-start = ((f32[64,24,128]{2,1,0:T(8,128)}), f32[64,24,128]{2,1,0:T(8,128)}, u32[]{:S(2)}, u32[]{:S(2)}) async-start(f32[64,24,128]{2,1,0:T(8,128)} %bitcast.48), calls=%async_computation | async-start | bytes 1572864 | tf_op jit(solution)/shard_map/all_to_all | solution.py:24
  24.6 13.5 %collective-permute-start.1 = (f32[256,768]{1,0:T(8,128)S(1)}, f32[256,768]{1,0:T(8,128)S(1)}, u32[]{:S(2)}, u32[]{:S(2)}) collective-permute-start(f32[256,768]{1,0:T(8,128)S(1)} %copy-done.1), channel_id=1, source_target_pairs={{0,16},{16,0},{1,17},{17,1},{2,18},{18,2},{3,19},{19,3},{4,20},{20... | collective-permute-start | bytes 2359304 | tf_op jit(solution)/shard_map/ppermute | solution.py:15
  26.7 20.7 %collective-permute-start.3 = (f32[256,768]{1,0:T(8,128)S(1)}, f32[256,768]{1,0:T(8,128)}, u32[]{:S(2)}, u32[]{:S(2)}) collective-permute-start(f32[256,768]{1,0:T(8,128)S(1)} %collective-permute-done.2.refs_2_), channel_id=1, source_target_pairs={{0,16},{16,0},{1,17},{17,1},{2,18},{18,2},{3,19},{19,3},{4,20},{20... | collective-permute-start | bytes 2359304 | tf_op jit(solution)/shard_map/ppermute | solution.py:15
  29.0 18.4 %collective-permute-start.5 = (f32[256,768]{1,0:T(8,128)S(1)}, f32[256,768]{1,0:T(8,128)}, u32[]{:S(2)}, u32[]{:S(2)}) collective-permute-start(f32[256,768]{1,0:T(8,128)S(1)} %collective-permute-done.4.refs_6_), channel_id=1, source_target_pairs={{0,16},{16,0},{1,17},{17,1},{2,18},{18,2},{3,19},{19,3},{4,20},{20... | collective-permute-start | bytes 2359304 | tf_op jit(solution)/shard_map/ppermute | solution.py:15
  31.1 26.6 %collective-permute-start.6 = (f32[256,768]{1,0:T(8,128)S(1)}, f32[256,768]{1,0:T(8,128)}, u32[]{:S(2)}, u32[]{:S(2)}) collective-permute-start(f32[256,768]{1,0:T(8,128)S(1)} %collective-permute-done.4.refs_6_), channel_id=1, source_target_pairs={{0,32},{32,0},{1,33},{33,1},{2,34},{34,2},{3,35},{35,3},{4,36},{36... | collective-permute-start | bytes 2359304 | tf_op jit(solution)/shard_map/ppermute | solution.py:15
  34.6 25.8 %collective-permute-start.7 = (f32[256,768]{1,0:T(8,128)S(1)}, f32[256,768]{1,0:T(8,128)}, u32[]{:S(2)}, u32[]{:S(2)}) collective-permute-start(f32[256,768]{1,0:T(8,128)S(1)} %collective-permute-done.2.refs_2_), channel_id=1, source_target_pairs={{0,56},{8,48},{16,40},{24,32},{32,24},{40,16},{48,8},{56,0},{1,57}... | collective-permute-start | bytes 2359304 | tf_op jit(solution)/shard_map/ppermute | solution.py:20
  49.4 18.1 %all-to-all-start.1 = ((f32[8,96,128]{2,1,0:T(8,128)}), f32[8,96,128]{2,1,0:T(8,128)S(1)}, u32[]{:S(2)}, u32[]{:S(2)}) async-start(f32[8,96,128]{2,1,0:T(8,128)} %broadcast_in_dim.14), calls=%async_computation.1 | async-start | bytes 786432 | tf_op jit(solution)/shard_map/all_to_all | solution.py:24
  72.2 34.3 %all-to-all-start.2 = ((f32[12,16,768]{2,1,0:T(8,128)}), f32[12,16,768]{2,1,0:T(8,128)}, u32[]{:S(2)}, u32[]{:S(2)}) async-start(f32[12,16,768]{2,1,0:T(8,128)} %shard_map.94), calls=%async_computation.2 | async-start | bytes 1179648 | tf_op jit(solution)/shard_map/all_to_all | solution.py:24
  85.1 22.6 %collective-permute-start = (f32[2,8,768]{2,1,0:T(8,128)S(1)}, f32[2,8,768]{2,1,0:T(8,128)S(1)}, u32[]{:S(2)}, u32[]{:S(2)}) collective-permute-start(f32[2,8,768]{2,1,0:T(8,128)S(1)} %get-tuple-element.30), channel_id=1, source_target_pairs={{0,8},{8,0},{1,9},{9,1},{2,10},{10,2},{3,11},{11,3},{4,12},{12,4},... | collective-permute-start | bytes 147464 | tf_op jit(solution)/shard_map/ppermute | solution.py:15
  137.8 51.5 %copy-start = (f32[768,768]{1,0:T(8,128)S(1)}, f32[768,768]{1,0:T(8,128)}, u32[]{:S(2)}) copy-start(f32[768,768]{1,0:T(8,128)} %left_ref.3) | copy-start | bytes 7077892
  159.7 29.6 %all-to-all-start.4 = ((f32[16,4,24,128]{3,2,1,0:T(8,128)}), f32[16,4,24,128]{3,2,1,0:T(8,128)S(1)}, u32[]{:S(2)}, u32[]{:S(2)}) async-start(f32[16,4,24,128]{3,2,1,0:T(8,128)} %broadcast_in_dim.15), calls=%async_computation.4 | async-start | bytes 1572864 | tf_op jit(solution)/shard_map/all_to_all | solution.py:24
  167.2 7.5 %collective-permute-start.8 = (f32[2,8,768]{2,1,0:T(8,128)S(1)}, f32[2,8,768]{2,1,0:T(8,128)S(1)}, u32[]{:S(2)}, u32[]{:S(2)}) collective-permute-start(f32[2,8,768]{2,1,0:T(8,128)S(1)} %get-tuple-element.28), channel_id=1, source_target_pairs={{0,8},{8,0},{1,9},{9,1},{2,10},{10,2},{3,11},{11,3},{4,12},{12,4},... | collective-permute-start | bytes 147464 | tf_op jit(solution)/shard_map/ppermute | solution.py:15
  189.3 1.1 copy-start.2

commit v8 on v7

--- a/solution.py
+++ b/solution.py
@@ -315,6 +315,7 @@
     me = (2 * xl + core).astype(jnp.int32).reshape(1)
     back_part = rotate_back(me, column, basis, peers)
     back_part = exchange(back_part.reshape((-1,) + back_part.shape[2:]), ("xl", "core", "y"))
+    back_part, *moments = lax.optimization_barrier((back_part, moments[0], moments[1]))
     back_chunk = jnp.sum(back_part.reshape((4, peers) + back_part.shape[1:]), axis=1)
     got = copies_to(back_chunk, COL).reshape((2, peers) + back_chunk.shape)
     new_weight, direction = finish(got, left_basis, master_weight)

time: 194 us -> 196 us (1.010)
  waiting for transfers between devices: 56 us -> 44.6 us
  blocking collectives: 46.1 us -> 56.2 us
  other arithmetic: 3.18 us -> 6.1 us
  local copies, waits for them, and re-layouts: 3.52 us -> 1.5 us
    all_to_all x4, waiting for transfers between devices: 47.5 us -> 35.8 us  [exchange(): return lax.all_to_all(x, axes, 0, 0, tiled=True)]
    all_to_all x1, blocking collectives: 20.8 us -> 30.8 us  [exchange(): return lax.all_to_all(x, axes, 0, 0, tiled=True)]
  transfers between devices with their start and end apart: 13 -> 13, of which waited for: 7 -> 7; matrix products, arithmetic and copies ran while one was open for 2% -> 4% of each run, Pallas kernels for 2% -> 2%
where the time goes in v8:
time: 196 us; the launch traced here: 195 us
  starting transfers between devices  68 us (35%)
  blocking collectives  56.2 us (29%)
  waiting for transfers between devices  44.6 us (23%)
  Pallas kernels  17.6 us (9%)
  other arithmetic  6.1 us (3%)
    all_to_all x4, starting transfers between devices, exchange(): return lax.all_to_all(x, axes, 0, 0, tiled=True)  36.5 us
    all_to_all x4, waiting for transfers between devices, exchange(): return lax.all_to_all(x, axes, 0, 0, tiled=True)  35.8 us
    all_to_all x1, blocking collectives, exchange(): return lax.all_to_all(x, axes, 0, 0, tiled=True)  30.8 us
    all_gather x1, blocking collectives, shards(): column = lax.all_gather(normed, 'z', axis=0, tiled=False)  25.4 us
    ppermute x7, starting transfers between devices, swap(): return lax.ppermute(x, axis, [(0, 1), (1, 0)])  24 us
    ppermute x2, starting transfers between devices, cross(): lax.ppermute(x, ('xl', 'core', 'xh'), [(i, i ^ flip) for i in range(8)])  7.49 us
    ppermute x7, waiting for transfers between devices, swap(): return lax.ppermute(x, axis, [(0, 1), (1, 0)])  6.04 us
    pallas_call x1, Pallas kernels, rotate_back(): pl.pallas_call(back_kernel, grid=(2,), in_specs=[pl.BlockSpec(memory_spac...  5.51 us
  transfers between devices with their start and end apart: 13, of which 7 were waited for; matrix products, arithmetic and copies ran while one was open for 4% of the time, Pallas kernels for 2%

profile of v8, /device:TPU:8, one launch (start us, length us, event | category | flops | bytes accessed | tf_op | source)
XLA Modules:
  0.0 194.8 jit_solution(8704805190186408527)
XLA Ops:
  0.6 3.5 %collective-permute-start.2 = (f32[256,768]{1,0:T(8,128)}, f32[256,768]{1,0:T(8,128)S(1)}, u32[]{:S(2)}, u32[]{:S(2)}) collective-permute-start(f32[256,768]{1,0:T(8,128)} %refs_0_.1), channel_id=1, source_target_pairs={{0,32},{32,0},{1,33},{33,1},{2,34},{34,2},{3,35},{35,3},{4,36},{36... | collective-permute-start | bytes 2359304 | tf_op jit(solution)/shard_map/ppermute | solution.py:15
  4.2 4.0 %collective-permute-start.4 = (f32[256,768]{1,0:T(8,128)}, f32[256,768]{1,0:T(8,128)S(1)}, u32[]{:S(2)}, u32[]{:S(2)}) collective-permute-start(f32[256,768]{1,0:T(8,128)} %refs_0_.1), channel_id=1, source_target_pairs={{0,40},{8,32},{16,56},{24,48},{32,8},{40,0},{48,24},{56,16},{1,41}... | collective-permute-start | bytes 2359304 | tf_op jit(solution)/shard_map/ppermute | solution.py:20
  8.2 4.4 %shard_map.93 = f32[4,2,8,24,128]{4,3,2,1,0:T(8,128)} custom-call(f32[768,768]{1,0:T(8,128)} %left_ref.3, bf16[768,256]{1,0:T(8,128)(2,1)} %gradient_ref.1), custom_call_target="tpu_custom_call" | custom-call | flops 603979776 | bytes 4000000 | tf_op jit(solution)/shard_map/pallas_call | solution.py:85
  12.6 12.0 %all-to-all-start = ((f32[64,24,128]{2,1,0:T(8,128)}), f32[64,24,128]{2,1,0:T(8,128)}, u32[]{:S(2)}, u32[]{:S(2)}) async-start(f32[64,24,128]{2,1,0:T(8,128)} %bitcast.47), calls=%async_computation | async-start | bytes 1572864 | tf_op jit(solution)/shard_map/all_to_all | solution.py:24
  26.7 2.3 %collective-permute-start.3 = (f32[256,768]{1,0:T(8,128)S(1)}, f32[256,768]{1,0:T(8,128)}, u32[]{:S(2)}, u32[]{:S(2)}) collective-permute-start(f32[256,768]{1,0:T(8,128)S(1)} %collective-permute-done.2.refs_2_), channel_id=1, source_target_pairs={{0,16},{16,0},{1,17},{17,1},{2,18},{18,2},{3,19},{19,3},{4,20},{20... | collective-permute-start | bytes 2359304 | tf_op jit(solution)/shard_map/ppermute | solution.py:15
  31.1 3.6 %collective-permute-start.6 = (f32[256,768]{1,0:T(8,128)S(1)}, f32[256,768]{1,0:T(8,128)}, u32[]{:S(2)}, u32[]{:S(2)}) collective-permute-start(f32[256,768]{1,0:T(8,128)S(1)} %collective-permute-done.4.refs_6_), channel_id=1, source_target_pairs={{0,32},{32,0},{1,33},{33,1},{2,34},{34,2},{3,35},{35,3},{4,36},{36... | collective-permute-start | bytes 2359304 | tf_op jit(solution)/shard_map/ppermute | solution.py:15
  34.6 3.5 %collective-permute-start.7 = (f32[256,768]{1,0:T(8,128)S(1)}, f32[256,768]{1,0:T(8,128)}, u32[]{:S(2)}, u32[]{:S(2)}) collective-permute-start(f32[256,768]{1,0:T(8,128)S(1)} %collective-permute-done.2.refs_2_), channel_id=1, source_target_pairs={{0,56},{8,48},{16,40},{24,32},{32,24},{40,16},{48,8},{56,0},{1,57}... | collective-permute-start | bytes 2359304 | tf_op jit(solution)/shard_map/ppermute | solution.py:20
  38.1 9.3 %all-to-all-done = f32[64,24,128]{2,1,0:T(8,128)} async-done(((f32[64,24,128]{2,1,0:T(8,128)}), f32[64,24,128]{2,1,0:T(8,128)}, u32[]{:S(2)}, u32[]{:S(2)}) %all-to-all-start) | async-done | bytes 786464 | tf_op jit(solution)/shard_map/all_to_all | solution.py:24
  49.4 5.1 %all-to-all-start.1 = ((f32[8,96,128]{2,1,0:T(8,128)}), f32[8,96,128]{2,1,0:T(8,128)S(1)}, u32[]{:S(2)}, u32[]{:S(2)}) async-start(f32[8,96,128]{2,1,0:T(8,128)} %broadcast_in_dim.14), calls=%async_computation.1 | async-start | bytes 786432 | tf_op jit(solution)/shard_map/all_to_all | solution.py:24
  54.5 3.2 %collective-permute-done.6.refs_4_ = f32[256,768]{1,0:T(8,128)} collective-permute-done((f32[256,768]{1,0:T(8,128)S(1)}, f32[256,768]{1,0:T(8,128)}, u32[]{:S(2)}, u32[]{:S(2)}) %collective-permute-start.6) | collective-permute-done | bytes 786464 | tf_op jit(solution)/shard_map/ppermute | solution.py:15
  57.7 2.7 %collective-permute-done.7.refs_5_ = f32[256,768]{1,0:T(8,128)} collective-permute-done((f32[256,768]{1,0:T(8,128)S(1)}, f32[256,768]{1,0:T(8,128)}, u32[]{:S(2)}, u32[]{:S(2)}) %collective-permute-start.7) | collective-permute-done | bytes 786464 | tf_op jit(solution)/shard_map/ppermute | solution.py:20
  60.4 7.1 %all-to-all-done.1.left_ref = f32[8,96,128]{2,1,0:T(8,128)S(1)} async-done(((f32[8,96,128]{2,1,0:T(8,128)}), f32[8,96,128]{2,1,0:T(8,128)S(1)}, u32[]{:S(2)}, u32[]{:S(2)}) %all-to-all-start.1) | async-done | bytes 393248 | tf_op jit(solution)/shard_map/all_to_all | solution.py:24
  67.5 4.7 %shard_map.94 = f32[12,16,768]{2,1,0:T(8,128)} custom-call(f32[8,96,128]{2,1,0:T(8,128)S(1)} %all-to-all-done.1.left_ref, f32[256,768]{1,0:T(8,128)S(1)} %copy-done.1, f32[256,768]{1,0:T(8,128)S(1)} %collective-permute-done.1.refs_1_, f32[256,768]{1,0:T(8,128)S(1)} %collective-permute-done.2.refs_2_, f32[256,768]{1,0:T(8,128)} %collective-permute-done.3.refs_3_, ...), custom_call_target="tpu_custom_call" | custom-call | flops 905969664 | bytes 8000000 | tf_op jit(solution)/shard_map/pallas_call | solution.py:137
  72.2 12.1 %all-to-all-start.2 = ((f32[12,16,768]{2,1,0:T(8,128)}), f32[12,16,768]{2,1,0:T(8,128)}, u32[]{:S(2)}, u32[]{:S(2)}) async-start(f32[12,16,768]{2,1,0:T(8,128)} %shard_map.94), calls=%async_computation.2 | async-start | bytes 1179648 | tf_op jit(solution)/shard_map/all_to_all | solution.py:24
  85.1 4.3 %collective-permute-start = (f32[2,8,768]{2,1,0:T(8,128)S(1)}, f32[2,8,768]{2,1,0:T(8,128)S(1)}, u32[]{:S(2)}, u32[]{:S(2)}) collective-permute-start(f32[2,8,768]{2,1,0:T(8,128)S(1)} %get-tuple-element.36), channel_id=1, source_target_pairs={{0,8},{8,0},{1,9},{9,1},{2,10},{10,2},{3,11},{11,3},{4,12},{12,4},... | collective-permute-start | bytes 147464 | tf_op jit(solution)/shard_map/ppermute | solution.py:15
  89.4 17.1 %all-to-all-done.2 = f32[12,16,768]{2,1,0:T(8,128)} async-done(((f32[12,16,768]{2,1,0:T(8,128)}), f32[12,16,768]{2,1,0:T(8,128)}, u32[]{:S(2)}, u32[]{:S(2)}) %all-to-all-start.2) | async-done | bytes 589856 | tf_op jit(solution)/shard_map/all_to_all | solution.py:24
  108.3 25.4 %all_gather.4.column_ref = f32[12,16,768]{2,1,0:T(8,128)S(1)} all-gather(f32[1,16,768]{2,1,0:T(8,128)S(1)} %get-tuple-element.30), channel_id=1, replica_groups=mesh['z'=12,'xl'=2,'core'=2,'xh'=2,'y'=8] {'z'}, dimensions={0}, use_global_device_ids=true | all-gather | bytes 638976 | tf_op jit(solution)/shard_map/all_gather | solution.py:308
  133.6 5.5 %shard_map.95 = f32[4,8,24,128]{3,2,1,0:T(8,128)} custom-call(s32[1]{0:T(128)} %bitcast.me_ref, f32[12,16,768]{2,1,0:T(8,128)S(1)} %all_gather.4.column_ref, f32[256,768]{1,0:T(8,128)S(1)} %copy-done.1, f32[256,768]{1,0:T(8,128)S(1)} %collective-permute-done.1.refs_1_, f32[256,768]{1,0:T(8,128)S(1)} %collective-permute-done.2.refs_2_, ...), custom_call_target="tpu_custom_call" | custom-call | flops 905969664 | bytes 8000000 | tf_op jit(solution)/shard_map/pallas_call | solution.py:194
  139.1 7.5 %all-to-all-start.3 = ((f32[32,24,128]{2,1,0:T(8,128)}), f32[32,24,128]{2,1,0:T(8,128)S(1)}, u32[]{:S(2)}, u32[]{:S(2)}) async-start(f32[32,24,128]{2,1,0:T(8,128)} %bitcast.11), calls=%async_computation.3 | async-start | bytes 786432 | tf_op jit(solution)/shard_map/all_to_all | solution.py:24
  148.0 6.2 %collective-permute-start.8 = (f32[2,8,768]{2,1,0:T(8,128)}, f32[2,8,768]{2,1,0:T(8,128)}, u32[]{:S(2)}, u32[]{:S(2)}) collective-permute-start(f32[2,8,768]{2,1,0:T(8,128)} %get-tuple-element.34), channel_id=1, source_target_pairs={{0,8},{8,0},{1,9},{9,1},{2,10},{10,2},{3,11},{11,3},{4,12},{12,4},... | collective-permute-start | bytes 147464 | tf_op jit(solution)/shard_map/ppermute | solution.py:15
  154.3 2.8 %collective-permute-done.8 = f32[2,8,768]{2,1,0:T(8,128)} collective-permute-done((f32[2,8,768]{2,1,0:T(8,128)}, f32[2,8,768]{2,1,0:T(8,128)}, u32[]{:S(2)}, u32[]{:S(2)}) %collective-permute-start.8) | collective-permute-done | bytes 49184 | tf_op jit(solution)/shard_map/ppermute | solution.py:15
  158.6 2.3 %all-to-all-done.3 = f32[32,24,128]{2,1,0:T(8,128)S(1)} async-done(((f32[32,24,128]{2,1,0:T(8,128)}), f32[32,24,128]{2,1,0:T(8,128)S(1)}, u32[]{:S(2)}, u32[]{:S(2)}) %all-to-all-start.3) | async-done | bytes 393248 | tf_op jit(solution)/shard_map/all_to_all | solution.py:24
  161.0 30.8 %all_to_all.25 = f32[16,4,24,128]{3,2,1,0:T(8,128)S(1)} all-to-all(f32[16,4,24,128]{3,2,1,0:T(8,128)S(1)} %broadcast_in_dim.15), channel_id=1, replica_groups=mesh['z'=12,'xl'=2,'core'=2,'xh'=2,'y'=8] {'xh','y'}, dimensions={0} | all-to-all | bytes 1572864 | tf_op jit(solution)/shard_map/all_to_all | solution.py:24
  191.8 3.0 %shard_map.96 = (bf16[768,256]{1,0:T(8,128)(2,1)}, f32[768,256]{1,0:T(8,128)}) custom-call(f32[2,8,4,24,128]{4,3,2,1,0:T(8,128)S(1)} %bitcast.46, f32[768,768]{1,0:T(8,128)S(1)} %copy-done, f32[768,256]{1,0:T(8,128)S(1)} %copy-done.2), custom_call_target="tpu_custom_call" | custom-call | flops 905969664 | bytes 6000000 | tf_op jit(solution)/shard_map/pallas_call | solution.py:247
  (26 shorter events, 11.7 us)
Async XLA Ops:
  0.6 24.0 %copy-start.1 = (f32[256,768]{1,0:T(8,128)S(1)}, f32[256,768]{1,0:T(8,128)}, u32[]{:S(2)}) copy-start(f32[256,768]{1,0:T(8,128)} %refs_0_.1) | copy-start | bytes 2359300
  0.6 26.0 %collective-permute-start.2 = (f32[256,768]{1,0:T(8,128)}, f32[256,768]{1,0:T(8,128)S(1)}, u32[]{:S(2)}, u32[]{:S(2)}) collective-permute-start(f32[256,768]{1,0:T(8,128)} %refs_0_.1), channel_id=1, source_target_pairs={{0,32},{32,0},{1,33},{33,1},{2,34},{34,2},{3,35},{35,3},{4,36},{36... | collective-permute-start | bytes 2359304 | tf_op jit(solution)/shard_map/ppermute | solution.py:15
  4.2 24.8 %collective-permute-start.4 = (f32[256,768]{1,0:T(8,128)}, f32[256,768]{1,0:T(8,128)S(1)}, u32[]{:S(2)}, u32[]{:S(2)}) collective-permute-start(f32[256,768]{1,0:T(8,128)} %refs_0_.1), channel_id=1, source_target_pairs={{0,40},{8,32},{16,56},{24,48},{32,8},{40,0},{48,24},{56,16},{1,41}... | collective-permute-start | bytes 2359304 | tf_op jit(solution)/shard_map/ppermute | solution.py:20
  12.6 34.8 %all-to-all-start = ((f32[64,24,128]{2,1,0:T(8,128)}), f32[64,24,128]{2,1,0:T(8,128)}, u32[]{:S(2)}, u32[]{:S(2)}) async-start(f32[64,24,128]{2,1,0:T(8,128)} %bitcast.47), calls=%async_computation | async-start | bytes 1572864 | tf_op jit(solution)/shard_map/all_to_all | solution.py:24
  24.6 13.5 %collective-permute-start.1 = (f32[256,768]{1,0:T(8,128)S(1)}, f32[256,768]{1,0:T(8,128)S(1)}, u32[]{:S(2)}, u32[]{:S(2)}) collective-permute-start(f32[256,768]{1,0:T(8,128)S(1)} %copy-done.1), channel_id=1, source_target_pairs={{0,16},{16,0},{1,17},{17,1},{2,18},{18,2},{3,19},{19,3},{4,20},{20... | collective-permute-start | bytes 2359304 | tf_op jit(solution)/shard_map/ppermute | solution.py:15
  26.7 20.7 %collective-permute-start.3 = (f32[256,768]{1,0:T(8,128)S(1)}, f32[256,768]{1,0:T(8,128)}, u32[]{:S(2)}, u32[]{:S(2)}) collective-permute-start(f32[256,768]{1,0:T(8,128)S(1)} %collective-permute-done.2.refs_2_), channel_id=1, source_target_pairs={{0,16},{16,0},{1,17},{17,1},{2,18},{18,2},{3,19},{19,3},{4,20},{20... | collective-permute-start | bytes 2359304 | tf_op jit(solution)/shard_map/ppermute | solution.py:15
  29.0 18.4 %collective-permute-start.5 = (f32[256,768]{1,0:T(8,128)S(1)}, f32[256,768]{1,0:T(8,128)}, u32[]{:S(2)}, u32[]{:S(2)}) collective-permute-start(f32[256,768]{1,0:T(8,128)S(1)} %collective-permute-done.4.refs_6_), channel_id=1, source_target_pairs={{0,16},{16,0},{1,17},{17,1},{2,18},{18,2},{3,19},{19,3},{4,20},{20... | collective-permute-start | bytes 2359304 | tf_op jit(solution)/shard_map/ppermute | solution.py:15
  31.1 26.6 %collective-permute-start.6 = (f32[256,768]{1,0:T(8,128)S(1)}, f32[256,768]{1,0:T(8,128)}, u32[]{:S(2)}, u32[]{:S(2)}) collective-permute-start(f32[256,768]{1,0:T(8,128)S(1)} %collective-permute-done.4.refs_6_), channel_id=1, source_target_pairs={{0,32},{32,0},{1,33},{33,1},{2,34},{34,2},{3,35},{35,3},{4,36},{36... | collective-permute-start | bytes 2359304 | tf_op jit(solution)/shard_map/ppermute | solution.py:15
  34.6 25.8 %collective-permute-start.7 = (f32[256,768]{1,0:T(8,128)S(1)}, f32[256,768]{1,0:T(8,128)}, u32[]{:S(2)}, u32[]{:S(2)}) collective-permute-start(f32[256,768]{1,0:T(8,128)S(1)} %collective-permute-done.2.refs_2_), channel_id=1, source_target_pairs={{0,56},{8,48},{16,40},{24,32},{32,24},{40,16},{48,8},{56,0},{1,57}... | collective-permute-start | bytes 2359304 | tf_op jit(solution)/shard_map/ppermute | solution.py:20
  49.4 18.1 %all-to-all-start.1 = ((f32[8,96,128]{2,1,0:T(8,128)}), f32[8,96,128]{2,1,0:T(8,128)S(1)}, u32[]{:S(2)}, u32[]{:S(2)}) async-start(f32[8,96,128]{2,1,0:T(8,128)} %broadcast_in_dim.14), calls=%async_computation.1 | async-start | bytes 786432 | tf_op jit(solution)/shard_map/all_to_all | solution.py:24
  72.2 34.3 %all-to-all-start.2 = ((f32[12,16,768]{2,1,0:T(8,128)}), f32[12,16,768]{2,1,0:T(8,128)}, u32[]{:S(2)}, u32[]{:S(2)}) async-start(f32[12,16,768]{2,1,0:T(8,128)} %shard_map.94), calls=%async_computation.2 | async-start | bytes 1179648 | tf_op jit(solution)/shard_map/all_to_all | solution.py:24
  85.1 22.5 %collective-permute-start = (f32[2,8,768]{2,1,0:T(8,128)S(1)}, f32[2,8,768]{2,1,0:T(8,128)S(1)}, u32[]{:S(2)}, u32[]{:S(2)}) collective-permute-start(f32[2,8,768]{2,1,0:T(8,128)S(1)} %get-tuple-element.36), channel_id=1, source_target_pairs={{0,8},{8,0},{1,9},{9,1},{2,10},{10,2},{3,11},{11,3},{4,12},{12,4},... | collective-permute-start | bytes 147464 | tf_op jit(solution)/shard_map/ppermute | solution.py:15
  139.1 52.7 %copy-start = (f32[768,768]{1,0:T(8,128)S(1)}, f32[768,768]{1,0:T(8,128)}, u32[]{:S(2)}) copy-start(f32[768,768]{1,0:T(8,128)} %left_ref.3) | copy-start | bytes 7077892
  139.1 52.7 %copy-start.2 = (f32[768,256]{1,0:T(8,128)S(1)}, f32[768,256]{1,0:T(8,128)}, u32[]{:S(2)}) copy-start(f32[768,256]{1,0:T(8,128)} %master_ref.1) | copy-start | bytes 2359300
  139.1 21.7 %all-to-all-start.3 = ((f32[32,24,128]{2,1,0:T(8,128)}), f32[32,24,128]{2,1,0:T(8,128)S(1)}, u32[]{:S(2)}, u32[]{:S(2)}) async-start(f32[32,24,128]{2,1,0:T(8,128)} %bitcast.11), calls=%async_computation.3 | async-start | bytes 786432 | tf_op jit(solution)/shard_map/all_to_all | solution.py:24
  148.0 9.1 %collective-permute-start.8 = (f32[2,8,768]{2,1,0:T(8,128)}, f32[2,8,768]{2,1,0:T(8,128)}, u32[]{:S(2)}, u32[]{:S(2)}) collective-permute-start(f32[2,8,768]{2,1,0:T(8,128)} %get-tuple-element.34), channel_id=1, source_target_pairs={{0,8},{8,0},{1,9},{9,1},{2,10},{10,2},{3,11},{11,3},{4,12},{12,4},... | collective-permute-start | bytes 147464 | tf_op jit(solution)/shard_map/ppermute | solution.py:15

commit v9 on v7

--- a/solution.py
+++ b/solution.py
@@ -214,6 +214,32 @@
     )(me, column, *basis)
 
 
+def sum_kernel(me_ref, parts_ref, out_ref):
+    for i in range(parts_ref.shape[0]):
+        total = jnp.sum(parts_ref[jnp.bitwise_xor(me_ref[0], i)], axis=0)
+        for peer in range(out_ref.shape[0]):
+            out_ref[peer, i] = total
+
+
+def sum_and_copy(me, parts, peers):
+    ring, senders, *block = parts.shape
+    shape = (peers, ring, *block)
+    return pl.pallas_call(
+        sum_kernel,
+        grid=(1,),
+        in_specs=[
+            pl.BlockSpec(memory_space=pltpu.SMEM),
+            pl.BlockSpec(parts.shape, lambda i: (0, 0, 0, 0)),
+        ],
+        out_specs=pl.BlockSpec(shape, lambda i: (0, 0, 0, 0)),
+        out_shape=pltpu.HBM(shape, jnp.float32),
+        compiler_params=pltpu.CompilerParams(vmem_limit_bytes=24 * 2**20),
+        cost_estimate=pl.CostEstimate(
+            flops=ring * senders * block[0] * LANES, bytes_accessed=1_200_000, transcendentals=0
+        ),
+    )(me, parts)
+
+
 def finish_kernel(got_ref, left_ref, master_ref, weight_ref, direction_ref, rows, back, high, low):
     peers, few = got_ref.shape[1], 8
     piece = got_ref.shape[3] // 2
@@ -291,10 +317,9 @@
     parts = start(left_basis, gradient, peers)
     parts = exchange(parts.reshape((-1,) + parts.shape[3:]), ("xl", "core", "xh", "y"))
     parts, early = lax.optimization_barrier((parts, early))
-    left_chunk = jnp.sum(parts.reshape(2, 2, 2 * peers, -1, LANES), axis=2)
-    left_chunk = jnp.where(xl == 0, left_chunk, left_chunk[::-1])
-    left_chunk = jnp.where(core == 0, left_chunk, left_chunk[:, ::-1])
-    left_rotated = copies_to(left_chunk.reshape(-1, LANES), "y")
+    me = (2 * xl + core).astype(jnp.int32).reshape(1)
+    left_copies = sum_and_copy(me, parts.reshape(4, 2 * peers, -1, LANES), peers)
+    left_rotated = exchange(left_copies.reshape(peers, -1, LANES), "y")
     basis = early[:4] + [by_xh, by_xh_core] + early[4:]
 
     rotated = jnp.sum(exchange(forth(left_rotated, basis, few), "z"), axis=0)
@@ -312,11 +337,11 @@
         xh == 0, jnp.concatenate([mine, other], axis=1), jnp.concatenate([other, mine], axis=1)
     )
 
-    me = (2 * xl + core).astype(jnp.int32).reshape(1)
     back_part = rotate_back(me, column, basis, peers)
     back_part = exchange(back_part.reshape((-1,) + back_part.shape[2:]), ("xl", "core", "y"))
-    back_chunk = jnp.sum(back_part.reshape((4, peers) + back_part.shape[1:]), axis=1)
-    got = copies_to(back_chunk, COL).reshape((2, peers) + back_chunk.shape)
+    back_part = back_part.reshape((4, peers) + back_part.shape[1:])
+    back_copies = sum_and_copy(jnp.zeros_like(me), back_part, 2 * peers)
+    got = exchange(back_copies, COL).reshape((2, peers) + back_copies.shape[1:])
     new_weight, direction = finish(got, left_basis, master_weight)
     return (new_weight, direction, moments[0], moments[1])
 

time: 194 us -> 194 us (level)
  Pallas kernels: 16.8 us -> 19.7 us
    pallas_call x0 -> x2, Pallas kernels: none -> 2.9 us  [sum_and_copy(): pl.pallas_call(sum_kernel, grid=(1,), in_specs=[pl.BlockSpec(memory_space...]
  transfers between devices with their start and end apart: 13 -> 13, of which waited for: 7 -> 7; matrix products, arithmetic and copies ran while one was open for 2% -> 1% of each run, Pallas kernels for 2% -> 3%
where the time goes in v9:
time: 194 us; the launch traced here: 193 us
  starting transfers between devices  66.9 us (34%)
  waiting for transfers between devices  56.1 us (29%)
  blocking collectives  46 us (24%)
  Pallas kernels  19.7 us (10%)
  other arithmetic  1.97 us (1%)
    all_to_all x4, waiting for transfers between devices, exchange(): return lax.all_to_all(x, axes, 0, 0, tiled=True)  47.5 us
    all_to_all x4, starting transfers between devices, exchange(): return lax.all_to_all(x, axes, 0, 0, tiled=True)  36.7 us
    all_gather x1, blocking collectives, shards(): column = lax.all_gather(normed, 'z', axis=0, tiled=False)  25.3 us
    ppermute x7, starting transfers between devices, swap(): return lax.ppermute(x, axis, [(0, 1), (1, 0)])  22.7 us
    all_to_all x1, blocking collectives, exchange(): return lax.all_to_all(x, axes, 0, 0, tiled=True)  20.7 us
    ppermute x2, starting transfers between devices, cross(): lax.ppermute(x, ('xl', 'core', 'xh'), [(i, i ^ flip) for i in range(8)])  7.49 us
    ppermute x7, waiting for transfers between devices, swap(): return lax.ppermute(x, axis, [(0, 1), (1, 0)])  5.88 us
    pallas_call x1, Pallas kernels, rotate_back(): pl.pallas_call(back_kernel, grid=(2,), in_specs=[pl.BlockSpec(memory_spac...  4.79 us
  transfers between devices with their start and end apart: 13, of which 7 were waited for; matrix products, arithmetic and copies ran while one was open for 1% of the time, Pallas kernels for 3%

profile of v9, /device:TPU:8, one launch (start us, length us, event | category | flops | bytes accessed | tf_op | source)
XLA Modules:
  0.0 193.3 jit_solution(3574600821273194633)
XLA Ops:
  0.6 3.5 %collective-permute-start.2 = (f32[256,768]{1,0:T(8,128)}, f32[256,768]{1,0:T(8,128)S(1)}, u32[]{:S(2)}, u32[]{:S(2)}) collective-permute-start(f32[256,768]{1,0:T(8,128)} %refs_0_.1), channel_id=1, source_target_pairs={{0,32},{32,0},{1,33},{33,1},{2,34},{34,2},{3,35},{35,3},{4,36},{36... | collective-permute-start | bytes 2359304 | tf_op jit(solution)/shard_map/ppermute | solution.py:15
  4.2 4.0 %collective-permute-start.4 = (f32[256,768]{1,0:T(8,128)}, f32[256,768]{1,0:T(8,128)S(1)}, u32[]{:S(2)}, u32[]{:S(2)}) collective-permute-start(f32[256,768]{1,0:T(8,128)} %refs_0_.1), channel_id=1, source_target_pairs={{0,40},{8,32},{16,56},{24,48},{32,8},{40,0},{48,24},{56,16},{1,41}... | collective-permute-start | bytes 2359304 | tf_op jit(solution)/shard_map/ppermute | solution.py:20
  8.2 4.4 %shard_map.93 = f32[4,2,8,24,128]{4,3,2,1,0:T(8,128)} custom-call(f32[768,768]{1,0:T(8,128)} %left_ref.3, bf16[768,256]{1,0:T(8,128)(2,1)} %gradient_ref.1), custom_call_target="tpu_custom_call" | custom-call | flops 603979776 | bytes 4000000 | tf_op jit(solution)/shard_map/pallas_call | solution.py:85
  12.6 12.0 %all-to-all-start = ((f32[64,24,128]{2,1,0:T(8,128)}), f32[64,24,128]{2,1,0:T(8,128)}, u32[]{:S(2)}, u32[]{:S(2)}) async-start(f32[64,24,128]{2,1,0:T(8,128)} %bitcast.47), calls=%async_computation | async-start | bytes 1572864 | tf_op jit(solution)/shard_map/all_to_all | solution.py:24
  26.7 2.3 %collective-permute-start.3 = (f32[256,768]{1,0:T(8,128)S(1)}, f32[256,768]{1,0:T(8,128)}, u32[]{:S(2)}, u32[]{:S(2)}) collective-permute-start(f32[256,768]{1,0:T(8,128)S(1)} %collective-permute-done.2.refs_2_), channel_id=1, source_target_pairs={{0,16},{16,0},{1,17},{17,1},{2,18},{18,2},{3,19},{19,3},{4,20},{20... | collective-permute-start | bytes 2359304 | tf_op jit(solution)/shard_map/ppermute | solution.py:15
  31.0 3.6 %collective-permute-start.6 = (f32[256,768]{1,0:T(8,128)S(1)}, f32[256,768]{1,0:T(8,128)}, u32[]{:S(2)}, u32[]{:S(2)}) collective-permute-start(f32[256,768]{1,0:T(8,128)S(1)} %collective-permute-done.4.refs_6_), channel_id=1, source_target_pairs={{0,32},{32,0},{1,33},{33,1},{2,34},{34,2},{3,35},{35,3},{4,36},{36... | collective-permute-start | bytes 2359304 | tf_op jit(solution)/shard_map/ppermute | solution.py:15
  34.6 3.5 %collective-permute-start.7 = (f32[256,768]{1,0:T(8,128)S(1)}, f32[256,768]{1,0:T(8,128)}, u32[]{:S(2)}, u32[]{:S(2)}) collective-permute-start(f32[256,768]{1,0:T(8,128)S(1)} %collective-permute-done.2.refs_2_), channel_id=1, source_target_pairs={{0,56},{8,48},{16,40},{24,32},{32,24},{40,16},{48,8},{56,0},{1,57}... | collective-permute-start | bytes 2359304 | tf_op jit(solution)/shard_map/ppermute | solution.py:20
  38.1 9.3 %all-to-all-done = f32[64,24,128]{2,1,0:T(8,128)} async-done(((f32[64,24,128]{2,1,0:T(8,128)}), f32[64,24,128]{2,1,0:T(8,128)}, u32[]{:S(2)}, u32[]{:S(2)}) %all-to-all-start) | async-done | bytes 786464 | tf_op jit(solution)/shard_map/all_to_all | solution.py:24
  49.3 5.1 %all-to-all-start.1 = ((f32[8,96,128]{2,1,0:T(8,128)}), f32[8,96,128]{2,1,0:T(8,128)S(1)}, u32[]{:S(2)}, u32[]{:S(2)}) async-start(f32[8,96,128]{2,1,0:T(8,128)} %bitcast.48), calls=%async_computation.1 | async-start | bytes 786432 | tf_op jit(solution)/shard_map/all_to_all | solution.py:24
  54.4 3.3 %collective-permute-done.6.refs_4_ = f32[256,768]{1,0:T(8,128)} collective-permute-done((f32[256,768]{1,0:T(8,128)S(1)}, f32[256,768]{1,0:T(8,128)}, u32[]{:S(2)}, u32[]{:S(2)}) %collective-permute-start.6) | collective-permute-done | bytes 786464 | tf_op jit(solution)/shard_map/ppermute | solution.py:15
  57.7 2.7 %collective-permute-done.7.refs_5_ = f32[256,768]{1,0:T(8,128)} collective-permute-done((f32[256,768]{1,0:T(8,128)S(1)}, f32[256,768]{1,0:T(8,128)}, u32[]{:S(2)}, u32[]{:S(2)}) %collective-permute-start.7) | collective-permute-done | bytes 786464 | tf_op jit(solution)/shard_map/ppermute | solution.py:20
  60.4 7.1 %all-to-all-done.1.left_ref = f32[8,96,128]{2,1,0:T(8,128)S(1)} async-done(((f32[8,96,128]{2,1,0:T(8,128)}), f32[8,96,128]{2,1,0:T(8,128)S(1)}, u32[]{:S(2)}, u32[]{:S(2)}) %all-to-all-start.1) | async-done | bytes 393248 | tf_op jit(solution)/shard_map/all_to_all | solution.py:24
  67.5 4.7 %shard_map.95 = f32[12,16,768]{2,1,0:T(8,128)} custom-call(f32[8,96,128]{2,1,0:T(8,128)S(1)} %all-to-all-done.1.left_ref, f32[256,768]{1,0:T(8,128)S(1)} %copy-done.1, f32[256,768]{1,0:T(8,128)S(1)} %collective-permute-done.1.refs_1_, f32[256,768]{1,0:T(8,128)S(1)} %collective-permute-done.2.refs_2_, f32[256,768]{1,0:T(8,128)} %collective-permute-done.3.refs_3_, ...), custom_call_target="tpu_custom_call" | custom-call | flops 905969664 | bytes 8000000 | tf_op jit(solution)/shard_map/pallas_call | solution.py:137
  72.1 12.1 %all-to-all-start.2 = ((f32[12,16,768]{2,1,0:T(8,128)}), f32[12,16,768]{2,1,0:T(8,128)}, u32[]{:S(2)}, u32[]{:S(2)}) async-start(f32[12,16,768]{2,1,0:T(8,128)} %shard_map.95), calls=%async_computation.2 | async-start | bytes 1179648 | tf_op jit(solution)/shard_map/all_to_all | solution.py:24
  85.0 4.3 %collective-permute-start = (f32[2,8,768]{2,1,0:T(8,128)S(1)}, f32[2,8,768]{2,1,0:T(8,128)S(1)}, u32[]{:S(2)}, u32[]{:S(2)}) collective-permute-start(f32[2,8,768]{2,1,0:T(8,128)S(1)} %get-tuple-element.30), channel_id=1, source_target_pairs={{0,8},{8,0},{1,9},{9,1},{2,10},{10,2},{3,11},{11,3},{4,12},{12,4},... | collective-permute-start | bytes 147464 | tf_op jit(solution)/shard_map/ppermute | solution.py:15
  89.3 17.2 %all-to-all-done.2 = f32[12,16,768]{2,1,0:T(8,128)} async-done(((f32[12,16,768]{2,1,0:T(8,128)}), f32[12,16,768]{2,1,0:T(8,128)}, u32[]{:S(2)}, u32[]{:S(2)}) %all-to-all-start.2) | async-done | bytes 589856 | tf_op jit(solution)/shard_map/all_to_all | solution.py:24
  107.7 25.3 %all_gather.4.column_ref = f32[12,16,768]{2,1,0:T(8,128)S(1)} all-gather(f32[1,16,768]{2,1,0:T(8,128)S(1)} %get-tuple-element.24), channel_id=1, replica_groups=mesh['z'=12,'xl'=2,'core'=2,'xh'=2,'y'=8] {'z'}, dimensions={0}, use_global_device_ids=true | all-gather | bytes 638976 | tf_op jit(solution)/shard_map/all_gather | solution.py:333
  133.0 4.8 %shard_map.96 = f32[4,8,24,128]{3,2,1,0:T(8,128)S(1)} custom-call(s32[1]{0:T(128)} %bitcast.me_ref, f32[12,16,768]{2,1,0:T(8,128)S(1)} %all_gather.4.column_ref, f32[256,768]{1,0:T(8,128)S(1)} %copy-done.1, f32[256,768]{1,0:T(8,128)S(1)} %collective-permute-done.1.refs_1_, f32[256,768]{1,0:T(8,128)S(1)} %collective-permute-done.2.refs_2_, ...), custom_call_target="tpu_custom_call" | custom-call | flops 905969664 | bytes 8000000 | tf_op jit(solution)/shard_map/pallas_call | solution.py:194
  137.8 20.7 %all_to_all.25 = f32[32,24,128]{2,1,0:T(8,128)S(1)} all-to-all(f32[32,24,128]{2,1,0:T(8,128)S(1)} %bitcast.45), channel_id=1, replica_groups=mesh['z'=12,'xl'=2,'core'=2,'xh'=2,'y'=8] {'xl','core','y'}, dimensions={0} | all-to-all | bytes 786432 | tf_op jit(solution)/shard_map/all_to_all | solution.py:24
  159.5 7.6 %all-to-all-start.4 = ((f32[16,4,24,128]{3,2,1,0:T(8,128)}), f32[16,4,24,128]{3,2,1,0:T(8,128)S(1)}, u32[]{:S(2)}, u32[]{:S(2)}) async-start(f32[16,4,24,128]{3,2,1,0:T(8,128)} %shard_map.97), calls=%async_computation.4 | async-start | bytes 1572864 | tf_op jit(solution)/shard_map/all_to_all | solution.py:24
  167.1 4.9 %collective-permute-start.8 = (f32[2,8,768]{2,1,0:T(8,128)S(1)}, f32[2,8,768]{2,1,0:T(8,128)S(1)}, u32[]{:S(2)}, u32[]{:S(2)}) collective-permute-start(f32[2,8,768]{2,1,0:T(8,128)S(1)} %get-tuple-element.28), channel_id=1, source_target_pairs={{0,8},{8,0},{1,9},{9,1},{2,10},{10,2},{3,11},{11,3},{4,12},{12,4},... | collective-permute-start | bytes 147464 | tf_op jit(solution)/shard_map/ppermute | solution.py:15
  172.0 2.6 %collective-permute-done.8 = f32[2,8,768]{2,1,0:T(8,128)S(1)} collective-permute-done((f32[2,8,768]{2,1,0:T(8,128)S(1)}, f32[2,8,768]{2,1,0:T(8,128)S(1)}, u32[]{:S(2)}, u32[]{:S(2)}) %collective-permute-start.8) | collective-permute-done | bytes 49184 | tf_op jit(solution)/shard_map/ppermute | solution.py:15
  175.3 13.9 %all-to-all-done.4 = f32[16,4,24,128]{3,2,1,0:T(8,128)S(1)} async-done(((f32[16,4,24,128]{3,2,1,0:T(8,128)}), f32[16,4,24,128]{3,2,1,0:T(8,128)S(1)}, u32[]{:S(2)}, u32[]{:S(2)}) %all-to-all-start.4) | async-done | bytes 786464 | tf_op jit(solution)/shard_map/all_to_all | solution.py:24
  190.4 2.9 %shard_map.98 = (bf16[768,256]{1,0:T(8,128)(2,1)}, f32[768,256]{1,0:T(8,128)}) custom-call(f32[2,8,4,24,128]{4,3,2,1,0:T(8,128)S(1)} %bitcast.44, f32[768,768]{1,0:T(8,128)S(1)} %copy-done, f32[768,256]{1,0:T(8,128)S(1)} %copy-done.2), custom_call_target="tpu_custom_call" | custom-call | flops 905969664 | bytes 6000000 | tf_op jit(solution)/shard_map/pallas_call | solution.py:273
  (22 shorter events, 10.8 us)
Async XLA Ops:
  0.6 24.0 %copy-start.1 = (f32[256,768]{1,0:T(8,128)S(1)}, f32[256,768]{1,0:T(8,128)}, u32[]{:S(2)}) copy-start(f32[256,768]{1,0:T(8,128)} %refs_0_.1) | copy-start | bytes 2359300
  0.6 26.0 %collective-permute-start.2 = (f32[256,768]{1,0:T(8,128)}, f32[256,768]{1,0:T(8,128)S(1)}, u32[]{:S(2)}, u32[]{:S(2)}) collective-permute-start(f32[256,768]{1,0:T(8,128)} %refs_0_.1), channel_id=1, source_target_pairs={{0,32},{32,0},{1,33},{33,1},{2,34},{34,2},{3,35},{35,3},{4,36},{36... | collective-permute-start | bytes 2359304 | tf_op jit(solution)/shard_map/ppermute | solution.py:15
  4.2 24.8 %collective-permute-start.4 = (f32[256,768]{1,0:T(8,128)}, f32[256,768]{1,0:T(8,128)S(1)}, u32[]{:S(2)}, u32[]{:S(2)}) collective-permute-start(f32[256,768]{1,0:T(8,128)} %refs_0_.1), channel_id=1, source_target_pairs={{0,40},{8,32},{16,56},{24,48},{32,8},{40,0},{48,24},{56,16},{1,41}... | collective-permute-start | bytes 2359304 | tf_op jit(solution)/shard_map/ppermute | solution.py:20
  12.6 34.8 %all-to-all-start = ((f32[64,24,128]{2,1,0:T(8,128)}), f32[64,24,128]{2,1,0:T(8,128)}, u32[]{:S(2)}, u32[]{:S(2)}) async-start(f32[64,24,128]{2,1,0:T(8,128)} %bitcast.47), calls=%async_computation | async-start | bytes 1572864 | tf_op jit(solution)/shard_map/all_to_all | solution.py:24
  24.6 13.5 %collective-permute-start.1 = (f32[256,768]{1,0:T(8,128)S(1)}, f32[256,768]{1,0:T(8,128)S(1)}, u32[]{:S(2)}, u32[]{:S(2)}) collective-permute-start(f32[256,768]{1,0:T(8,128)S(1)} %copy-done.1), channel_id=1, source_target_pairs={{0,16},{16,0},{1,17},{17,1},{2,18},{18,2},{3,19},{19,3},{4,20},{20... | collective-permute-start | bytes 2359304 | tf_op jit(solution)/shard_map/ppermute | solution.py:15
  26.7 20.7 %collective-permute-start.3 = (f32[256,768]{1,0:T(8,128)S(1)}, f32[256,768]{1,0:T(8,128)}, u32[]{:S(2)}, u32[]{:S(2)}) collective-permute-start(f32[256,768]{1,0:T(8,128)S(1)} %collective-permute-done.2.refs_2_), channel_id=1, source_target_pairs={{0,16},{16,0},{1,17},{17,1},{2,18},{18,2},{3,19},{19,3},{4,20},{20... | collective-permute-start | bytes 2359304 | tf_op jit(solution)/shard_map/ppermute | solution.py:15
  29.0 18.4 %collective-permute-start.5 = (f32[256,768]{1,0:T(8,128)S(1)}, f32[256,768]{1,0:T(8,128)}, u32[]{:S(2)}, u32[]{:S(2)}) collective-permute-start(f32[256,768]{1,0:T(8,128)S(1)} %collective-permute-done.4.refs_6_), channel_id=1, source_target_pairs={{0,16},{16,0},{1,17},{17,1},{2,18},{18,2},{3,19},{19,3},{4,20},{20... | collective-permute-start | bytes 2359304 | tf_op jit(solution)/shard_map/ppermute | solution.py:15
  31.0 26.6 %collective-permute-start.6 = (f32[256,768]{1,0:T(8,128)S(1)}, f32[256,768]{1,0:T(8,128)}, u32[]{:S(2)}, u32[]{:S(2)}) collective-permute-start(f32[256,768]{1,0:T(8,128)S(1)} %collective-permute-done.4.refs_6_), channel_id=1, source_target_pairs={{0,32},{32,0},{1,33},{33,1},{2,34},{34,2},{3,35},{35,3},{4,36},{36... | collective-permute-start | bytes 2359304 | tf_op jit(solution)/shard_map/ppermute | solution.py:15
  34.6 25.8 %collective-permute-start.7 = (f32[256,768]{1,0:T(8,128)S(1)}, f32[256,768]{1,0:T(8,128)}, u32[]{:S(2)}, u32[]{:S(2)}) collective-permute-start(f32[256,768]{1,0:T(8,128)S(1)} %collective-permute-done.2.refs_2_), channel_id=1, source_target_pairs={{0,56},{8,48},{16,40},{24,32},{32,24},{40,16},{48,8},{56,0},{1,57}... | collective-permute-start | bytes 2359304 | tf_op jit(solution)/shard_map/ppermute | solution.py:20
  49.3 18.1 %all-to-all-start.1 = ((f32[8,96,128]{2,1,0:T(8,128)}), f32[8,96,128]{2,1,0:T(8,128)S(1)}, u32[]{:S(2)}, u32[]{:S(2)}) async-start(f32[8,96,128]{2,1,0:T(8,128)} %bitcast.48), calls=%async_computation.1 | async-start | bytes 786432 | tf_op jit(solution)/shard_map/all_to_all | solution.py:24
  72.1 34.4 %all-to-all-start.2 = ((f32[12,16,768]{2,1,0:T(8,128)}), f32[12,16,768]{2,1,0:T(8,128)}, u32[]{:S(2)}, u32[]{:S(2)}) async-start(f32[12,16,768]{2,1,0:T(8,128)} %shard_map.95), calls=%async_computation.2 | async-start | bytes 1179648 | tf_op jit(solution)/shard_map/all_to_all | solution.py:24
  85.0 22.6 %collective-permute-start = (f32[2,8,768]{2,1,0:T(8,128)S(1)}, f32[2,8,768]{2,1,0:T(8,128)S(1)}, u32[]{:S(2)}, u32[]{:S(2)}) collective-permute-start(f32[2,8,768]{2,1,0:T(8,128)S(1)} %get-tuple-element.30), channel_id=1, source_target_pairs={{0,8},{8,0},{1,9},{9,1},{2,10},{10,2},{3,11},{11,3},{4,12},{12,4},... | collective-permute-start | bytes 147464 | tf_op jit(solution)/shard_map/ppermute | solution.py:15
  137.8 51.4 %copy-start = (f32[768,768]{1,0:T(8,128)S(1)}, f32[768,768]{1,0:T(8,128)}, u32[]{:S(2)}) copy-start(f32[768,768]{1,0:T(8,128)} %left_ref.3) | copy-start | bytes 7077892
  159.5 29.7 %all-to-all-start.4 = ((f32[16,4,24,128]{3,2,1,0:T(8,128)}), f32[16,4,24,128]{3,2,1,0:T(8,128)S(1)}, u32[]{:S(2)}, u32[]{:S(2)}) async-start(f32[16,4,24,128]{3,2,1,0:T(8,128)} %shard_map.97), calls=%async_computation.4 | async-start | bytes 1572864 | tf_op jit(solution)/shard_map/all_to_all | solution.py:24
  167.1 7.5 %collective-permute-start.8 = (f32[2,8,768]{2,1,0:T(8,128)S(1)}, f32[2,8,768]{2,1,0:T(8,128)S(1)}, u32[]{:S(2)}, u32[]{:S(2)}) collective-permute-start(f32[2,8,768]{2,1,0:T(8,128)S(1)} %get-tuple-element.28), channel_id=1, source_target_pairs={{0,8},{8,0},{1,9},{9,1},{2,10},{10,2},{3,11},{11,3},{4,12},{12,4},... | collective-permute-start | bytes 147464 | tf_op jit(solution)/shard_map/ppermute | solution.py:15
  189.2 1.1 copy-start.2
